TPU v7x, 32 devices: a whole 2x2x4 slice. The times are simulated.
32 devices in a mesh: dp: 8 (over z, x), tensor: 4 (over y, core).
Axes of the slice: x: 2, y: 2, z: 4, core: 2. Of those that a mesh axis runs over, the one named last changes fastest.
Arguments:
- tokens: bfloat16 [16, 320, 2048], P('dp', 'tensor'), may hold values from -6 to 6
- cotangent: bfloat16 [16, 320, 2048], P('dp', 'tensor'), may hold values from -6 to 6
- project_weight: float32 [3, 2048, 2048], P(None, 'dp', 'tensor'), may hold values from -0.14142136 to 0.14142136
- output_weight: float32 [2048, 2048], P('tensor', 'dp'), may hold values from -0.75 to 0.75
- gate_up_weight: float32 [2, 2048, 5632], P(None, 'dp', 'tensor'), may hold values from -0.125 to 0.125
- down_weight: float32 [5632, 2048], P('tensor', 'dp'), may hold values from -0.078125 to 0.078125
- norm_params: float32 [2, 2048], P(None, 'dp'), may hold values from -0.5 to 2.25
- first_project: float32 [3, 2048, 2048], P(None, 'dp', 'tensor'), may hold values from -6 to 6
- first_output: float32 [2048, 2048], P('tensor', 'dp'), may hold values from -0.4375 to 0.4375
- first_gate_up: float32 [2, 2048, 5632], P(None, 'dp', 'tensor'), may hold values from -1.25 to 1.25
- first_down: float32 [5632, 2048], P('tensor', 'dp'), may hold values from -2 to 2
- first_norm: float32 [2, 2048], P(None, 'dp'), may hold values from -6 to 6
- second_project: float32 [3, 2048, 2048], P(None, 'dp', 'tensor'), may hold values from 0.014848 to 0.06144
- second_output: float32 [2048, 2048], P('tensor', 'dp'), may hold values from 6.656e-05 to 0.00026624
- second_gate_up: float32 [2, 2048, 5632], P(None, 'dp', 'tensor'), may hold values from 0.0007168 to 0.0029696
- second_down: float32 [5632, 2048], P('tensor', 'dp'), may hold values from 0.0016384 to 0.006656
- second_norm: float32 [2, 2048], P(None, 'dp'), may hold values from 0.0512 to 0.2048
Outputs:
- layer_out: bfloat16 [16, 320, 2048], P('dp', 'tensor')
- input_grad: bfloat16 [16, 320, 2048], P('dp', 'tensor')
- grad_project: float32 [3, 2048, 2048], P(None, 'dp', 'tensor')
- grad_output: float32 [2048, 2048], P('tensor', 'dp')
- grad_gate_up: float32 [2, 2048, 5632], P(None, 'dp', 'tensor')
- grad_down: float32 [5632, 2048], P('tensor', 'dp')
- grad_norm_params: float32 [2, 2048], P(None, 'dp')
- norm_total: float32 [], replicated
- new_project: float32 [3, 2048, 2048], P(None, 'dp', 'tensor')
- new_output: float32 [2048, 2048], P('tensor', 'dp')
- new_gate_up: float32 [2, 2048, 5632], P(None, 'dp', 'tensor')
- new_down: float32 [5632, 2048], P('tensor', 'dp')
- new_norm_params: float32 [2, 2048], P(None, 'dp')
- moment_project: float32 [3, 2048, 2048], P(None, 'dp', 'tensor')
- moment_output: float32 [2048, 2048], P('tensor', 'dp')
- moment_gate_up: float32 [2, 2048, 5632], P(None, 'dp', 'tensor')
- moment_down: float32 [5632, 2048], P('tensor', 'dp')
- moment_norm: float32 [2, 2048], P(None, 'dp')
- square_project: float32 [3, 2048, 2048], P(None, 'dp', 'tensor')
- square_output: float32 [2048, 2048], P('tensor', 'dp')
- square_gate_up: float32 [2, 2048, 5632], P(None, 'dp', 'tensor')
- square_down: float32 [5632, 2048], P('tensor', 'dp')
- square_norm: float32 [2, 2048], P(None, 'dp')
All inputs are finite; a program needn't handle non-finite values.
Results may differ from a plain program's by a relative error of at most 0.012.
The roundings to bfloat16 on the way count: a program that leaves them out, or rounds other values in their place, can miss the bound.
Values may be sent and summed in bfloat16 or wider, within the bound.
A program may use at most 256 MiB of HBM per device.

v0:
```python
import math

import jax
import jax.numpy as jnp
from jax import lax
from jax.sharding import PartitionSpec as P

D = 2048
HEAD_DIM = 64
FF = 5632
SEQ = 320
STEP = 10
ROT = 16


BETA_ONE = 0.9
BETA_TWO = 0.999
ADAM_EPS = 1e-08
NORM_EPS = 1e-05
MASK_FILL = -1e30


def angle_tables(length):
    half_rot = ROT // 2
    inverse = 10000.0 ** (-2.0 * jnp.arange(half_rot, dtype=jnp.float32) / ROT)
    angles = jnp.arange(length, dtype=jnp.float32)[:, None] * inverse[None, :]
    return (jnp.cos(angles)[:, None, :], jnp.sin(angles)[:, None, :])


def rotate(values_in, cosine, sine_table, direction):
    half_rot = ROT // 2
    first_half = values_in[..., :half_rot]
    second_half = values_in[..., half_rot:ROT]
    return jnp.concatenate(
        [
            first_half * cosine - direction * second_half * sine_table,
            second_half * cosine + direction * first_half * sine_table,
            values_in[..., ROT:],
        ],
        axis=-1,
    )


def contract_rows(left_side, right_side):
    return lax.dot_general(
        left_side, right_side, (((0,), (0,)), ((), ())), preferred_element_type=jnp.float32
    )


def contract_cols(left_side, right_side):
    return lax.dot_general(
        left_side, right_side, (((1,), (1,)), ((), ())), preferred_element_type=jnp.float32
    )


def adam_update(weight_old, gradient, moment_old, square_old, factor, rate, decay):
    clipped = gradient * factor
    moment_new = BETA_ONE * moment_old + (1.0 - BETA_ONE) * clipped
    square_new = BETA_TWO * square_old + (1.0 - BETA_TWO) * clipped * clipped
    moment_hat = moment_new / (1.0 - BETA_ONE**STEP)
    square_hat = square_new / (1.0 - BETA_TWO**STEP)
    weight_new = weight_old - rate * (
        moment_hat / (jnp.sqrt(square_hat) + ADAM_EPS) + decay * weight_old
    )
    return (weight_new, moment_new, square_new)


def local(
    tokens,
    cotangent,
    project_weight,
    output_weight,
    gate_up_weight,
    down_weight,
    norm_params,
    first_project,
    first_output,
    first_gate_up,
    first_down,
    first_norm,
    second_project,
    second_output,
    second_gate_up,
    second_down,
    second_norm,
):
    project_low = project_weight.astype(jnp.bfloat16)
    output_low = output_weight.astype(jnp.bfloat16)
    gate_up_low = gate_up_weight.astype(jnp.bfloat16)
    down_low = down_weight.astype(jnp.bfloat16)
    norm_low = norm_params.astype(jnp.bfloat16)
    fore_weights = (
        lax.all_gather(project_low, "dp", axis=1, tiled=True),
        lax.all_gather(output_low, "dp", axis=1, tiled=True),
        lax.all_gather(gate_up_low, "dp", axis=1, tiled=True),
        lax.all_gather(down_low, "dp", axis=1, tiled=True),
        lax.all_gather(norm_low, "dp", axis=1, tiled=True),
    )
    full_project, full_output, full_gate_up, full_down, full_norm = fore_weights
    gain_full = full_norm[0].astype(jnp.float32)
    shift_full = full_norm[1].astype(jnp.float32)
    micro_count = tokens.shape[0]
    layer_outs = []
    input_grads = []
    local_grads = None
    reduced = None
    for micro_index in range(micro_count):
        tok_rows = tokens[micro_index].astype(jnp.float32)
        row_mean = jnp.mean(tok_rows, axis=1, keepdims=True)
        centered = tok_rows - row_mean
        row_scale = lax.rsqrt(jnp.mean(centered * centered, axis=1, keepdims=True) + NORM_EPS)
        unit_rows = centered * row_scale
        normed = (unit_rows * gain_full + shift_full).astype(jnp.bfloat16)
        gathered = lax.all_gather(normed, "tensor", axis=0, tiled=True)
        seq_len = gathered.shape[0]
        projected = jnp.einsum(
            "sd,kdc->ksc", gathered, full_project, preferred_element_type=jnp.float32
        )
        local_width = projected.shape[2]
        local_heads = local_width // HEAD_DIM
        cosine, sine_table = angle_tables(seq_len)
        query_rot = rotate(
            projected[0].reshape(seq_len, local_heads, HEAD_DIM), cosine, sine_table, 1.0
        ).astype(jnp.bfloat16)
        key_rot = rotate(
            projected[1].reshape(seq_len, local_heads, HEAD_DIM), cosine, sine_table, 1.0
        ).astype(jnp.bfloat16)
        value_low = projected[2].reshape(seq_len, local_heads, HEAD_DIM).astype(jnp.bfloat16)
        positions = jnp.arange(seq_len)
        causal = (positions[:, None] >= positions[None, :])[None]
        scores = jnp.where(
            causal,
            jnp.einsum("qhd,khd->hqk", query_rot, key_rot, preferred_element_type=jnp.float32)
            * 0.125,
            MASK_FILL,
        )
        row_top = jnp.max(scores, axis=2, keepdims=True)
        exponent = jnp.exp(scores - row_top)
        row_total = jnp.sum(exponent, axis=2, keepdims=True)
        soft_low = (exponent / row_total).astype(jnp.bfloat16)
        log_total = row_top + jnp.log(row_total)
        attended = (
            jnp.einsum("hqk,khd->qhd", soft_low, value_low, preferred_element_type=jnp.float32)
            .reshape(seq_len, local_width)
            .astype(jnp.bfloat16)
        )
        gate_up = jnp.einsum(
            "sd,kdc->ksc", gathered, full_gate_up, preferred_element_type=jnp.float32
        )
        gate_pre = gate_up[0]
        up_pre = gate_up[1]
        sigmoid_gate = jax.nn.sigmoid(gate_pre)
        swish_gate = gate_pre * sigmoid_gate
        hidden_low = (swish_gate * up_pre).astype(jnp.bfloat16)
        summed = lax.psum_scatter(
            jnp.dot(attended, full_output, preferred_element_type=jnp.float32)
            + jnp.dot(hidden_low, full_down, preferred_element_type=jnp.float32),
            "tensor",
            scatter_dimension=0,
            tiled=True,
        )
        layer_outs.append((tok_rows + summed).astype(jnp.bfloat16))
        cot_low = cotangent[micro_index]
        cot_full = lax.all_gather(cot_low, "tensor", axis=0, tiled=True)
        grad_output = contract_rows(attended, cot_full)
        grad_down = contract_rows(hidden_low, cot_full)
        d_att = (
            contract_cols(cot_full, full_output)
            .astype(jnp.bfloat16)
            .reshape(seq_len, local_heads, HEAD_DIM)
        )
        d_hid = contract_cols(cot_full, full_down).astype(jnp.bfloat16).astype(jnp.float32)
        d_gate = d_hid * up_pre * (sigmoid_gate * (1.0 + gate_pre * (1.0 - sigmoid_gate)))
        d_up = d_hid * swish_gate
        d_gate_up = jnp.stack([d_gate, d_up]).astype(jnp.bfloat16)
        grad_gate_up = jnp.einsum(
            "sd,ksc->kdc", gathered, d_gate_up, preferred_element_type=jnp.float32
        )
        rescored = jnp.where(
            causal,
            jnp.einsum("qhd,khd->hqk", query_rot, key_rot, preferred_element_type=jnp.float32)
            * 0.125,
            MASK_FILL,
        )
        soft_again = jnp.exp(rescored - log_total)
        soft_again_low = soft_again.astype(jnp.bfloat16)
        d_value = jnp.einsum(
            "hqk,qhd->khd", soft_again_low, d_att, preferred_element_type=jnp.float32
        ).astype(jnp.bfloat16)
        d_prob = jnp.einsum("qhd,khd->hqk", d_att, value_low, preferred_element_type=jnp.float32)
        d_score = (
            soft_again * (d_prob - jnp.sum(d_prob * soft_again, axis=2, keepdims=True))
        ).astype(jnp.bfloat16)
        d_query = rotate(
            0.125
            * jnp.einsum("hqk,khd->qhd", d_score, key_rot, preferred_element_type=jnp.float32),
            cosine,
            sine_table,
            -1.0,
        ).astype(jnp.bfloat16)
        d_key = rotate(
            0.125
            * jnp.einsum("hqk,qhd->khd", d_score, query_rot, preferred_element_type=jnp.float32),
            cosine,
            sine_table,
            -1.0,
        ).astype(jnp.bfloat16)
        d_project = jnp.stack(
            [
                d_query.reshape(seq_len, local_width),
                d_key.reshape(seq_len, local_width),
                d_value.reshape(seq_len, local_width),
            ]
        )
        grad_project = jnp.einsum(
            "sd,ksc->kdc", gathered, d_project, preferred_element_type=jnp.float32
        )
        d_normed = lax.psum_scatter(
            jnp.einsum("ksc,kdc->sd", d_project, full_project, preferred_element_type=jnp.float32)
            + jnp.einsum(
                "ksc,kdc->sd", d_gate_up, full_gate_up, preferred_element_type=jnp.float32
            ),
            "tensor",
            scatter_dimension=0,
            tiled=True,
        )
        d_unit = d_normed * gain_full
        d_input = row_scale * (
            d_unit
            - jnp.mean(d_unit, axis=1, keepdims=True)
            - unit_rows * jnp.mean(d_unit * unit_rows, axis=1, keepdims=True)
        )
        input_grads.append((cot_low.astype(jnp.float32) + d_input).astype(jnp.bfloat16))
        grad_norm = jnp.stack([jnp.sum(d_normed * unit_rows, axis=0), jnp.sum(d_normed, axis=0)])
        fresh = (grad_project, grad_output, grad_gate_up, grad_down, grad_norm)
        local_grads = (
            fresh
            if local_grads is None
            else tuple((earlier + later for earlier, later in zip(local_grads, fresh)))
        )
    reduced = (
        lax.psum_scatter(local_grads[0], "dp", scatter_dimension=1, tiled=True),
        lax.psum_scatter(local_grads[1], "dp", scatter_dimension=1, tiled=True),
        lax.psum_scatter(local_grads[2], "dp", scatter_dimension=1, tiled=True),
        lax.psum_scatter(local_grads[3], "dp", scatter_dimension=1, tiled=True),
        lax.psum_scatter(local_grads[4], "dp", scatter_dimension=1, tiled=True),
    )
    norm_reduced = lax.psum(reduced[4], "tensor")
    grads_final = (reduced[0], reduced[1], reduced[2], reduced[3], norm_reduced)
    square_local = (
        jnp.sum(reduced[0] * reduced[0])
        + jnp.sum(reduced[1] * reduced[1])
        + jnp.sum(reduced[2] * reduced[2])
        + jnp.sum(reduced[3] * reduced[3])
        + jnp.sum(norm_reduced * norm_reduced) / lax.axis_size("tensor")
    )
    square_total = lax.psum(square_local, ("dp", "tensor"))
    norm_total = jnp.sqrt(square_total)
    limit = 0.03 * math.sqrt(
        (4 * D * D + 3 * D * FF + 2 * D) * micro_count * lax.axis_size("dp") * SEQ
    )
    factor = jnp.minimum(1.0, limit / (norm_total + 1e-06))
    rates = (
        2.0 / math.sqrt(D),
        2.0 / math.sqrt(D // 32),
        2.0 / math.sqrt(D),
        2.0 / math.sqrt(FF),
        0.5,
    )
    decays = (0.1, 0.1, 0.1, 0.1, 0.0)
    masters = (project_weight, output_weight, gate_up_weight, down_weight, norm_params)
    firsts = (first_project, first_output, first_gate_up, first_down, first_norm)
    seconds = (second_project, second_output, second_gate_up, second_down, second_norm)
    updated = [
        adam_update(
            masters[index],
            grads_final[index],
            firsts[index],
            seconds[index],
            factor,
            rates[index],
            decays[index],
        )
        for index in range(5)
    ]
    return (
        jnp.stack(layer_outs),
        jnp.stack(input_grads),
        grads_final[0],
        grads_final[1],
        grads_final[2],
        grads_final[3],
        grads_final[4],
        norm_total,
        updated[0][0],
        updated[1][0],
        updated[2][0],
        updated[3][0],
        updated[4][0],
        updated[0][1],
        updated[1][1],
        updated[2][1],
        updated[3][1],
        updated[4][1],
        updated[0][2],
        updated[1][2],
        updated[2][2],
        updated[3][2],
        updated[4][2],
    )


def solution(mesh):
    placed = (
        P("dp", "tensor", None),
        P("dp", "tensor", None),
        P(None, "dp", "tensor"),
        P("tensor", "dp"),
        P(None, "dp", "tensor"),
        P("tensor", "dp"),
        P(None, "dp"),
        P(None, "dp", "tensor"),
        P("tensor", "dp"),
        P(None, "dp", "tensor"),
        P("tensor", "dp"),
        P(None, "dp"),
        P(None, "dp", "tensor"),
        P("tensor", "dp"),
        P(None, "dp", "tensor"),
        P("tensor", "dp"),
        P(None, "dp"),
    )
    return jax.shard_map(
        local,
        mesh=mesh,
        in_specs=placed,
        out_specs=(
            P("dp", "tensor", None),
            P("dp", "tensor", None),
            P(None, "dp", "tensor"),
            P("tensor", "dp"),
            P(None, "dp", "tensor"),
            P("tensor", "dp"),
            P(None, "dp"),
            P(),
            P(None, "dp", "tensor"),
            P("tensor", "dp"),
            P(None, "dp", "tensor"),
            P("tensor", "dp"),
            P(None, "dp"),
            P(None, "dp", "tensor"),
            P("tensor", "dp"),
            P(None, "dp", "tensor"),
            P("tensor", "dp"),
            P(None, "dp"),
            P(None, "dp", "tensor"),
            P("tensor", "dp"),
            P(None, "dp", "tensor"),
            P("tensor", "dp"),
            P(None, "dp"),
        ),
        check_vma=False,
    )
```

profile of v0, /device:TPU:0, one launch (start us, length us, event | category | flops | bytes accessed | tf_op | source)
XLA Modules:
  0.0 1715.8 jit_solution(16923742541578721800)
XLA Ops:
  12.1 22.2 %all_gather.27 = bf16[2,2048]{1,0:T(2,128)(2,1)S(1)} all-gather(bf16[2,256]{1,0:T(2,128)(2,1)S(1)} %convert_element_type.187), channel_id=1, replica_groups=mesh['dp'=8,'tensor'=4] {'dp'}, dimensions={1}, use_global_device_ids=true | all-gather | bytes 9216 | tf_op jit(solution)/shard_map/all_gather | solution.py:97
  38.1 3.2 convert_element_type.196
  43.7 41.1 %all-gather.15.cloned.1.call-done = bf16[512,2048]{1,0:T(8,128)(2,1)} async-done(((bf16[512,256]{1,0:T(8,128)(2,1)}), bf16[512,2048]{1,0:T(8,128)(2,1)}) %all-gather.15.cloned.1.call-update) | async-done | bytes 2097168 | tf_op jit(solution)/shard_map/all_gather | solution.py:94
  87.9 15.5 all-gather.25.cloned.1.call-done
  106.5 17.1 all-gather.11.cloned.1.call-done
  123.6 101.7 %all-gather.13.cloned.1.call-done = bf16[3,2048,512]{2,1,0:T(8,128)(2,1)} async-done(((bf16[3,256,512]{2,1,0:T(8,128)(2,1)}), bf16[3,2048,512]{2,1,0:T(8,128)(2,1)}) %all-gather.13.cloned.1.call-update) | async-done | bytes 6291472 | tf_op jit(solution)/shard_map/all_gather | solution.py:93
  225.3 5.4 convolution_bitcast_fusion.7
  234.9 8.7 all-gather.21.cloned.1.call-done
  243.7 5.4 convolution_bitcast_fusion.6
  262.3 3.3 multiply_reduce_fusion.1
  281.8 128.3 %all-gather.17.cloned.1.call-done = bf16[2,2048,1408]{2,1,0:T(8,128)(2,1)} async-done(((bf16[2,256,1408]{2,1,0:T(8,128)(2,1)}), bf16[2,2048,1408]{2,1,0:T(8,128)(2,1)}) %all-gather.17.cloned.1.call-update) | async-done | bytes 11534352 | tf_op jit(solution)/shard_map/all_gather | solution.py:95
  410.1 8.5 convolution_bitcast_fusion.1
  418.6 85.9 %all-gather.19.cloned.1.call-done = bf16[1408,2048]{1,0:T(8,128)(2,1)} async-done(((bf16[1408,256]{1,0:T(8,128)(2,1)}), bf16[1408,2048]{1,0:T(8,128)(2,1)}) %all-gather.19.cloned.1.call-update) | async-done | bytes 5767184 | tf_op jit(solution)/shard_map/all_gather | solution.py:96
  504.5 8.2 fusion.63
  512.7 7.0 convolution_bitcast_fusion.3
  519.7 7.3 fusion.5
  536.9 7.7 convolution_bitcast_fusion
  544.7 6.9 fusion.64
  551.6 7.0 convolution_bitcast_fusion.2
  558.6 7.3 fusion.6
  574.7 3.3 convolution_add_fusion.1
  578.5 5.2 fusion.137
  586.2 5.0 fusion.138
  594.6 7.5 fusion.39
  606.3 13.5 add_bitcast_fusion.1
  619.8 4.9 fusion.26
  624.7 6.3 convolution_add_fusion
  632.3 12.3 fusion.37
  644.6 16.0 add_bitcast_fusion
  663.6 3.5 copy.153
  671.8 3.4 copy.150
  675.2 3.5 copy.151
  678.7 13.3 reduce-scatter.22.cloned.1.call-done
  693.9 35.8 %reduce-scatter.12.cloned.1.call-done = f32[80,2048]{1,0:T(8,128)} async-done(((f32[320,2048]{1,0:T(8,128)}), f32[80,2048]{1,0:T(8,128)}) %reduce-scatter.12.cloned.1.call-update) | async-done | bytes 655376 | tf_op jit(solution)/shard_map/reduce_scatter | solution.py:155
  729.7 37.2 %reduce-scatter.14.cloned.1.call-done = f32[80,2048]{1,0:T(8,128)} async-done(((f32[320,2048]{1,0:T(8,128)}), f32[80,2048]{1,0:T(8,128)}) %reduce-scatter.14.cloned.1.call-update) | async-done | bytes 655376 | tf_op jit(solution)/shard_map/reduce_scatter | solution.py:155
  770.7 63.9 %reduce-scatter.28.cloned.1.call-done = f32[256,2]{1,0:T(8,128)} async-done(((f32[2048,2]{1,0:T(8,128)}), f32[256,2]{1,0:T(8,128)}) %reduce-scatter.28.cloned.1.call-update) | async-done | bytes 2064
  835.6 5.6 psum.14
  842.5 202.3 %reduce-scatter.20.cloned.1.call-done = f32[3,256,512]{1,2,0:T(8,128)} async-done(((f32[3,2048,512]{1,2,0:T(8,128)}), f32[3,256,512]{1,2,0:T(8,128)}) %reduce-scatter.20.cloned.1.call-update) | async-done | bytes 1572880 | tf_op jit(solution)/shard_map/reduce_scatter | solution.py:242
  1048.5 192.5 %reduce-scatter.26.cloned.1.call-done = f32[1408,256]{1,0:T(8,128)} async-done(((f32[1408,2048]{1,0:T(8,128)}), f32[1408,256]{1,0:T(8,128)}) %reduce-scatter.26.cloned.1.call-update) | async-done | bytes 1441808 | tf_op jit(solution)/shard_map/reduce_scatter | solution.py:245
  1243.4 374.9 %reduce-scatter.24.cloned.1.call-done = f32[2,256,1408]{1,2,0:T(8,128)} async-done(((f32[2,2048,1408]{1,2,0:T(8,128)}), f32[2,256,1408]{1,2,0:T(8,128)}) %reduce-scatter.24.cloned.1.call-update) | async-done | bytes 2883600 | tf_op jit(solution)/shard_map/reduce_scatter | solution.py:244
  1624.6 39.5 %psum.15 = f32[]{:T(128)} all-reduce(f32[]{:T(128)S(6)} %add.283), channel_id=1, replica_groups=mesh['dp'=8,'tensor'=4] {'dp','tensor'}, use_global_device_ids=true, to_apply=%region_33.34 | all-reduce | flops 1 | bytes 8 | tf_op jit(solution)/shard_map/psum | solution.py:257
  1664.8 4.8 multiply_subtract_fusion.1
  1669.7 3.2 copy.156
  1672.9 8.4 multiply_subtract_fusion
  1681.3 3.4 copy.157
  1687.7 3.4 copy.159
  1694.1 3.4 copy.161
  1703.3 4.6 multiply_subtract_fusion.2
  (332 shorter events, 116.6 us)
Async XLA Ops:
  7.2 27.1 %copy-start.6 = (bf16[2,80,2048]{2,1,0:T(8,128)(2,1)S(1)}, bf16[2,80,2048]{2,1,0:T(8,128)(2,1)}, u32[]{:S(2)}) copy-start(bf16[2,80,2048]{2,1,0:T(8,128)(2,1)} %param.17) | copy-start | bytes 1966084
  7.2 36.5 %all-gather.23.cloned.1.call-start = ((), (), s32[]{:S(2)}) async-start(), calls=%async_computation.23 | async-start | bytes 1638400 | tf_op jit(solution)/shard_map/all_gather | solution.py:164
  9.3 27.1 %copy-start.12 = (f32[3,256,512]{2,1,0:T(8,128)S(1)}, f32[3,256,512]{2,1,0:T(8,128)}, u32[]{:S(2)}) copy-start(f32[3,256,512]{2,1,0:T(8,128)} %param.19) | copy-start | bytes 4718596
  9.3 75.5 %all-gather.15.cloned.1.call-start = ((), (), s32[]{:S(2)}) async-start(), calls=%async_computation.11 | async-start | bytes 2359296 | tf_op jit(solution)/shard_map/all_gather | solution.py:94
  11.3 92.1 %all-gather.25.cloned.1.call-start = ((), (), s32[]{:S(2)}) async-start(), calls=%async_computation.24 | async-start | bytes 1638400 | tf_op jit(solution)/shard_map/all_gather | solution.py:164
  12.0 111.6 %all-gather.11.cloned.1.call-start = ((), (), s32[]{:S(2)}) async-start(), calls=%async_computation.9 | async-start | bytes 1638400 | tf_op jit(solution)/shard_map/all_gather | solution.py:114
  36.3 189.0 %all-gather.13.cloned.1.call-start = ((), (), s32[]{:S(2)}) async-start(), calls=%async_computation.10 | async-start | bytes 7077888 | tf_op jit(solution)/shard_map/all_gather | solution.py:93
  37.4 206.3 %all-gather.21.cloned.1.call-start = ((), (), s32[]{:S(2)}) async-start(), calls=%async_computation.15 | async-start | bytes 1638400 | tf_op jit(solution)/shard_map/all_gather | solution.py:114
  38.0 372.1 %all-gather.17.cloned.1.call-start = ((), (), s32[]{:S(2)}) async-start(), calls=%async_computation.12 | async-start | bytes 12976128 | tf_op jit(solution)/shard_map/all_gather | solution.py:95
  41.2 463.3 %all-gather.19.cloned.1.call-start = ((), (), s32[]{:S(2)}) async-start(), calls=%async_computation.13 | async-start | bytes 6488064 | tf_op jit(solution)/shard_map/all_gather | solution.py:96
  42.3 559.9 %reduce-scatter.16.cloned.1.call-start = ((), (), s32[]{:S(2)}) async-start(), calls=%async_computation.17 | async-start | bytes 3276800 | tf_op jit(solution)/shard_map/reduce_scatter | solution.py:218
  43.7 212.4 %copy-start.67 = (f32[320,8]{0,1:T(8,128)}, f32[320,8]{0,1:T(8,128)S(1)}, u32[]{:S(2)}) copy-start(f32[320,8]{0,1:T(8,128)S(1)} %get-tuple-element.171) | copy-start | bytes 30724
  278.1 132.0 %copy-start.8 = (bf16[320,2048]{1,0:T(8,128)(2,1)S(1)}, bf16[320,2048]{1,0:T(8,128)(2,1)}, u32[]{:S(2)}) copy-start(bf16[320,2048]{1,0:T(8,128)(2,1)} %all-gather.11.cloned.1.call-done) | copy-start | bytes 3932164
  279.7 240.0 %copy-start.38 = (bf16[1,320,512]{2,1,0:T(8,128)(2,1)}, bf16[1,320,512]{2,1,0:T(8,128)(2,1)S(1)}, u32[]{:S(2)}) copy-start(bf16[1,320,512]{2,1,0:T(8,128)(2,1)S(1)} %copy.137) | copy-start | bytes 983044
  504.5 8.2 copy-start.4
  512.7 7.0 copy-start.52
  512.7 7.0 copy-start.40
  527.0 75.1 %reduce-scatter.18.cloned.1.call-start = ((), (), s32[]{:S(2)}) async-start(), calls=%async_computation.18 | async-start | bytes 3276800 | tf_op jit(solution)/shard_map/reduce_scatter | solution.py:218
  536.9 7.8 copy-start.18
  536.9 14.7 slice-start
  536.9 14.7 slice-start.1
  551.6 7.0 copy-start.41
  551.6 7.0 copy-start.43
  566.0 126.1 %reduce-scatter.22.cloned.1.call-start = ((), (), s32[]{:S(2)}) async-start(), calls=%async_computation.20 | async-start | bytes 4718592 | tf_op jit(solution)/shard_map/reduce_scatter | solution.py:243
  578.0 151.7 %reduce-scatter.12.cloned.1.call-start = ((), (), s32[]{:S(2)}) async-start(), calls=%async_computation.14 | async-start | bytes 3276800 | tf_op jit(solution)/shard_map/reduce_scatter | solution.py:155
  586.1 180.8 %reduce-scatter.14.cloned.1.call-start = ((), (), s32[]{:S(2)}) async-start(), calls=%async_computation.16 | async-start | bytes 3276800 | tf_op jit(solution)/shard_map/reduce_scatter | solution.py:155
  593.6 8.6 copy-start.64
  593.6 8.6 copy-start.80
  593.6 8.6 copy-start.82
  593.6 8.6 copy-start.86
  593.6 8.6 copy-start.89
  593.6 241.0 %reduce-scatter.28.cloned.1.call-start = ((), (), s32[]{:S(2)}) async-start(), calls=%async_computation.25 | async-start | bytes 1179648
  606.2 438.6 %reduce-scatter.20.cloned.1.call-start = ((), (), s32[]{:S(2)}) async-start(), calls=%async_computation.19 | async-start | bytes 14155776 | tf_op jit(solution)/shard_map/reduce_scatter | solution.py:242
  619.7 621.3 %reduce-scatter.26.cloned.1.call-start = ((), (), s32[]{:S(2)}) async-start(), calls=%async_computation.22 | async-start | bytes 12976128 | tf_op jit(solution)/shard_map/reduce_scatter | solution.py:245
  631.0 987.3 %reduce-scatter.24.cloned.1.call-start = ((), (), s32[]{:S(2)}) async-start(), calls=%async_computation.21 | async-start | bytes 25952256 | tf_op jit(solution)/shard_map/reduce_scatter | solution.py:244
  632.2 12.3 copy-start.9
  675.2 18.7 %copy-start.96 = (f32[80]{0:T(128)S(1)}, f32[80]{0:T(128)}, u32[]{:S(2)}) copy-start(f32[80]{0:T(128)} %get-tuple-element.95) | copy-start | bytes 964
  675.2 18.7 %copy-start.95 = (f32[80]{0:T(128)S(1)}, f32[80]{0:T(128)}, u32[]{:S(2)}) copy-start(f32[80]{0:T(128)} %get-tuple-element.99) | copy-start | bytes 964
  675.2 18.7 %copy-start.94 = (f32[80]{0:T(128)S(1)}, f32[80]{0:T(128)}, u32[]{:S(2)}) copy-start(f32[80]{0:T(128)} %get-tuple-element.96) | copy-start | bytes 964
  675.2 18.7 %copy-start.93 = (f32[80]{0:T(128)S(1)}, f32[80]{0:T(128)}, u32[]{:S(2)}) copy-start(f32[80]{0:T(128)} %get-tuple-element.98) | copy-start | bytes 964
  675.2 91.7 %copy-start.22 = (bf16[2,80,2048]{2,1,0:T(8,128)(2,1)S(1)}, bf16[2,80,2048]{2,1,0:T(8,128)(2,1)}, u32[]{:S(2)}) copy-start(bf16[2,80,2048]{2,1,0:T(8,128)(2,1)} %param.18) | copy-start | bytes 1966084
  675.2 91.7 %copy-start.23 = (f32[80,2048]{1,0:T(8,128)S(1)}, f32[80,2048]{1,0:T(8,128)}, u32[]{:S(2)}) copy-start(f32[80,2048]{1,0:T(8,128)} %reduce-scatter.16.cloned.1.call-done) | copy-start | bytes 1966084
  675.2 91.7 %copy-start.24 = (f32[80,2048]{1,0:T(8,128)S(1)}, f32[80,2048]{1,0:T(8,128)}, u32[]{:S(2)}) copy-start(f32[80,2048]{1,0:T(8,128)} %reduce-scatter.18.cloned.1.call-done) | copy-start | bytes 1966084
  675.2 91.7 %copy-start.87 = (f32[80]{0:T(128)S(1)}, f32[80]{0:T(128)}, u32[]{:S(2)}) copy-start(f32[80]{0:T(128)} %copy-done.85) | copy-start | bytes 964
  675.2 91.7 %copy-start.90 = (f32[80]{0:T(128)S(1)}, f32[80]{0:T(128)}, u32[]{:S(2)}) copy-start(f32[80]{0:T(128)} %copy-done.88) | copy-start | bytes 964
  841.2 856.3 %copy-start.78 = (f32[2,256]{1,0:T(2,128)}, f32[2,256]{1,0:T(2,128)S(1)}, u32[]{:S(2)}) copy-start(f32[2,256]{1,0:T(2,128)S(1)} %psum.14) | copy-start | bytes 6148
  1048.5 574.4 %copy-start.7 = (f32[3,256,512]{1,2,0:T(8,128)S(1)}, f32[3,256,512]{1,2,0:T(8,128)}, u32[]{:S(2)}) copy-start(f32[3,256,512]{1,2,0:T(8,128)} %reduce-scatter.20.cloned.1.call-done) | copy-start | bytes 4718596
  1621.5 43.3 %copy-start.14 = (f32[3,256,512]{1,2,0:T(8,128)S(1)}, f32[3,256,512]{1,2,0:T(8,128)}, u32[]{:S(2)}) copy-start(f32[3,256,512]{1,2,0:T(8,128)} %copy.149) | copy-start | bytes 4718596
  (69 other events, 190.7 us)
Sparse Core Ops, SparseCore 0:
  10.2 20.8 all-gather.22
  33.7 51.0 all-gather.14
  87.0 16.3 all-gather.24
  105.4 18.1 all-gather.10
  126.2 99.0 all-gather.12
  227.3 16.3 all-gather.20
  246.4 163.6 all-gather.16
  412.7 91.7 all-gather.18
  527.1 32.8 reduce-scatter.15
  566.1 33.1 reduce-scatter.17
  603.5 88.4 reduce-scatter.21
  695.2 34.4 reduce-scatter.11
  732.2 34.6 reduce-scatter.13
  771.1 63.4 reduce-scatter.27
  838.1 206.7 reduce-scatter.19
  1048.8 192.1 reduce-scatter.25
  1244.8 373.4 reduce-scatter.23
where the time goes:
time: 1730 us; the launch traced here: 1720 us
  waiting for transfers between devices  1320 us (76%)
  matrix products  174 us (10%)
  local copies, waits for them, and re-layouts  75.6 us (4%)
  blocking collectives  67.4 us (4%)
  other arithmetic  56.8 us (3%)
  between operations  20.7 us (1%)
    reduce_scatter x1, waiting for transfers between devices, local(): lax.psum_scatter(local_grads[2], 'dp', scatter_dimension=1, tiled=True)  375 us
    reduce_scatter x1, waiting for transfers between devices, local(): lax.psum_scatter(local_grads[0], 'dp', scatter_dimension=1, tiled=True)  202 us
    reduce_scatter x1, waiting for transfers between devices, local(): lax.psum_scatter(local_grads[3], 'dp', scatter_dimension=1, tiled=True)  193 us
    all_gather x1, waiting for transfers between devices, local(): lax.all_gather(gate_up_low, 'dp', axis=1, tiled=True)  128 us
    all_gather x1, waiting for transfers between devices, local(): lax.all_gather(project_low, 'dp', axis=1, tiled=True)  102 us
    all_gather x1, waiting for transfers between devices, local(): lax.all_gather(down_low, 'dp', axis=1, tiled=True)  85.9 us
    reduce_scatter x2, waiting for transfers between devices, local(): lax.psum_scatter(jnp.dot(attended, full_output, preferred_element_type=jn...  73 us
    unnamed x18, waiting for transfers between devices  65.4 us
  transfers between devices with their start and end apart: 17, of which 14 were waited for; matrix products, arithmetic and copies ran while one was open for 13% of the time, Pallas kernels for 0%

commit v1 on v0

v1 whole, which is shorter than its diff:
```python
import math

import jax
import jax.numpy as jnp
from jax import lax
from jax.sharding import PartitionSpec as P

D = 2048
HEAD_DIM = 64
FF = 5632
SEQ = 320
STEP = 10
ROT = 16

BETA_ONE = 0.9
BETA_TWO = 0.999
ADAM_EPS = 1e-08
NORM_EPS = 1e-05
MASK_FILL = -1e30

BOTH = ("dp", "tensor")


def swap(values, dp_flip, tensor_flip):
    dp_size, tensor_size = lax.axis_size("dp"), lax.axis_size("tensor")
    pairs = [
        (d * tensor_size + t, (d ^ dp_flip) * tensor_size + (t ^ tensor_flip))
        for d in range(dp_size)
        for t in range(tensor_size)
    ]
    return lax.ppermute(values, BOTH, pairs)


def relative(values, axis, me, count):
    width = values.shape[axis] // count
    return jnp.concatenate(
        [lax.dynamic_slice_in_dim(values, (me ^ r) * width, width, axis) for r in range(count)],
        axis=axis,
    )


def flip_blocks(values, axis, count, flip):
    width = values.shape[axis] // count
    return jnp.concatenate(
        [lax.slice_in_dim(values, (r ^ flip) * width, ((r ^ flip) + 1) * width, axis=axis) for r in range(count)],
        axis=axis,
    )


def gather_blocks(mine, other):
    half = lax.axis_size("dp") // 2
    outer = [mine] + [swap(other if j % 2 else mine, 2 * j, 0) for j in range(1, half)]
    blocks = []
    for block in outer:
        blocks += [block, swap(block, 1, 0)]
    return blocks


def gather_rows(values):
    count = lax.axis_size("dp")
    other = flip_blocks(swap(values, 2, 0), values.ndim - 1, count, 2)
    pair = jnp.concatenate([values, other], axis=0)
    four = jnp.concatenate([pair, swap(pair, 0, 2)], axis=0)
    return jnp.concatenate([four, swap(four, 0, 1)], axis=0)


def scatter_rows(partial):
    count = lax.axis_size("dp")
    quarter = partial.shape[0] // 2
    four = partial[:quarter].astype(jnp.float32) + swap(partial[quarter:].astype(jnp.bfloat16), 0, 1)
    quarter //= 2
    pair = four[:quarter] + swap(four[quarter:].astype(jnp.bfloat16), 0, 2)
    quarter //= 2
    other = swap(pair[quarter:].astype(jnp.bfloat16), 2, 0).astype(jnp.float32)
    return pair[:quarter] + flip_blocks(other, 2, count, 2)


def scatter_blocks(partial_of):
    half = lax.axis_size("dp") // 2
    away = swap(partial_of(1).astype(jnp.bfloat16), 1, 0)
    summed = partial_of(0) + away.astype(jnp.float32)
    low = summed.astype(jnp.bfloat16)
    mine, other = summed[0], None
    for j in range(1, half):
        came = swap(low[j], 2 * j, 0).astype(jnp.float32)
        if j % 2 == 0:
            mine = mine + came
        else:
            other = came if other is None else other + came
    return mine, other


def rotate(values_in, cosine, sine_table, direction):
    half_rot = ROT // 2
    first_half = values_in[..., :half_rot]
    second_half = values_in[..., half_rot:ROT]
    return jnp.concatenate(
        [
            first_half * cosine - direction * second_half * sine_table,
            second_half * cosine + direction * first_half * sine_table,
            values_in[..., ROT:],
        ],
        axis=-1,
    )


def dot_plain(a, b):
    return lax.dot_general(a, b, (((1,), (0,)), ((), ())), preferred_element_type=jnp.float32)


def dot_rows(a, b):
    return lax.dot_general(a, b, (((0,), (0,)), ((), ())), preferred_element_type=jnp.float32)


def dot_cols(a, b):
    return lax.dot_general(a, b, (((1,), (1,)), ((), ())), preferred_element_type=jnp.float32)


def adam_update(weight_old, gradient, moment_old, square_old, factor, rate, decay):
    clipped = gradient * factor
    moment_new = BETA_ONE * moment_old + (1.0 - BETA_ONE) * clipped
    square_new = BETA_TWO * square_old + (1.0 - BETA_TWO) * clipped * clipped
    moment_hat = moment_new / (1.0 - BETA_ONE**STEP)
    square_hat = square_new / (1.0 - BETA_TWO**STEP)
    weight_new = weight_old - rate * (
        moment_hat / (jnp.sqrt(square_hat) + ADAM_EPS) + decay * weight_old
    )
    return (weight_new, moment_new, square_new)


def local(
    tokens,
    cotangent,
    project_weight,
    output_weight,
    gate_up_weight,
    down_weight,
    norm_params,
    first_project,
    first_output,
    first_gate_up,
    first_down,
    first_norm,
    second_project,
    second_output,
    second_gate_up,
    second_down,
    second_norm,
):
    count = lax.axis_size("dp")
    blocks_half = count // 2
    me = lax.axis_index("dp")
    side = (me // 2) % 2
    spot = lax.axis_index("tensor")
    micro_count, piece = tokens.shape[0], tokens.shape[1]
    head_cols = project_weight.shape[2] // 2
    unit_cols = gate_up_weight.shape[2] // 2
    rows_each = project_weight.shape[1]
    heads = head_cols // HEAD_DIM

    def halves(first, second):
        first, second = first.astype(jnp.bfloat16), second.astype(jnp.bfloat16)
        return jnp.where(side == 0, first, second), jnp.where(side == 0, second, first)

    def project_half(s):
        return jnp.concatenate(
            [project_weight[k, :, s * head_cols : (s + 1) * head_cols] for k in range(3)], axis=1
        )

    def gate_up_half(s):
        return jnp.concatenate(
            [gate_up_weight[k, :, s * unit_cols : (s + 1) * unit_cols] for k in range(2)], axis=1
        )

    def out_half(s):
        return jnp.concatenate(
            [
                output_weight[s * head_cols : (s + 1) * head_cols],
                down_weight[s * unit_cols : (s + 1) * unit_cols],
            ],
            axis=0,
        )

    norm_full = relative(
        lax.all_gather(norm_params.astype(jnp.bfloat16), "dp", axis=1, tiled=True), 1, me, count
    ).astype(jnp.float32)
    gain, shift = norm_full[0], norm_full[1]

    w_project = jnp.concatenate(gather_blocks(*halves(project_half(0), project_half(1))), axis=0)
    w_gate_up = jnp.concatenate(gather_blocks(*halves(gate_up_half(0), gate_up_half(1))), axis=0)
    w_out = jnp.concatenate(gather_blocks(*halves(out_half(0), out_half(1))), axis=1)

    tok_rows = relative(tokens, 2, me, count).astype(jnp.float32)
    row_mean = jnp.mean(tok_rows, axis=2, keepdims=True)
    centered = tok_rows - row_mean
    row_scale = lax.rsqrt(jnp.mean(centered * centered, axis=2, keepdims=True) + NORM_EPS)
    unit_rows = centered * row_scale
    normed = (unit_rows * gain + shift).astype(jnp.bfloat16)
    cot_low = relative(cotangent, 2, me, count)

    all_normed = gather_rows(normed)
    all_cot = gather_rows(cot_low)
    blocks_all = all_normed.shape[0]
    rows_all = blocks_all * piece
    all_normed = all_normed.reshape(rows_all, D)
    all_cot = all_cot.reshape(rows_all, D)

    spots = lax.axis_size("tensor")
    order = jnp.array([0, 2, 1, 3])
    positions = ((spot ^ order)[:, None] * piece + jnp.arange(piece)[None, :]).reshape(-1)
    inverse = 10000.0 ** (-2.0 * jnp.arange(ROT // 2, dtype=jnp.float32) / ROT)
    angles = positions.astype(jnp.float32)[:, None] * inverse[None, :]
    cosine, sine_table = jnp.cos(angles)[:, None, :], jnp.sin(angles)[:, None, :]
    causal = (positions[:, None] >= positions[None, :])[None, None]
    seqs = 2 * micro_count
    seq_len = spots * piece

    def to_heads(values):
        return (
            values.reshape(spots, seqs, piece, heads, HEAD_DIM)
            .transpose(1, 0, 2, 3, 4)
            .reshape(seqs, seq_len, heads, HEAD_DIM)
        )

    def from_heads(values):
        return (
            values.reshape(seqs, spots, piece, heads * HEAD_DIM)
            .transpose(1, 0, 2, 3)
            .reshape(rows_all, heads * HEAD_DIM)
        )

    projected = dot_plain(all_normed, w_project)
    query = rotate(to_heads(projected[:, :head_cols]), cosine, sine_table, 1.0).astype(jnp.bfloat16)
    key = rotate(to_heads(projected[:, head_cols : 2 * head_cols]), cosine, sine_table, 1.0).astype(
        jnp.bfloat16
    )
    value = to_heads(projected[:, 2 * head_cols :]).astype(jnp.bfloat16)
    scores = jnp.where(
        causal,
        jnp.einsum("sqhd,skhd->shqk", query, key, preferred_element_type=jnp.float32) * 0.125,
        MASK_FILL,
    )
    row_top = jnp.max(scores, axis=3, keepdims=True)
    exponent = jnp.exp(scores - row_top)
    row_total = jnp.sum(exponent, axis=3, keepdims=True)
    soft = exponent / row_total
    soft_low = soft.astype(jnp.bfloat16)
    attended = from_heads(
        jnp.einsum("shqk,skhd->sqhd", soft_low, value, preferred_element_type=jnp.float32)
    ).astype(jnp.bfloat16)

    gate_up = dot_plain(all_normed, w_gate_up)
    gate_pre, up_pre = gate_up[:, :unit_cols], gate_up[:, unit_cols:]
    sigmoid_gate = jax.nn.sigmoid(gate_pre)
    swish_gate = gate_pre * sigmoid_gate
    hidden = (swish_gate * up_pre).astype(jnp.bfloat16)
    middle = jnp.concatenate([attended, hidden], axis=1)

    def grad_out_part(i):
        cot_part = all_cot.reshape(rows_all, blocks_half, 2, rows_each)[:, :, i].reshape(rows_all, -1)
        return dot_rows(middle, cot_part).reshape(-1, blocks_half, rows_each).transpose(1, 0, 2)

    grad_out_mine, grad_out_other = scatter_blocks(grad_out_part)

    d_middle = dot_cols(all_cot, w_out).astype(jnp.bfloat16)
    d_hid = d_middle[:, head_cols:].astype(jnp.float32)
    d_gate = d_hid * up_pre * (sigmoid_gate * (1.0 + gate_pre * (1.0 - sigmoid_gate)))
    d_up = d_hid * swish_gate
    d_gate_up = jnp.concatenate([d_gate, d_up], axis=1).astype(jnp.bfloat16)

    def normed_part(i):
        return all_normed.reshape(rows_all, blocks_half, 2, rows_each)[:, :, i].reshape(rows_all, -1)

    grad_gu_mine, grad_gu_other = scatter_blocks(
        lambda i: dot_rows(normed_part(i), d_gate_up).reshape(blocks_half, rows_each, -1)
    )

    d_att = to_heads(d_middle[:, :head_cols])
    d_value = jnp.einsum("shqk,sqhd->skhd", soft_low, d_att, preferred_element_type=jnp.float32)
    d_prob = jnp.einsum("sqhd,skhd->shqk", d_att, value, preferred_element_type=jnp.float32)
    d_score = (
        soft * (d_prob - jnp.sum(d_prob * soft, axis=3, keepdims=True))
    ).astype(jnp.bfloat16)
    d_query = rotate(
        0.125 * jnp.einsum("shqk,skhd->sqhd", d_score, key, preferred_element_type=jnp.float32),
        cosine,
        sine_table,
        -1.0,
    )
    d_key = rotate(
        0.125 * jnp.einsum("shqk,sqhd->skhd", d_score, query, preferred_element_type=jnp.float32),
        cosine,
        sine_table,
        -1.0,
    )
    d_project = jnp.concatenate(
        [from_heads(d_query), from_heads(d_key), from_heads(d_value)], axis=1
    ).astype(jnp.bfloat16)

    d_normed = scatter_rows(
        (dot_cols(d_project, w_project) + dot_cols(d_gate_up, w_gate_up)).reshape(
            blocks_all, piece, D
        )
    )
    grad_p_mine, grad_p_other = scatter_blocks(
        lambda i: dot_rows(normed_part(i), d_project).reshape(blocks_half, rows_each, -1)
    )
    summed = scatter_rows(dot_plain(middle, w_out).reshape(blocks_all, piece, D))
    layer_out = relative((tok_rows + summed).astype(jnp.bfloat16), 2, me, count)

    d_unit = d_normed * gain
    d_input = row_scale * (
        d_unit
        - jnp.mean(d_unit, axis=2, keepdims=True)
        - unit_rows * jnp.mean(d_unit * unit_rows, axis=2, keepdims=True)
    )
    input_grad = relative((cot_low.astype(jnp.float32) + d_input).astype(jnp.bfloat16), 2, me, count)

    grad_norm = jnp.stack(
        [jnp.sum(d_normed * unit_rows, axis=(0, 1)), jnp.sum(d_normed, axis=(0, 1))]
    ).reshape(2, blocks_half, 2, rows_each)
    grad_norm = grad_norm[:, :, 0] + swap(grad_norm[:, :, 1], 1, 0)
    own = grad_norm[:, 0]
    for j in range(1, blocks_half):
        own = own + swap(grad_norm[:, j], 2 * j, 0)
    own = own + swap(own, 0, 2)
    norm_grad = own + swap(own, 0, 1)

    def both(mine, other, axis):
        return jnp.concatenate(
            [jnp.where(side == 0, mine, other), jnp.where(side == 0, other, mine)], axis=axis
        )

    def columns(mine, other, k, width):
        span = slice(k * width, (k + 1) * width)
        return both(mine[:, span], other[:, span], 1)

    grads = (
        jnp.stack([columns(grad_p_mine, grad_p_other, k, head_cols) for k in range(3)]),
        both(grad_out_mine[:head_cols], grad_out_other[:head_cols], 0),
        jnp.stack([columns(grad_gu_mine, grad_gu_other, k, unit_cols) for k in range(2)]),
        both(grad_out_mine[head_cols:], grad_out_other[head_cols:], 0),
        norm_grad,
    )
    square_local = sum(jnp.sum(g * g) for g in grads[:4]) + jnp.sum(norm_grad * norm_grad) / spots
    norm_total = jnp.sqrt(lax.psum(square_local, BOTH))
    limit = 0.03 * math.sqrt((4 * D * D + 3 * D * FF + 2 * D) * micro_count * count * SEQ)
    factor = jnp.minimum(1.0, limit / (norm_total + 1e-06))
    rates = (
        2.0 / math.sqrt(D),
        2.0 / math.sqrt(D // 32),
        2.0 / math.sqrt(D),
        2.0 / math.sqrt(FF),
        0.5,
    )
    decays = (0.1, 0.1, 0.1, 0.1, 0.0)
    masters = (project_weight, output_weight, gate_up_weight, down_weight, norm_params)
    firsts = (first_project, first_output, first_gate_up, first_down, first_norm)
    seconds = (second_project, second_output, second_gate_up, second_down, second_norm)
    updated = [
        adam_update(*parts) for parts in zip(masters, grads, firsts, seconds, [factor] * 5, rates, decays)
    ]
    return (
        layer_out,
        input_grad,
        *grads,
        norm_total,
        *[u[0] for u in updated],
        *[u[1] for u in updated],
        *[u[2] for u in updated],
    )


def solution(mesh):
    wide = P("dp", "tensor", None)
    stacked = P(None, "dp", "tensor")
    tall = P("tensor", "dp")
    params = (stacked, tall, stacked, tall, P(None, "dp"))
    return jax.shard_map(
        local,
        mesh=mesh,
        in_specs=(wide, wide, *params, *params, *params),
        out_specs=(wide, wide, *params, P(), *params, *params, *params),
        check_vma=False,
    )
```

time: 1730 us -> 788 us (0.46)
  waiting for transfers between devices: 1320 us -> 264 us
  local copies, waits for them, and re-layouts: 75.6 us -> 168 us
  starting transfers between devices: 1.28 us -> 86.9 us
  matrix products: 174 us -> 112 us
  other arithmetic: 56.8 us -> 74.8 us
    reduce_scatter x8 -> x0, waiting for transfers between devices: 856 us -> none  [the longest x1 375 us: local(): lax.psum_scatter(local_grads[2], 'dp', scatter_dimension=1, tiled=True)]
    all_gather x8 -> x0, waiting for transfers between devices: 398 us -> none  [the longest x1 128 us: local(): lax.all_gather(gate_up_low, 'dp', axis=1, tiled=True)]
    ppermute x0 -> x51, waiting for transfers between devices: none -> 264 us  [swap(): return lax.ppermute(values, BOTH, pairs)]
    ppermute x0 -> x51, starting transfers between devices: none -> 86.9 us  [swap(): return lax.ppermute(values, BOTH, pairs)]
    slice x11 -> x32, local copies, waits for them, and re-layouts: 9.01 us -> 79.5 us  [the longest x3 31.3 us: normed_part(): all_normed.reshape(rows_all, blocks_half, 2, rows_each)[:, :, i]]
    dot_general x36 -> x17, matrix products: 174 us -> 107 us  [the longest x6 36.3 us: dot_rows(): lax.dot_general(a, b, (((0,), (0,)), ((), ())), preferred_element_type=jn...]
    unnamed x18 -> x0, waiting for transfers between devices: 65.4 us -> none
    unnamed x216 -> x237, local copies, waits for them, and re-layouts: 51.4 us -> 22.8 us
  transfers between devices with their start and end apart: 17 -> 51, of which waited for: 14 -> 20; matrix products, arithmetic and copies ran while one was open for 13% -> 27% of each run, Pallas kernels for 0% -> 0%
where the time goes in v1:
time: 788 us; the launch traced here: 779 us
  waiting for transfers between devices  264 us (34%)
  local copies, waits for them, and re-layouts  168 us (21%)
  matrix products  112 us (14%)
  starting transfers between devices  86.9 us (11%)
  other arithmetic  74.8 us (9%)
  blocking collectives  65.3 us (8%)
  between operations  8.46 us (1%)
    ppermute x51, waiting for transfers between devices, swap(): return lax.ppermute(values, BOTH, pairs)  264 us
    ppermute x51, starting transfers between devices, swap(): return lax.ppermute(values, BOTH, pairs)  86.9 us
    psum x1, blocking collectives, local(): norm_total = jnp.sqrt(lax.psum(square_local, BOTH))  37.9 us
    dot_general x6, matrix products, dot_rows(): lax.dot_general(a, b, (((0,), (0,)), ((), ())), preferred_element_type=jn...  36.3 us
    slice x3, local copies, waits for them, and re-layouts, normed_part(): all_normed.reshape(rows_all, blocks_half, 2, rows_each)[:, :, i]  31.3 us
    dot_general x3, matrix products, dot_cols(): lax.dot_general(a, b, (((1,), (1,)), ((), ())), preferred_element_type=jn...  29.8 us
    slice x3, local copies, waits for them, and re-layouts, grad_out_part(): all_cot.reshape(rows_all, blocks_half, 2, rows_each)[:, :, i]  29.6 us
    all_gather x1, blocking collectives, local(): lax.all_gather(norm_params.astype(jnp.bfloat16), 'dp', axis=1, tiled=True)  27.4 us
  transfers between devices with their start and end apart: 51, of which 20 were waited for; matrix products, arithmetic and copies ran while one was open for 27% of the time, Pallas kernels for 0%

profile of v1, /device:TPU:0, one launch (start us, length us, event | category | flops | bytes accessed | tf_op | source)
XLA Modules:
  0.0 779.1 jit_solution(7974501595369263709)
XLA Ops:
  13.0 27.4 %all_gather.3 = bf16[2,2048]{1,0:T(2,128)(2,1)S(1)} all-gather(bf16[2,256]{1,0:T(2,128)(2,1)S(1)} %convert_element_type.166), channel_id=1, replica_groups=mesh['dp'=8,'tensor'=4] {'dp'}, dimensions={1}, use_global_device_ids=true | all-gather | bytes 9216 | tf_op jit(solution)/shard_map/all_gather | solution.py:185
  71.2 26.0 %collective-permute-done.27 = bf16[2,80,2048]{2,1,0:T(8,128)(2,1)S(1)} collective-permute-done((bf16[2,80,2048]{2,1,0:T(8,128)(2,1)S(1)}, bf16[2,80,2048]{2,1,0:T(8,128)(2,1)S(1)}, u32[]{:S(2)}, u32[]{:S(2)}) %collective-permute-start.27) | collective-permute-done | bytes 655392 | tf_op jit(solution)/shard_map/ppermute | solution.py:31
  99.7 17.1 %collective-permute-done.11 = bf16[256,1408]{1,0:T(8,128)(2,1)S(1)} collective-permute-done((bf16[256,1408]{1,0:T(8,128)(2,1)S(1)}, bf16[256,1408]{1,0:T(8,128)(2,1)S(1)}, u32[]{:S(2)}, u32[]{:S(2)}) %collective-permute-start.11) | collective-permute-done | bytes 720928 | tf_op jit(solution)/shard_map/ppermute | solution.py:31
  118.1 26.8 %collective-permute-done.20 = bf16[960,256]{1,0:T(8,128)(2,1)S(1)} collective-permute-done((bf16[960,256]{1,0:T(8,128)(2,1)}, bf16[960,256]{1,0:T(8,128)(2,1)S(1)}, u32[]{:S(2)}, u32[]{:S(2)}) %collective-permute-start.20) | collective-permute-done | bytes 491552 | tf_op jit(solution)/shard_map/ppermute | solution.py:31
  150.3 36.0 %collective-permute-done.13 = bf16[256,1408]{1,0:T(8,128)(2,1)S(1)} collective-permute-done((bf16[256,1408]{1,0:T(8,128)(2,1)S(1)}, bf16[256,1408]{1,0:T(8,128)(2,1)S(1)}, u32[]{:S(2)}, u32[]{:S(2)}) %collective-permute-start.13) | collective-permute-done | bytes 720928 | tf_op jit(solution)/shard_map/ppermute | solution.py:31
  190.8 9.8 %collective-permute-done.21 = bf16[960,256]{1,0:T(8,128)(2,1)S(1)} collective-permute-done((bf16[960,256]{1,0:T(8,128)(2,1)S(1)}, bf16[960,256]{1,0:T(8,128)(2,1)S(1)}, u32[]{:S(2)}, u32[]{:S(2)}) %collective-permute-start.21) | collective-permute-done | bytes 491552 | tf_op jit(solution)/shard_map/ppermute | solution.py:31
  204.3 22.2 %collective-permute-done.23 = bf16[960,256]{1,0:T(8,128)(2,1)S(1)} collective-permute-done((bf16[960,256]{1,0:T(8,128)(2,1)S(1)}, bf16[960,256]{1,0:T(8,128)(2,1)S(1)}, u32[]{:S(2)}, u32[]{:S(2)}) %collective-permute-start.23) | collective-permute-done | bytes 491552 | tf_op jit(solution)/shard_map/ppermute | solution.py:31
  228.8 12.0 %collective-permute-done.14 = bf16[256,1408]{1,0:T(8,128)(2,1)S(1)} collective-permute-done((bf16[256,1408]{1,0:T(8,128)(2,1)S(1)}, bf16[256,1408]{1,0:T(8,128)(2,1)S(1)}, u32[]{:S(2)}, u32[]{:S(2)}) %collective-permute-start.14) | collective-permute-done | bytes 720928 | tf_op jit(solution)/shard_map/ppermute | solution.py:31
  243.0 5.6 collective-permute-done.16
  252.0 4.3 fusion.122
  258.9 4.0 reshape.277
  268.8 4.0 reshape.279
  288.0 5.1 pad_maximum_fusion.1
  293.1 9.4 %reshape_reshape.5 = bf16[1280,4,2,256]{3,2,1,0:T(2,128)(2,1)} reshape(bf16[16,80,2048]{2,1,0:T(8,128)(2,1)} %pad_maximum_fusion.1) | data formatting | bytes 10485760 | tf_op jit(solution)/shard_map/reshape;reshape | solution.py:260
  302.5 8.7 %convolution_convert_fusion = bf16[1280,960]{1,0:T(8,128)(2,1)S(1)} fusion(bf16[1280,2048]{1,0:T(8,128)(2,1)} %bitcast.247, bf16[960,2048]{1,0:T(8,128)(2,1)} %copy-done.70), kind=kOutput, calls=%fused_computation.29 | convolution fusion | flops 5034393600 | bytes 11632640 | tf_op jit(solution)/shard_map/dot_general | solution.py:116
  317.2 5.1 fusion.118
  322.3 5.1 fusion.80
  328.1 4.5 multiply_reduce_fusion
  332.5 7.0 multiply_convert_fusion
  344.1 4.6 fusion.77
  348.7 9.4 %reshape_reshape.4 = bf16[1280,4,2,256]{3,2,1,0:T(2,128)(2,1)} reshape(bf16[16,80,2048]{2,1,0:T(8,128)(2,1)} %copy-done.2) | data formatting | bytes 10485760 | tf_op jit(solution)/shard_map/reshape;reshape | solution.py:272
  362.1 12.0 %fusion.123 = f32[1280,1408]{1,0:T(8,128)S(1)} fusion(bf16[1280,2048]{1,0:T(8,128)(2,1)} %bitcast.246, bf16[2048,1408]{1,0:T(8,128)(2,1)} %copy-done.68), kind=kOutput, calls=%fused_computation.322 | convolution fusion | flops 7381975040 | bytes 18219008 | tf_op jit(solution)/shard_map/dot_general | solution.py:108
  374.1 4.4 fusion.5
  378.5 8.9 %fusion.106 = (bf16[1280,4,1,256]{3,2,1,0:T(2,128)(2,1)}, bf16[1280,4,1,256]{3,2,1,0:T(2,128)(2,1)}) fusion(bf16[1280,4,2,256]{3,2,1,0:T(2,128)(2,1)S(1)} %bitcast.242), kind=kLoop, calls=%fused_computation.305 | loop fusion | bytes 10485760 | tf_op jit(solution)/shard_map/slice | solution.py:260
  387.5 9.6 %copy.81 = bf16[1280,4,1,256]{0,3,1,2:T(8,128)(2,1)S(1)} copy(bf16[1280,4,1,256]{3,2,1,0:T(2,128)(2,1)} %get-tuple-element.63) | data formatting | bytes 5242880 | tf_op jit(solution)/shard_map/slice | solution.py:260
  397.1 6.2 convert_bitcast_fusion
  411.5 11.8 %fusion.107 = (bf16[1280,4,1,256]{3,2,1,0:T(2,128)(2,1)}, bf16[1280,4,1,256]{3,2,1,0:T(2,128)(2,1)}) fusion(bf16[1280,4,2,256]{3,2,1,0:T(2,128)(2,1)} %reshape_reshape.4), kind=kLoop, calls=%fused_computation.306 | loop fusion | bytes 10485760 | tf_op jit(solution)/shard_map/slice | solution.py:272
  423.4 9.7 %copy.78 = bf16[1280,4,1,256]{0,3,1,2:T(8,128)(2,1)S(1)} copy(bf16[1280,4,1,256]{3,2,1,0:T(2,128)(2,1)} %get-tuple-element.65) | data formatting | bytes 5242880 | tf_op jit(solution)/shard_map/slice | solution.py:272
  433.1 5.6 fusion.47
  439.0 12.9 %fusion.86 = f32[1280,2048]{1,0:T(8,128)} fusion(bf16[2048,1408]{1,0:T(8,128)(2,1)} %copy-done.68, bf16[1280,704]{1,0:T(8,128)(2,1)S(1)} %copy-done.48, bf16[1280,704]{1,0:T(8,128)(2,1)S(1)} %copy-done.46), kind=kOutput, calls=%fused_computation.146 | convolution fusion | flops 7389184000 | bytes 19857408 | tf_op jit(solution)/shard_map/dot_general | solution.py:116
  452.0 8.2 %convolution_add_fusion = f32[1280,2048]{1,0:T(8,128)S(1)} fusion(f32[1280,2048]{1,0:T(8,128)} %fusion.86, bf16[2048,768]{1,0:T(8,128)(2,1)} %copy-done.73, bf16[1280,256]{1,0:T(8,128)(2,1)S(1)} %bitcast.266, bf16[1280,256]{1,0:T(8,128)(2,1)S(1)} %bitcast.263, bf16[1280,256]{1,0:T(8,128)(2,1)S(1)} %bitcast.260), kind=kOutput, calls=%fused_computation.1 | convolution fusion | flops 4035051520 | bytes 26083328 | tf_op jit(solution)/shard_map/dot_general | solution.py:116
  460.2 5.7 fusion.85
  471.3 11.1 %copy.79 = bf16[1280,4,1,256]{0,3,1,2:T(8,128)(2,1)} copy(bf16[1280,4,1,256]{3,2,1,0:T(2,128)(2,1)} %get-tuple-element.62) | data formatting | bytes 5242880 | tf_op jit(solution)/shard_map/slice | solution.py:260
  482.4 9.8 %copy.77 = bf16[1280,4,1,256]{0,3,1,2:T(8,128)(2,1)S(1)} copy(bf16[1280,4,1,256]{3,2,1,0:T(2,128)(2,1)} %get-tuple-element.64) | data formatting | bytes 5242880 | tf_op jit(solution)/shard_map/slice | solution.py:272
  492.2 9.7 %convolution_convert_fusion.1 = bf16[4,256,1408]{2,1,0:T(8,128)(2,1)} fusion(bf16[1280,4,1,256]{0,3,1,2:T(8,128)(2,1)} %copy-done.39, bf16[1280,704]{1,0:T(8,128)(2,1)} %get-tuple-element.60, bf16[1280,704]{1,0:T(8,128)(2,1)} %get-tuple-element.59), kind=kOutput, calls=%fused_computation.30 | convolution fusion | flops 3699638272 | bytes 9109504 | tf_op jit(solution)/shard_map/dot_general | solution.py:112
  503.7 3.8 fusion.119
  512.0 4.6 fusion.120
  516.8 19.1 %collective-permute-done.35 = bf16[256,768]{1,0:T(8,128)(2,1)S(1)} collective-permute-done((bf16[256,768]{1,0:T(8,128)(2,1)S(1)}, bf16[256,768]{1,0:T(8,128)(2,1)S(1)}, u32[]{:S(2)}, u32[]{:S(2)}) %collective-permute-start.35) | collective-permute-done | bytes 393248 | tf_op jit(solution)/shard_map/ppermute | solution.py:31
  536.1 19.2 %collective-permute-start.39 = (bf16[960,256]{1,0:T(8,128)(2,1)S(1)}, bf16[960,256]{1,0:T(8,128)(2,1)S(1)}, u32[]{:S(2)}, u32[]{:S(2)}) collective-permute-start(bf16[960,256]{1,0:T(8,128)(2,1)S(1)} %get-tuple-element.81), channel_id=1, source_target_pairs={{0,8},{1,9},{2,10},{3,11},{4,12},{5,13},{6,14},{7,15},{8,0},{9,1},... | collective-permute-start | bytes 1474568 | tf_op jit(solution)/shard_map/ppermute | solution.py:31
  560.2 26.1 %collective-permute-done.39 = bf16[960,256]{1,0:T(8,128)(2,1)S(1)} collective-permute-done((bf16[960,256]{1,0:T(8,128)(2,1)S(1)}, bf16[960,256]{1,0:T(8,128)(2,1)S(1)}, u32[]{:S(2)}, u32[]{:S(2)}) %collective-permute-start.39) | collective-permute-done | bytes 491552 | tf_op jit(solution)/shard_map/ppermute | solution.py:31
  597.3 6.5 fusion.121
  613.3 26.2 %collective-permute-done.42 = bf16[256,1408]{1,0:T(8,128)(2,1)S(1)} collective-permute-done((bf16[256,1408]{1,0:T(8,128)(2,1)S(1)}, bf16[256,1408]{1,0:T(8,128)(2,1)S(1)}, u32[]{:S(2)}, u32[]{:S(2)}) %collective-permute-start.42) | collective-permute-done | bytes 720928 | tf_op jit(solution)/shard_map/ppermute | solution.py:31
  639.7 14.3 %collective-permute-done.43 = bf16[256,1408]{1,0:T(8,128)(2,1)S(1)} collective-permute-done((bf16[256,1408]{1,0:T(8,128)(2,1)S(1)}, bf16[256,1408]{1,0:T(8,128)(2,1)S(1)}, u32[]{:S(2)}, u32[]{:S(2)}) %collective-permute-start.43) | collective-permute-done | bytes 720928 | tf_op jit(solution)/shard_map/ppermute | solution.py:31
  656.5 15.8 %collective-permute-start.32 = (bf16[2,80,2048]{2,1,0:T(8,128)(2,1)}, bf16[2,80,2048]{2,1,0:T(8,128)(2,1)}, u32[]{:S(2)}, u32[]{:S(2)}) collective-permute-start(bf16[2,80,2048]{2,1,0:T(8,128)(2,1)} %slice.667), channel_id=1, source_target_pairs={{0,8},{1,9},{2,10},{3,11},{4,12},{5,13},{6,14},{7,15},{8,0},{9,1},... | collective-permute-start | bytes 1966088 | tf_op jit(solution)/shard_map/ppermute | solution.py:31
  678.4 9.7 %collective-permute-done.32 = bf16[2,80,2048]{2,1,0:T(8,128)(2,1)} collective-permute-done((bf16[2,80,2048]{2,1,0:T(8,128)(2,1)}, bf16[2,80,2048]{2,1,0:T(8,128)(2,1)}, u32[]{:S(2)}, u32[]{:S(2)}) %collective-permute-start.32) | collective-permute-done | bytes 655392 | tf_op jit(solution)/shard_map/ppermute | solution.py:31
  720.6 37.9 %psum.7 = f32[]{:T(128)} all-reduce(f32[]{:T(128)S(6)} %add.343), channel_id=1, replica_groups=mesh['dp'=8,'tensor'=4] {'dp','tensor'}, use_global_device_ids=true, to_apply=%region_14.15 | all-reduce | flops 1 | bytes 8 | tf_op jit(solution)/shard_map/psum | solution.py:346
  759.8 5.6 multiply_subtract_fusion.2
  766.6 5.0 multiply_subtract_fusion
  (454 shorter events, 197.3 us)
Async XLA Ops:
  3.5 53.1 %collective-permute-start.3 = (bf16[256,768]{1,0:T(8,128)(2,1)}, bf16[256,768]{1,0:T(8,128)(2,1)}, u32[]{:S(2)}, u32[]{:S(2)}) collective-permute-start(bf16[256,768]{1,0:T(8,128)(2,1)} %get-tuple-element.54), channel_id=1, source_target_pairs={{0,4},{1,5},{2,6},{3,7},{4,0},{5,1},{6,2},{7,3},{8,12},{9,13},{10,... | collective-permute-start | bytes 1179656 | tf_op jit(solution)/shard_map/ppermute | solution.py:31
  6.4 91.0 %collective-permute-start.6 = (bf16[256,768]{1,0:T(8,128)(2,1)}, bf16[256,768]{1,0:T(8,128)(2,1)}, u32[]{:S(2)}, u32[]{:S(2)}) collective-permute-start(bf16[256,768]{1,0:T(8,128)(2,1)} %get-tuple-element.54), channel_id=1, source_target_pairs={{0,16},{1,17},{2,18},{3,19},{4,20},{5,21},{6,22},{7,23},{8,24},{9,... | collective-permute-start | bytes 1179656 | tf_op jit(solution)/shard_map/ppermute | solution.py:31
  9.0 50.8 %collective-permute-start.4 = (bf16[256,768]{1,0:T(8,128)(2,1)}, bf16[256,768]{1,0:T(8,128)(2,1)}, u32[]{:S(2)}, u32[]{:S(2)}) collective-permute-start(bf16[256,768]{1,0:T(8,128)(2,1)} %get-tuple-element.105), channel_id=1, source_target_pairs={{0,8},{1,9},{2,10},{3,11},{4,12},{5,13},{6,14},{7,15},{8,0},{9,1},... | collective-permute-start | bytes 1179656 | tf_op jit(solution)/shard_map/ppermute | solution.py:31
  41.9 19.1 %collective-permute-start = (bf16[2,80,2048]{2,1,0:T(8,128)(2,1)}, bf16[2,80,2048]{2,1,0:T(8,128)(2,1)}, u32[]{:S(2)}, u32[]{:S(2)}) collective-permute-start(bf16[2,80,2048]{2,1,0:T(8,128)(2,1)} %fusion.68), channel_id=1, source_target_pairs={{0,8},{1,9},{2,10},{3,11},{4,12},{5,13},{6,14},{7,15},{8,0},{9,1},... | collective-permute-start | bytes 1966088 | tf_op jit(solution)/shard_map/ppermute | solution.py:31
  43.5 22.0 %collective-permute-start.17 = (bf16[960,256]{1,0:T(8,128)(2,1)}, bf16[960,256]{1,0:T(8,128)(2,1)}, u32[]{:S(2)}, u32[]{:S(2)}) collective-permute-start(bf16[960,256]{1,0:T(8,128)(2,1)} %get-tuple-element.58), channel_id=1, source_target_pairs={{0,4},{1,5},{2,6},{3,7},{4,0},{5,1},{6,2},{7,3},{8,12},{9,13},{10,... | collective-permute-start | bytes 1474568 | tf_op jit(solution)/shard_map/ppermute | solution.py:31
  56.6 14.2 %collective-permute-start.18 = (bf16[960,256]{1,0:T(8,128)(2,1)S(1)}, bf16[960,256]{1,0:T(8,128)(2,1)S(1)}, u32[]{:S(2)}, u32[]{:S(2)}) collective-permute-start(bf16[960,256]{1,0:T(8,128)(2,1)S(1)} %copy-done.64), channel_id=1, source_target_pairs={{0,8},{1,9},{2,10},{3,11},{4,12},{5,13},{6,14},{7,15},{8,0},{9,1},... | collective-permute-start | bytes 1474568 | tf_op jit(solution)/shard_map/ppermute | solution.py:31
  59.9 37.3 %collective-permute-start.27 = (bf16[2,80,2048]{2,1,0:T(8,128)(2,1)S(1)}, bf16[2,80,2048]{2,1,0:T(8,128)(2,1)S(1)}, u32[]{:S(2)}, u32[]{:S(2)}) collective-permute-start(bf16[2,80,2048]{2,1,0:T(8,128)(2,1)S(1)} %constant_dynamic-update-slice_fusion.48), channel_id=1, source_target_pairs={{0,8},{1,9},{2,10},{3,11},{4,12},{5,13},{6,14},{7,15},{8,0},{9,1},... | collective-permute-start | bytes 1966088 | tf_op jit(solution)/shard_map/ppermute | solution.py:31
  61.0 36.5 %collective-permute-start.10 = (bf16[256,1408]{1,0:T(8,128)(2,1)S(1)}, bf16[256,1408]{1,0:T(8,128)(2,1)S(1)}, u32[]{:S(2)}, u32[]{:S(2)}) collective-permute-start(bf16[256,1408]{1,0:T(8,128)(2,1)S(1)} %get-tuple-element.56), channel_id=1, source_target_pairs={{0,4},{1,5},{2,6},{3,7},{4,0},{5,1},{6,2},{7,3},{8,12},{9,13},{10,... | collective-permute-start | bytes 2162696 | tf_op jit(solution)/shard_map/ppermute | solution.py:31
  65.5 81.4 %collective-permute-start.1 = (bf16[4,80,2048]{2,1,0:T(8,128)(2,1)S(1)}, bf16[4,80,2048]{2,1,0:T(8,128)(2,1)S(1)}, u32[]{:S(2)}, u32[]{:S(2)}) collective-permute-start(bf16[4,80,2048]{2,1,0:T(8,128)(2,1)S(1)} %maximum_maximum_fusion), channel_id=1, source_target_pairs={{0,2},{1,3},{2,0},{3,1},{4,6},{5,7},{6,4},{7,5},{8,10},{9,11},{10,... | collective-permute-start | bytes 3932168 | tf_op jit(solution)/shard_map/ppermute | solution.py:31
  70.8 47.2 %collective-permute-start.8 = (bf16[256,768]{1,0:T(8,128)(2,1)}, bf16[256,768]{1,0:T(8,128)(2,1)S(1)}, u32[]{:S(2)}, u32[]{:S(2)}) collective-permute-start(bf16[256,768]{1,0:T(8,128)(2,1)} %get-tuple-element.105), channel_id=1, source_target_pairs={{0,24},{1,25},{2,26},{3,27},{4,28},{5,29},{6,30},{7,31},{8,16},{9,... | collective-permute-start | bytes 1179656 | tf_op jit(solution)/shard_map/ppermute | solution.py:31
  97.2 19.6 %collective-permute-start.11 = (bf16[256,1408]{1,0:T(8,128)(2,1)S(1)}, bf16[256,1408]{1,0:T(8,128)(2,1)S(1)}, u32[]{:S(2)}, u32[]{:S(2)}) collective-permute-start(bf16[256,1408]{1,0:T(8,128)(2,1)S(1)} %get-tuple-element.99), channel_id=1, source_target_pairs={{0,8},{1,9},{2,10},{3,11},{4,12},{5,13},{6,14},{7,15},{8,0},{9,1},... | collective-permute-start | bytes 2162696 | tf_op jit(solution)/shard_map/ppermute | solution.py:31
  97.4 47.5 %collective-permute-start.20 = (bf16[960,256]{1,0:T(8,128)(2,1)}, bf16[960,256]{1,0:T(8,128)(2,1)S(1)}, u32[]{:S(2)}, u32[]{:S(2)}) collective-permute-start(bf16[960,256]{1,0:T(8,128)(2,1)} %get-tuple-element.58), channel_id=1, source_target_pairs={{0,16},{1,17},{2,18},{3,19},{4,20},{5,21},{6,22},{7,23},{8,24},{9,... | collective-permute-start | bytes 1474568 | tf_op jit(solution)/shard_map/ppermute | solution.py:31
  97.5 20.3 %collective-permute-start.5 = (bf16[256,768]{1,0:T(8,128)(2,1)}, bf16[256,768]{1,0:T(8,128)(2,1)S(1)}, u32[]{:S(2)}, u32[]{:S(2)}) collective-permute-start(bf16[256,768]{1,0:T(8,128)(2,1)} %collective-permute-done.4), channel_id=1, source_target_pairs={{0,4},{1,5},{2,6},{3,7},{4,0},{5,1},{6,2},{7,3},{8,12},{9,13},{10,... | collective-permute-start | bytes 1179656 | tf_op jit(solution)/shard_map/ppermute | solution.py:31
  116.8 31.6 %collective-permute-start.22 = (bf16[960,256]{1,0:T(8,128)(2,1)S(1)}, bf16[960,256]{1,0:T(8,128)(2,1)S(1)}, u32[]{:S(2)}, u32[]{:S(2)}) collective-permute-start(bf16[960,256]{1,0:T(8,128)(2,1)S(1)} %copy-done.64), channel_id=1, source_target_pairs={{0,24},{1,25},{2,26},{3,27},{4,28},{5,29},{6,30},{7,31},{8,16},{9,... | collective-permute-start | bytes 1474568 | tf_op jit(solution)/shard_map/ppermute | solution.py:31
  117.9 68.5 %collective-permute-start.13 = (bf16[256,1408]{1,0:T(8,128)(2,1)S(1)}, bf16[256,1408]{1,0:T(8,128)(2,1)S(1)}, u32[]{:S(2)}, u32[]{:S(2)}) collective-permute-start(bf16[256,1408]{1,0:T(8,128)(2,1)S(1)} %get-tuple-element.56), channel_id=1, source_target_pairs={{0,16},{1,17},{2,18},{3,19},{4,20},{5,21},{6,22},{7,23},{8,24},{9,... | collective-permute-start | bytes 2162696 | tf_op jit(solution)/shard_map/ppermute | solution.py:31
  118.0 31.4 %collective-permute-start.7 = (bf16[256,768]{1,0:T(8,128)(2,1)}, bf16[256,768]{1,0:T(8,128)(2,1)S(1)}, u32[]{:S(2)}, u32[]{:S(2)}) collective-permute-start(bf16[256,768]{1,0:T(8,128)(2,1)} %collective-permute-done.6), channel_id=1, source_target_pairs={{0,4},{1,5},{2,6},{3,7},{4,0},{5,1},{6,2},{7,3},{8,12},{9,13},{10,... | collective-permute-start | bytes 1179656 | tf_op jit(solution)/shard_map/ppermute | solution.py:31
  144.9 43.5 %collective-permute-start.9 = (bf16[256,768]{1,0:T(8,128)(2,1)S(1)}, bf16[256,768]{1,0:T(8,128)(2,1)S(1)}, u32[]{:S(2)}, u32[]{:S(2)}) collective-permute-start(bf16[256,768]{1,0:T(8,128)(2,1)S(1)} %collective-permute-done.8), channel_id=1, source_target_pairs={{0,4},{1,5},{2,6},{3,7},{4,0},{5,1},{6,2},{7,3},{8,12},{9,13},{10,... | collective-permute-start | bytes 1179656 | tf_op jit(solution)/shard_map/ppermute | solution.py:31
  147.0 41.6 %collective-permute-start.19 = (bf16[960,256]{1,0:T(8,128)(2,1)S(1)}, bf16[960,256]{1,0:T(8,128)(2,1)S(1)}, u32[]{:S(2)}, u32[]{:S(2)}) collective-permute-start(bf16[960,256]{1,0:T(8,128)(2,1)S(1)} %collective-permute-done.18), channel_id=1, source_target_pairs={{0,4},{1,5},{2,6},{3,7},{4,0},{5,1},{6,2},{7,3},{8,12},{9,13},{10,... | collective-permute-start | bytes 1474568 | tf_op jit(solution)/shard_map/ppermute | solution.py:31
  148.4 100.3 %collective-permute-start.2 = (bf16[8,80,2048]{2,1,0:T(8,128)(2,1)S(1)}, bf16[8,80,2048]{2,1,0:T(8,128)(2,1)S(1)}, u32[]{:S(2)}, u32[]{:S(2)}) collective-permute-start(bf16[8,80,2048]{2,1,0:T(8,128)(2,1)S(1)} %pad_maximum_fusion.4), channel_id=1, source_target_pairs={{0,1},{1,0},{2,3},{3,2},{4,5},{5,4},{6,7},{7,6},{8,9},{9,8},{10,11... | collective-permute-start | bytes 7864328 | tf_op jit(solution)/shard_map/ppermute | solution.py:31
  149.5 52.6 %collective-permute-start.15 = (bf16[256,1408]{1,0:T(8,128)(2,1)S(1)}, bf16[256,1408]{1,0:T(8,128)(2,1)S(1)}, u32[]{:S(2)}, u32[]{:S(2)}) collective-permute-start(bf16[256,1408]{1,0:T(8,128)(2,1)S(1)} %get-tuple-element.99), channel_id=1, source_target_pairs={{0,24},{1,25},{2,26},{3,27},{4,28},{5,29},{6,30},{7,31},{8,16},{9,... | collective-permute-start | bytes 2162696 | tf_op jit(solution)/shard_map/ppermute | solution.py:31
  186.3 14.2 %collective-permute-start.21 = (bf16[960,256]{1,0:T(8,128)(2,1)S(1)}, bf16[960,256]{1,0:T(8,128)(2,1)S(1)}, u32[]{:S(2)}, u32[]{:S(2)}) collective-permute-start(bf16[960,256]{1,0:T(8,128)(2,1)S(1)} %collective-permute-done.20), channel_id=1, source_target_pairs={{0,4},{1,5},{2,6},{3,7},{4,0},{5,1},{6,2},{7,3},{8,12},{9,13},{10,... | collective-permute-start | bytes 1474568 | tf_op jit(solution)/shard_map/ppermute | solution.py:31
  188.4 40.2 %collective-permute-start.12 = (bf16[256,1408]{1,0:T(8,128)(2,1)S(1)}, bf16[256,1408]{1,0:T(8,128)(2,1)S(1)}, u32[]{:S(2)}, u32[]{:S(2)}) collective-permute-start(bf16[256,1408]{1,0:T(8,128)(2,1)S(1)} %collective-permute-done.11), channel_id=1, source_target_pairs={{0,4},{1,5},{2,6},{3,7},{4,0},{5,1},{6,2},{7,3},{8,12},{9,13},{10,... | collective-permute-start | bytes 2162696 | tf_op jit(solution)/shard_map/ppermute | solution.py:31
  188.6 37.9 %collective-permute-start.23 = (bf16[960,256]{1,0:T(8,128)(2,1)S(1)}, bf16[960,256]{1,0:T(8,128)(2,1)S(1)}, u32[]{:S(2)}, u32[]{:S(2)}) collective-permute-start(bf16[960,256]{1,0:T(8,128)(2,1)S(1)} %collective-permute-done.22), channel_id=1, source_target_pairs={{0,4},{1,5},{2,6},{3,7},{4,0},{5,1},{6,2},{7,3},{8,12},{9,13},{10,... | collective-permute-start | bytes 1474568 | tf_op jit(solution)/shard_map/ppermute | solution.py:31
  200.5 40.5 %collective-permute-start.28 = (bf16[4,80,2048]{2,1,0:T(8,128)(2,1)S(1)}, bf16[4,80,2048]{2,1,0:T(8,128)(2,1)S(1)}, u32[]{:S(2)}, u32[]{:S(2)}) collective-permute-start(bf16[4,80,2048]{2,1,0:T(8,128)(2,1)S(1)} %maximum_maximum_fusion.1), channel_id=1, source_target_pairs={{0,2},{1,3},{2,0},{3,1},{4,6},{5,7},{6,4},{7,5},{8,10},{9,11},{10,... | collective-permute-start | bytes 3932168 | tf_op jit(solution)/shard_map/ppermute | solution.py:31
  202.1 38.7 %collective-permute-start.14 = (bf16[256,1408]{1,0:T(8,128)(2,1)S(1)}, bf16[256,1408]{1,0:T(8,128)(2,1)S(1)}, u32[]{:S(2)}, u32[]{:S(2)}) collective-permute-start(bf16[256,1408]{1,0:T(8,128)(2,1)S(1)} %collective-permute-done.13), channel_id=1, source_target_pairs={{0,4},{1,5},{2,6},{3,7},{4,0},{5,1},{6,2},{7,3},{8,12},{9,13},{10,... | collective-permute-start | bytes 2162696 | tf_op jit(solution)/shard_map/ppermute | solution.py:31
  226.5 22.0 %collective-permute-start.16 = (bf16[256,1408]{1,0:T(8,128)(2,1)S(1)}, bf16[256,1408]{1,0:T(8,128)(2,1)S(1)}, u32[]{:S(2)}, u32[]{:S(2)}) collective-permute-start(bf16[256,1408]{1,0:T(8,128)(2,1)S(1)} %collective-permute-done.15), channel_id=1, source_target_pairs={{0,4},{1,5},{2,6},{3,7},{4,0},{5,1},{6,2},{7,3},{8,12},{9,13},{10,... | collective-permute-start | bytes 2162696 | tf_op jit(solution)/shard_map/ppermute | solution.py:31
  243.0 44.9 %collective-permute-start.29 = (bf16[8,80,2048]{2,1,0:T(8,128)(2,1)}, bf16[8,80,2048]{2,1,0:T(8,128)(2,1)}, u32[]{:S(2)}, u32[]{:S(2)}) collective-permute-start(bf16[8,80,2048]{2,1,0:T(8,128)(2,1)} %pad_maximum_fusion.6), channel_id=1, source_target_pairs={{0,1},{1,0},{2,3},{3,2},{4,5},{5,4},{6,7},{7,6},{8,9},{9,8},{10,11... | collective-permute-start | bytes 7864328 | tf_op jit(solution)/shard_map/ppermute | solution.py:31
  403.3 106.5 %collective-permute-start.37 = (bf16[4,960,256]{2,1,0:T(8,128)(2,1)}, bf16[4,960,256]{2,1,0:T(8,128)(2,1)}, u32[]{:S(2)}, u32[]{:S(2)}) collective-permute-start(bf16[4,960,256]{2,1,0:T(8,128)(2,1)} %convert_bitcast_fusion), channel_id=1, source_target_pairs={{0,4},{1,5},{2,6},{3,7},{4,0},{5,1},{6,2},{7,3},{8,12},{9,13},{10,... | collective-permute-start | bytes 5898248 | tf_op jit(solution)/shard_map/ppermute | solution.py:31
  438.7 65.0 %collective-permute-start.33 = (bf16[4,256,768]{2,1,0:T(8,128)(2,1)}, bf16[4,256,768]{2,1,0:T(8,128)(2,1)}, u32[]{:S(2)}, u32[]{:S(2)}) collective-permute-start(bf16[4,256,768]{2,1,0:T(8,128)(2,1)} %fusion.47), channel_id=1, source_target_pairs={{0,4},{1,5},{2,6},{3,7},{4,0},{5,1},{6,2},{7,3},{8,12},{9,13},{10,... | collective-permute-start | bytes 4718600 | tf_op jit(solution)/shard_map/ppermute | solution.py:31
  501.9 95.4 %collective-permute-start.41 = (bf16[4,256,1408]{2,1,0:T(8,128)(2,1)}, bf16[4,256,1408]{2,1,0:T(8,128)(2,1)}, u32[]{:S(2)}, u32[]{:S(2)}) collective-permute-start(bf16[4,256,1408]{2,1,0:T(8,128)(2,1)} %convolution_convert_fusion.1), channel_id=1, source_target_pairs={{0,4},{1,5},{2,6},{3,7},{4,0},{5,1},{6,2},{7,3},{8,12},{9,13},{10,... | collective-permute-start | bytes 8650760 | tf_op jit(solution)/shard_map/ppermute | solution.py:31
  503.6 87.9 %collective-permute-start.30 = (bf16[8,80,2048]{2,1,0:T(8,128)(2,1)}, bf16[8,80,2048]{2,1,0:T(8,128)(2,1)}, u32[]{:S(2)}, u32[]{:S(2)}) collective-permute-start(bf16[8,80,2048]{2,1,0:T(8,128)(2,1)} %bitcast.33), channel_id=1, source_target_pairs={{0,1},{1,0},{2,3},{3,2},{4,5},{5,4},{6,7},{7,6},{8,9},{9,8},{10,11... | collective-permute-start | bytes 7864328 | tf_op jit(solution)/shard_map/ppermute | solution.py:31
  507.6 47.8 %collective-permute-start.34 = (bf16[256,768]{1,0:T(8,128)(2,1)S(1)}, bf16[256,768]{1,0:T(8,128)(2,1)S(1)}, u32[]{:S(2)}, u32[]{:S(2)}) collective-permute-start(bf16[256,768]{1,0:T(8,128)(2,1)S(1)} %get-tuple-element.96), channel_id=1, source_target_pairs={{0,16},{1,17},{2,18},{3,19},{4,20},{5,21},{6,22},{7,23},{8,24},{9,... | collective-permute-start | bytes 1179656 | tf_op jit(solution)/shard_map/ppermute | solution.py:31
  507.6 28.2 %collective-permute-start.35 = (bf16[256,768]{1,0:T(8,128)(2,1)S(1)}, bf16[256,768]{1,0:T(8,128)(2,1)S(1)}, u32[]{:S(2)}, u32[]{:S(2)}) collective-permute-start(bf16[256,768]{1,0:T(8,128)(2,1)S(1)} %get-tuple-element.98), channel_id=1, source_target_pairs={{0,8},{1,9},{2,10},{3,11},{4,12},{5,13},{6,14},{7,15},{8,0},{9,1},... | collective-permute-start | bytes 1179656 | tf_op jit(solution)/shard_map/ppermute | solution.py:31
  509.8 26.3 %collective-permute-start.36 = (bf16[256,768]{1,0:T(8,128)(2,1)S(1)}, bf16[256,768]{1,0:T(8,128)(2,1)S(1)}, u32[]{:S(2)}, u32[]{:S(2)}) collective-permute-start(bf16[256,768]{1,0:T(8,128)(2,1)S(1)} %get-tuple-element.97), channel_id=1, source_target_pairs={{0,24},{1,25},{2,26},{3,27},{4,28},{5,29},{6,30},{7,31},{8,16},{9,... | collective-permute-start | bytes 1179656 | tf_op jit(solution)/shard_map/ppermute | solution.py:31
  535.9 50.6 %collective-permute-start.38 = (bf16[960,256]{1,0:T(8,128)(2,1)S(1)}, bf16[960,256]{1,0:T(8,128)(2,1)S(1)}, u32[]{:S(2)}, u32[]{:S(2)}) collective-permute-start(bf16[960,256]{1,0:T(8,128)(2,1)S(1)} %get-tuple-element.79), channel_id=1, source_target_pairs={{0,16},{1,17},{2,18},{3,19},{4,20},{5,21},{6,22},{7,23},{8,24},{9,... | collective-permute-start | bytes 1474568 | tf_op jit(solution)/shard_map/ppermute | solution.py:31
  536.1 50.2 %collective-permute-start.39 = (bf16[960,256]{1,0:T(8,128)(2,1)S(1)}, bf16[960,256]{1,0:T(8,128)(2,1)S(1)}, u32[]{:S(2)}, u32[]{:S(2)}) collective-permute-start(bf16[960,256]{1,0:T(8,128)(2,1)S(1)} %get-tuple-element.81), channel_id=1, source_target_pairs={{0,8},{1,9},{2,10},{3,11},{4,12},{5,13},{6,14},{7,15},{8,0},{9,1},... | collective-permute-start | bytes 1474568 | tf_op jit(solution)/shard_map/ppermute | solution.py:31
  555.4 31.0 %collective-permute-start.40 = (bf16[960,256]{1,0:T(8,128)(2,1)S(1)}, bf16[960,256]{1,0:T(8,128)(2,1)S(1)}, u32[]{:S(2)}, u32[]{:S(2)}) collective-permute-start(bf16[960,256]{1,0:T(8,128)(2,1)S(1)} %get-tuple-element.80), channel_id=1, source_target_pairs={{0,24},{1,25},{2,26},{3,27},{4,28},{5,29},{6,30},{7,31},{8,16},{9,... | collective-permute-start | bytes 1474568 | tf_op jit(solution)/shard_map/ppermute | solution.py:31
  586.3 22.1 %collective-permute-start.24 = (bf16[8,80,2048]{2,1,0:T(8,128)(2,1)}, bf16[8,80,2048]{2,1,0:T(8,128)(2,1)}, u32[]{:S(2)}, u32[]{:S(2)}) collective-permute-start(bf16[8,80,2048]{2,1,0:T(8,128)(2,1)} %bitcast.20), channel_id=1, source_target_pairs={{0,1},{1,0},{2,3},{3,2},{4,5},{5,4},{6,7},{7,6},{8,9},{9,8},{10,11... | collective-permute-start | bytes 7864328 | tf_op jit(solution)/shard_map/ppermute | solution.py:31
  595.7 59.5 %collective-permute-start.31 = (bf16[4,80,2048]{2,1,0:T(8,128)(2,1)S(1)}, bf16[4,80,2048]{2,1,0:T(8,128)(2,1)S(1)}, u32[]{:S(2)}, u32[]{:S(2)}) collective-permute-start(bf16[4,80,2048]{2,1,0:T(8,128)(2,1)S(1)} %slice.665), channel_id=1, source_target_pairs={{0,2},{1,3},{2,0},{3,1},{4,6},{5,7},{6,4},{7,5},{8,10},{9,11},{10,... | collective-permute-start | bytes 3932168 | tf_op jit(solution)/shard_map/ppermute | solution.py:31
  604.0 35.5 %collective-permute-start.42 = (bf16[256,1408]{1,0:T(8,128)(2,1)S(1)}, bf16[256,1408]{1,0:T(8,128)(2,1)S(1)}, u32[]{:S(2)}, u32[]{:S(2)}) collective-permute-start(bf16[256,1408]{1,0:T(8,128)(2,1)S(1)} %get-tuple-element.72), channel_id=1, source_target_pairs={{0,16},{1,17},{2,18},{3,19},{4,20},{5,21},{6,22},{7,23},{8,24},{9,... | collective-permute-start | bytes 2162696 | tf_op jit(solution)/shard_map/ppermute | solution.py:31
  605.4 48.6 %collective-permute-start.43 = (bf16[256,1408]{1,0:T(8,128)(2,1)S(1)}, bf16[256,1408]{1,0:T(8,128)(2,1)S(1)}, u32[]{:S(2)}, u32[]{:S(2)}) collective-permute-start(bf16[256,1408]{1,0:T(8,128)(2,1)S(1)} %get-tuple-element.74), channel_id=1, source_target_pairs={{0,8},{1,9},{2,10},{3,11},{4,12},{5,13},{6,14},{7,15},{8,0},{9,1},... | collective-permute-start | bytes 2162696 | tf_op jit(solution)/shard_map/ppermute | solution.py:31
  606.9 47.1 %collective-permute-start.44 = (bf16[256,1408]{1,0:T(8,128)(2,1)S(1)}, bf16[256,1408]{1,0:T(8,128)(2,1)S(1)}, u32[]{:S(2)}, u32[]{:S(2)}) collective-permute-start(bf16[256,1408]{1,0:T(8,128)(2,1)S(1)} %get-tuple-element.73), channel_id=1, source_target_pairs={{0,24},{1,25},{2,26},{3,27},{4,28},{5,29},{6,30},{7,31},{8,16},{9,... | collective-permute-start | bytes 2162696 | tf_op jit(solution)/shard_map/ppermute | solution.py:31
  612.8 62.2 %collective-permute-start.25 = (bf16[4,80,2048]{2,1,0:T(8,128)(2,1)}, bf16[4,80,2048]{2,1,0:T(8,128)(2,1)}, u32[]{:S(2)}, u32[]{:S(2)}) collective-permute-start(bf16[4,80,2048]{2,1,0:T(8,128)(2,1)} %slice.666), channel_id=1, source_target_pairs={{0,2},{1,3},{2,0},{3,1},{4,6},{5,7},{6,4},{7,5},{8,10},{9,11},{10,... | collective-permute-start | bytes 3932168 | tf_op jit(solution)/shard_map/ppermute | solution.py:31
  656.5 31.6 %collective-permute-start.32 = (bf16[2,80,2048]{2,1,0:T(8,128)(2,1)}, bf16[2,80,2048]{2,1,0:T(8,128)(2,1)}, u32[]{:S(2)}, u32[]{:S(2)}) collective-permute-start(bf16[2,80,2048]{2,1,0:T(8,128)(2,1)} %slice.667), channel_id=1, source_target_pairs={{0,8},{1,9},{2,10},{3,11},{4,12},{5,13},{6,14},{7,15},{8,0},{9,1},... | collective-permute-start | bytes 1966088 | tf_op jit(solution)/shard_map/ppermute | solution.py:31
  678.4 23.2 %collective-permute-start.26 = (bf16[2,80,2048]{2,1,0:T(8,128)(2,1)}, bf16[2,80,2048]{2,1,0:T(8,128)(2,1)}, u32[]{:S(2)}, u32[]{:S(2)}) collective-permute-start(bf16[2,80,2048]{2,1,0:T(8,128)(2,1)} %slice.668), channel_id=1, source_target_pairs={{0,8},{1,9},{2,10},{3,11},{4,12},{5,13},{6,14},{7,15},{8,0},{9,1},... | collective-permute-start | bytes 1966088 | tf_op jit(solution)/shard_map/ppermute | solution.py:31
  697.3 8.1 %collective-permute-start.45 = (f32[2,4,256]{2,1,0:T(4,128)S(1)}, f32[2,4,256]{2,1,0:T(4,128)S(1)}, u32[]{:S(2)}, u32[]{:S(2)}) collective-permute-start(f32[2,4,256]{2,1,0:T(4,128)S(1)} %bitcast.272), channel_id=1, source_target_pairs={{0,4},{1,5},{2,6},{3,7},{4,0},{5,1},{6,2},{7,3},{8,12},{9,13},{10,... | collective-permute-start | bytes 24584 | tf_op jit(solution)/shard_map/ppermute | solution.py:31
  707.2 4.5 collective-permute-start.47
  708.2 5.4 collective-permute-start.48
  (95 other events, 1990.8 us)

commit v2 on v1

v2 whole, which is shorter than its diff:
```python
import math

import jax
import jax.numpy as jnp
from jax import lax
from jax.experimental import pallas as pl
from jax.experimental.pallas import tpu as pltpu
from jax.sharding import PartitionSpec as P

D = 2048
HEAD_DIM = 64
FF = 5632
SEQ = 320
STEP = 10
ROT = 16

BETA_ONE = 0.9
BETA_TWO = 0.999
ADAM_EPS = 1e-08
NORM_EPS = 1e-05
MASK_FILL = -1e30

BOTH = ("dp", "tensor")


def swap(values, dp_flip, tensor_flip):
    dp_size, tensor_size = lax.axis_size("dp"), lax.axis_size("tensor")
    pairs = [
        (d * tensor_size + t, (d ^ dp_flip) * tensor_size + (t ^ tensor_flip))
        for d in range(dp_size)
        for t in range(tensor_size)
    ]
    return lax.ppermute(values, BOTH, pairs)


def block_order(count):
    return [2 * j + i for i in range(2) for j in range(count // 2)]


def relative(values, axis, me, count):
    width = values.shape[axis] // count
    return jnp.concatenate(
        [lax.dynamic_slice_in_dim(values, (me ^ r) * width, width, axis) for r in block_order(count)],
        axis=axis,
    )


def from_relative(values, axis, me, count):
    width = values.shape[axis] // count
    places = [((me ^ g) % 2) * (count // 2) + (me ^ g) // 2 for g in range(count)]
    return jnp.concatenate(
        [lax.dynamic_slice_in_dim(values, place * width, width, axis) for place in places],
        axis=axis,
    )


def flip_blocks(values, axis, count):
    width = values.shape[axis] // count
    return jnp.concatenate(
        [lax.slice_in_dim(values, (p ^ 1) * width, ((p ^ 1) + 1) * width, axis=axis) for p in range(count)],
        axis=axis,
    )


def gather_blocks(mine, other):
    half = lax.axis_size("dp") // 2
    near = [mine] + [swap(other if j % 2 else mine, 2 * j, 0) for j in range(1, half)]
    return near + [swap(block, 1, 0) for block in near]


def gather_rows(values):
    other = flip_blocks(swap(values, 2, 0), values.ndim - 1, lax.axis_size("dp"))
    pair = jnp.concatenate([values, other], axis=0)
    four = jnp.concatenate([pair, swap(pair, 0, 2)], axis=0)
    return jnp.concatenate([four, swap(four, 0, 1)], axis=0)


def scatter_rows(partial_of):
    away = swap(partial_of(1).astype(jnp.bfloat16), 0, 1)
    four = partial_of(0) + away.astype(jnp.float32)
    half = four.shape[0] // 2
    pair = four[:half] + swap(four[half:].astype(jnp.bfloat16), 0, 2).astype(jnp.float32)
    half //= 2
    other = swap(pair[half:].astype(jnp.bfloat16), 2, 0).astype(jnp.float32)
    return pair[:half] + flip_blocks(other, 2, lax.axis_size("dp"))


def scatter_blocks(partial_of, axis):
    half = lax.axis_size("dp") // 2
    away = swap(partial_of(1).astype(jnp.bfloat16), 1, 0)
    summed = partial_of(0) + away.astype(jnp.float32)
    pieces = jnp.split(summed, half, axis=axis)
    mine, other = pieces[0], None
    for j in range(1, half):
        came = swap(pieces[j].astype(jnp.bfloat16), 2 * j, 0).astype(jnp.float32)
        if j % 2 == 0:
            mine = mine + came
        else:
            other = came if other is None else other + came
    return mine, other


def dot_plain(a, b):
    return lax.dot_general(a, b, (((1,), (0,)), ((), ())), preferred_element_type=jnp.float32)


def dot_rows(a, b):
    return lax.dot_general(a, b, (((0,), (0,)), ((), ())), preferred_element_type=jnp.float32)


def dot_cols(a, b):
    return lax.dot_general(a, b, (((1,), (1,)), ((), ())), preferred_element_type=jnp.float32)


def turn(values, tables, direction):
    cosine, low_sine, high_sine = tables
    lanes = values.shape[1]
    half_rot = ROT // 2
    moved = pltpu.roll(values, lanes - half_rot, 1) * low_sine + pltpu.roll(values, half_rot, 1) * high_sine
    return values * cosine + direction * moved


def head_probabilities(query, key, bias):
    scores = dot_cols(query, key) * 0.125 + bias
    exponent = jnp.exp(scores - jnp.max(scores, axis=1, keepdims=True))
    return exponent / jnp.sum(exponent, axis=1, keepdims=True)


def attention_fore(projected_ref, tables_ref, bias_ref, turned_ref, attended_ref):
    spots, _, piece, width = projected_ref.shape
    rows, third = spots * piece, width // 3
    tables = [tables_ref[k] for k in range(3)]
    first = lax.broadcasted_iota(jnp.int32, (rows, 128), 1) < HEAD_DIM
    for pair in range(third // 128):
        span = [slice(k * third + pair * 128, k * third + pair * 128 + 128) for k in range(3)]
        query, key, value = [projected_ref[:, 0, :, s].reshape(rows, 128) for s in span]
        query = turn(query, tables, 1.0).astype(jnp.bfloat16)
        key = turn(key, tables, 1.0).astype(jnp.bfloat16)
        value = value.astype(jnp.bfloat16)
        for s, part in zip(span, (query, key, value)):
            turned_ref[:, 0, :, s] = part.reshape(spots, piece, 128)
        none = jnp.zeros_like(query)
        outs = [
            dot_plain(head_probabilities(q, key, bias_ref[...]).astype(jnp.bfloat16), value)
            for q in (jnp.where(first, query, none), jnp.where(first, none, query))
        ]
        attended_ref[:, 0, :, span[0]] = (
            jnp.where(first, outs[0], outs[1]).astype(jnp.bfloat16).reshape(spots, piece, 128)
        )


def attention_back(turned_ref, d_att_ref, tables_ref, bias_ref, d_project_ref):
    spots, _, piece, width = turned_ref.shape
    rows, third = spots * piece, width // 3
    tables = [tables_ref[k] for k in range(3)]
    first = lax.broadcasted_iota(jnp.int32, (rows, 128), 1) < HEAD_DIM
    for pair in range(third // 128):
        span = [slice(k * third + pair * 128, k * third + pair * 128 + 128) for k in range(3)]
        query, key, value = [turned_ref[:, 0, :, s].reshape(rows, 128) for s in span]
        d_att = d_att_ref[:, 0, :, span[0]].reshape(rows, 128)
        none = jnp.zeros_like(query)
        parts = []
        for head in range(2):
            keep = first if head == 0 else jnp.logical_not(first)
            one_query = jnp.where(keep, query, none)
            one_d_att = jnp.where(keep, d_att, none)
            prob = head_probabilities(one_query, key, bias_ref[...])
            d_value = dot_rows(prob.astype(jnp.bfloat16), d_att)
            d_prob = dot_cols(one_d_att, value)
            d_score = (prob * (d_prob - jnp.sum(d_prob * prob, axis=1, keepdims=True))).astype(
                jnp.bfloat16
            )
            parts.append((dot_plain(d_score, key), dot_rows(d_score, query), d_value))
        joined = [jnp.where(first, one, two) for one, two in zip(*parts)]
        done = (turn(0.125 * joined[0], tables, -1.0), turn(0.125 * joined[1], tables, -1.0), joined[2])
        for s, part in zip(span, done):
            d_project_ref[:, 0, :, s] = part.astype(jnp.bfloat16).reshape(spots, piece, 128)


def join_gate_up(packed, whole):
    last = packed[:, 2 * whole :]
    gate = jnp.concatenate([packed[:, :whole], last], axis=1)
    up = jnp.concatenate([packed[:, whole : 2 * whole], pltpu.roll(last, 64, 1)], axis=1)
    return gate, up


def units_fore(normed_ref, weight_ref, packed_ref, hidden_ref):
    packed = dot_plain(normed_ref[...], weight_ref[...])
    packed_ref[...] = packed
    units = hidden_ref.shape[1]
    gate, up = join_gate_up(packed, units - 64)
    hidden_ref[...] = (gate * jax.nn.sigmoid(gate) * up).astype(jnp.bfloat16)[:, :units]


def units_back(cot_ref, weight_ref, packed_ref, d_packed_ref):
    units = weight_ref.shape[0]
    whole = units - 64
    d_hid = dot_cols(cot_ref[...], weight_ref[...]).astype(jnp.bfloat16).astype(jnp.float32)
    d_hid = jnp.concatenate([d_hid, jnp.zeros((d_hid.shape[0], 64), jnp.float32)], axis=1)
    gate, up = join_gate_up(packed_ref[...], whole)
    sigmoid_gate = jax.nn.sigmoid(gate)
    d_gate = d_hid * up * (sigmoid_gate * (1.0 + gate * (1.0 - sigmoid_gate)))
    d_up = d_hid * (gate * sigmoid_gate)
    first = lax.broadcasted_iota(jnp.int32, (gate.shape[0], 128), 1) < 64
    last = jnp.where(first, d_gate[:, whole:], pltpu.roll(d_up[:, whole:], 64, 1))
    d_packed_ref[:, :whole] = d_gate[:, :whole].astype(jnp.bfloat16)
    d_packed_ref[:, whole : 2 * whole] = d_up[:, :whole].astype(jnp.bfloat16)
    d_packed_ref[:, 2 * whole :] = last.astype(jnp.bfloat16)


def whole_block(shape):
    return pl.BlockSpec(shape, lambda *_: (0,) * len(shape))


KERNEL_PARAMS = pltpu.CompilerParams(vmem_limit_bytes=40 * 1024 * 1024)


def run_attention_fore(projected, tables, bias):
    spots, seqs, piece, width = projected.shape
    block = lambda w: pl.BlockSpec((spots, 1, piece, w), lambda s: (0, s, 0, 0))
    rows = spots * piece
    return pl.pallas_call(
        attention_fore,
        grid=(seqs,),
        in_specs=[block(width), whole_block(tables.shape), whole_block(bias.shape)],
        out_specs=[block(width), block(width // 3)],
        out_shape=[
            jax.ShapeDtypeStruct((spots, seqs, piece, width), jnp.bfloat16),
            jax.ShapeDtypeStruct((spots, seqs, piece, width // 3), jnp.bfloat16),
        ],
        compiler_params=KERNEL_PARAMS,
        cost_estimate=pl.CostEstimate(
            flops=seqs * rows * rows * width * 2, bytes_accessed=seqs * rows * width * 7, transcendentals=0
        ),
        name="attention_fore",
    )(projected, tables, bias)


def run_attention_back(turned, d_att, tables, bias):
    spots, seqs, piece, width = turned.shape
    block = lambda w: pl.BlockSpec((spots, 1, piece, w), lambda s: (0, s, 0, 0))
    rows = spots * piece
    return pl.pallas_call(
        attention_back,
        grid=(seqs,),
        in_specs=[block(width), block(width // 3), whole_block(tables.shape), whole_block(bias.shape)],
        out_specs=block(width),
        out_shape=jax.ShapeDtypeStruct((spots, seqs, piece, width), jnp.bfloat16),
        compiler_params=KERNEL_PARAMS,
        cost_estimate=pl.CostEstimate(
            flops=seqs * rows * rows * width * 5, bytes_accessed=seqs * rows * width * 5, transcendentals=0
        ),
        name="attention_back",
    )(turned, d_att, tables, bias)


def row_tile(rows):
    return 256 if rows % 256 == 0 else rows // 8


def run_units_fore(normed, weight):
    rows, units = normed.shape[0], weight.shape[1] // 2
    tile = row_tile(rows)
    block = lambda w: pl.BlockSpec((tile, w), lambda r: (r, 0))
    return pl.pallas_call(
        units_fore,
        grid=(rows // tile,),
        in_specs=[block(D), whole_block(weight.shape)],
        out_specs=[block(2 * units), block(units)],
        out_shape=[
            jax.ShapeDtypeStruct((rows, 2 * units), jnp.float32),
            jax.ShapeDtypeStruct((rows, units), jnp.bfloat16),
        ],
        compiler_params=KERNEL_PARAMS,
        cost_estimate=pl.CostEstimate(
            flops=rows * D * units * 4, bytes_accessed=rows * (D * 2 + units * 10), transcendentals=0
        ),
        name="units_fore",
    )(normed, weight)


def run_units_back(cot, weight, packed):
    rows, units = cot.shape[0], weight.shape[0]
    tile = row_tile(rows)
    block = lambda w: pl.BlockSpec((tile, w), lambda r: (r, 0))
    return pl.pallas_call(
        units_back,
        grid=(rows // tile,),
        in_specs=[block(D), whole_block(weight.shape), block(2 * units)],
        out_specs=block(2 * units),
        out_shape=jax.ShapeDtypeStruct((rows, 2 * units), jnp.bfloat16),
        compiler_params=KERNEL_PARAMS,
        cost_estimate=pl.CostEstimate(
            flops=rows * D * units * 2, bytes_accessed=rows * (D * 2 + units * 12), transcendentals=0
        ),
        name="units_back",
    )(cot, weight, packed)


def adam_update(weight_old, gradient, moment_old, square_old, factor, rate, decay):
    clipped = gradient * factor
    moment_new = BETA_ONE * moment_old + (1.0 - BETA_ONE) * clipped
    square_new = BETA_TWO * square_old + (1.0 - BETA_TWO) * clipped * clipped
    moment_hat = moment_new / (1.0 - BETA_ONE**STEP)
    square_hat = square_new / (1.0 - BETA_TWO**STEP)
    weight_new = weight_old - rate * (
        moment_hat / (jnp.sqrt(square_hat) + ADAM_EPS) + decay * weight_old
    )
    return (weight_new, moment_new, square_new)


def local(
    tokens,
    cotangent,
    project_weight,
    output_weight,
    gate_up_weight,
    down_weight,
    norm_params,
    first_project,
    first_output,
    first_gate_up,
    first_down,
    first_norm,
    second_project,
    second_output,
    second_gate_up,
    second_down,
    second_norm,
):
    count = lax.axis_size("dp")
    blocks_half = count // 2
    me = lax.axis_index("dp")
    side = (me // 2) % 2
    spot = lax.axis_index("tensor")
    spots = lax.axis_size("tensor")
    micro_count, piece = tokens.shape[0], tokens.shape[1]
    head_cols = project_weight.shape[2] // 2
    unit_cols = gate_up_weight.shape[2] // 2
    whole = unit_cols - 64
    rows_each = project_weight.shape[1]
    seqs = 2 * micro_count
    rows_all = spots * seqs * piece

    def halves(first, second):
        first, second = first.astype(jnp.bfloat16), second.astype(jnp.bfloat16)
        return jnp.where(side == 0, first, second), jnp.where(side == 0, second, first)

    def project_half(s):
        return jnp.concatenate(
            [project_weight[k, :, s * head_cols : (s + 1) * head_cols] for k in range(3)], axis=1
        )

    def unit_spans(s):
        return slice(s * whole, (s + 1) * whole), slice(2 * whole + 64 * s, 2 * whole + 64 * (s + 1))

    def gate_up_half(s):
        wide, narrow = unit_spans(s)
        return jnp.concatenate(
            [gate_up_weight[k, :, span] for span in (wide, narrow) for k in range(2)], axis=1
        )

    def output_half(s):
        return output_weight[s * head_cols : (s + 1) * head_cols]

    def down_half(s):
        return jnp.concatenate([down_weight[span] for span in unit_spans(s)], axis=0)

    def gather_half(half_of, axis):
        return jnp.concatenate(gather_blocks(*halves(half_of(0), half_of(1))), axis=axis)

    norm_low = norm_params.astype(jnp.bfloat16)
    norm_full = jnp.concatenate(gather_blocks(norm_low, norm_low), axis=1).astype(jnp.float32)
    gain, shift = norm_full[0], norm_full[1]

    w_project = gather_half(project_half, 0)
    w_gate_up = gather_half(gate_up_half, 0)
    w_down = gather_half(down_half, 1)
    w_output = gather_half(output_half, 1)

    tok_rows = relative(tokens, 2, me, count).astype(jnp.float32)
    row_mean = jnp.mean(tok_rows, axis=2, keepdims=True)
    centered = tok_rows - row_mean
    row_scale = lax.rsqrt(jnp.mean(centered * centered, axis=2, keepdims=True) + NORM_EPS)
    unit_rows = centered * row_scale
    normed = (unit_rows * gain + shift).astype(jnp.bfloat16)
    cot_low = relative(cotangent, 2, me, count)

    all_normed = gather_rows(normed).reshape(rows_all, D)
    all_cot = gather_rows(cot_low).reshape(rows_all, D)

    order = jnp.array([0, 2, 1, 3])
    positions = ((spot ^ order)[:, None] * piece + jnp.arange(piece)[None, :]).reshape(-1)
    half_rot = ROT // 2
    inverse = 10000.0 ** (-2.0 * jnp.arange(half_rot, dtype=jnp.float32) / ROT)
    angles = positions.astype(jnp.float32)[:, None] * inverse[None, :]
    cosine, sine = jnp.cos(angles), jnp.sin(angles)
    none = jnp.zeros_like(sine)
    rest = jnp.zeros((angles.shape[0], HEAD_DIM - ROT), jnp.float32)
    tables = jnp.stack(
        [
            jnp.tile(jnp.concatenate(parts, axis=1), (1, 2))
            for parts in ((cosine, cosine, rest + 1.0), (-sine, none, rest), (none, sine, rest))
        ]
    )
    bias = jnp.where(positions[:, None] >= positions[None, :], 0.0, MASK_FILL)

    projected = dot_plain(all_normed, w_project).reshape(spots, seqs, piece, 3 * head_cols)
    turned, attended = run_attention_fore(projected, tables, bias)
    attended = attended.reshape(rows_all, head_cols)
    packed, hidden = run_units_fore(all_normed, w_gate_up)

    half_d = D // 2

    def side_of(values, i):
        return values[:, i * half_d : (i + 1) * half_d]

    def core_of(values, c):
        return values[c * (rows_all // 2) : (c + 1) * (rows_all // 2)]

    grad_down = scatter_blocks(lambda i: dot_rows(hidden, side_of(all_cot, i)), 1)
    grad_output = scatter_blocks(lambda i: dot_rows(attended, side_of(all_cot, i)), 1)

    d_packed = run_units_back(all_cot, w_down, packed)
    grad_gate_up = scatter_blocks(lambda i: dot_rows(side_of(all_normed, i), d_packed), 0)

    d_att = dot_cols(all_cot, w_output).astype(jnp.bfloat16).reshape(spots, seqs, piece, head_cols)
    d_project = run_attention_back(turned, d_att, tables, bias).reshape(rows_all, 3 * head_cols)
    grad_project = scatter_blocks(lambda i: dot_rows(side_of(all_normed, i), d_project), 0)

    def split_rows(values):
        return values.reshape(-1, piece, D)

    d_normed = scatter_rows(
        lambda c: split_rows(
            dot_cols(core_of(d_project, c), w_project) + dot_cols(core_of(d_packed, c), w_gate_up)
        )
    )
    summed = scatter_rows(
        lambda c: split_rows(
            dot_plain(core_of(attended, c), w_output) + dot_plain(core_of(hidden, c), w_down)
        )
    )
    layer_out = from_relative((tok_rows + summed).astype(jnp.bfloat16), 2, me, count)

    d_unit = d_normed * gain
    d_input = row_scale * (
        d_unit
        - jnp.mean(d_unit, axis=2, keepdims=True)
        - unit_rows * jnp.mean(d_unit * unit_rows, axis=2, keepdims=True)
    )
    input_grad = from_relative((cot_low.astype(jnp.float32) + d_input).astype(jnp.bfloat16), 2, me, count)

    grad_norm = jnp.stack(
        [jnp.sum(d_normed * unit_rows, axis=(0, 1)), jnp.sum(d_normed, axis=(0, 1))]
    )
    grad_norm = grad_norm[:, :half_d] + swap(grad_norm[:, half_d:], 1, 0)
    grad_norm = grad_norm.reshape(2, blocks_half, rows_each)
    norm_grad = grad_norm[:, 0]
    for j in range(1, blocks_half):
        norm_grad = norm_grad + swap(grad_norm[:, j], 2 * j, 0)
    norm_grad = norm_grad + swap(norm_grad, 0, 2)
    norm_grad = norm_grad + swap(norm_grad, 0, 1)

    def in_order(pair):
        mine, other = pair
        return jnp.where(side == 0, mine, other), jnp.where(side == 0, other, mine)

    project_pair = in_order(grad_project)
    gate_up_pair = in_order(grad_gate_up)
    down_pair = in_order(grad_down)
    grads = (
        jnp.stack(
            [
                jnp.concatenate([g[:, k * head_cols : (k + 1) * head_cols] for g in project_pair], axis=1)
                for k in range(3)
            ]
        ),
        jnp.concatenate(in_order(grad_output), axis=0),
        jnp.stack(
            [
                jnp.concatenate(
                    [g[:, k * whole : (k + 1) * whole] for g in gate_up_pair]
                    + [g[:, 2 * whole + 64 * k : 2 * whole + 64 * (k + 1)] for g in gate_up_pair],
                    axis=1,
                )
                for k in range(2)
            ]
        ),
        jnp.concatenate([g[:whole] for g in down_pair] + [g[whole:] for g in down_pair], axis=0),
        norm_grad,
    )
    square_local = sum(jnp.sum(g * g) for g in grads[:4]) + jnp.sum(norm_grad * norm_grad) / spots
    norm_total = jnp.sqrt(lax.psum(square_local, BOTH))
    limit = 0.03 * math.sqrt((4 * D * D + 3 * D * FF + 2 * D) * micro_count * count * SEQ)
    factor = jnp.minimum(1.0, limit / (norm_total + 1e-06))
    rates = (
        2.0 / math.sqrt(D),
        2.0 / math.sqrt(D // 32),
        2.0 / math.sqrt(D),
        2.0 / math.sqrt(FF),
        0.5,
    )
    decays = (0.1, 0.1, 0.1, 0.1, 0.0)
    masters = (project_weight, output_weight, gate_up_weight, down_weight, norm_params)
    firsts = (first_project, first_output, first_gate_up, first_down, first_norm)
    seconds = (second_project, second_output, second_gate_up, second_down, second_norm)
    updated = [
        adam_update(*parts) for parts in zip(masters, grads, firsts, seconds, [factor] * 5, rates, decays)
    ]
    return (
        layer_out,
        input_grad,
        *grads,
        norm_total,
        *[u[0] for u in updated],
        *[u[1] for u in updated],
        *[u[2] for u in updated],
    )


def solution(mesh):
    wide = P("dp", "tensor", None)
    stacked = P(None, "dp", "tensor")
    tall = P("tensor", "dp")
    params = (stacked, tall, stacked, tall, P(None, "dp"))
    return jax.shard_map(
        local,
        mesh=mesh,
        in_specs=(wide, wide, *params, *params, *params),
        out_specs=(wide, wide, *params, P(), *params, *params, *params),
        check_vma=False,
    )
```

time: 788 us -> 730 us (0.926)
  local copies, waits for them, and re-layouts: 168 us -> 49.5 us
  waiting for transfers between devices: 264 us -> 327 us
  starting transfers between devices: 86.9 us -> 132 us
  Pallas kernels: 0 us -> 42.9 us
  matrix products: 112 us -> 70 us
  blocking collectives: 65.3 us -> 37.2 us
  other arithmetic: 74.8 us -> 58.4 us
    slice x35 -> x18, local copies, waits for them, and re-layouts: 83.9 us -> 6.78 us  [the longest x2 4.38 us: scatter_rows(): four[half:].astype(jnp.bfloat16)]
    ppermute x51 -> x69, waiting for transfers between devices: 264 us -> 327 us  [swap(): return lax.ppermute(values, BOTH, pairs)]
    ppermute x51 -> x69, starting transfers between devices: 86.9 us -> 132 us  [swap(): return lax.ppermute(values, BOTH, pairs)]
    pallas_call x0 -> x4, Pallas kernels: none -> 42.9 us  [the longest x1 16 us: run_attention_back(): pl.pallas_call(attention_back, grid=(seqs,), in_specs=[block(width), bloc...]
    all_gather x1 -> x0, blocking collectives: 27.4 us -> none  [local(): lax.all_gather(norm_params.astype(jnp.bfloat16), 'dp', axis=1, tiled=True)]
    another operation x5 -> x6, local copies, waits for them, and re-layouts: 22.2 us -> 1.72 us  [local(): jnp.tile(jnp.concatenate(parts, axis=1), (1, 2))]
    dot_general x5 -> x0, matrix products: 18.7 us -> none  [the longest x1 5.11 us: local(): jnp.einsum('shqk,skhd->sqhd', soft_low, value, preferred_element_type=jnp...]
    reshape x9 -> x0, local copies, waits for them, and re-layouts: 16.7 us -> none  [the longest x3 9.48 us: to_heads(): values.reshape(spots, seqs, piece, heads, HEAD_DIM).transpose(1, 0, 2, 3, 4)]
  transfers between devices with their start and end apart: 51 -> 69, of which waited for: 20 -> 34; matrix products, arithmetic and copies ran while one was open for 27% -> 16% of each run, Pallas kernels for 0% -> 2%
where the time goes in v2:
time: 730 us; the launch traced here: 725 us
  waiting for transfers between devices  327 us (45%)
  starting transfers between devices  132 us (18%)
  matrix products  70 us (10%)
  other arithmetic  58.4 us (8%)
  local copies, waits for them, and re-layouts  49.5 us (7%)
  Pallas kernels  42.9 us (6%)
  blocking collectives  37.2 us (5%)
  between operations  8.28 us (1%)
    ppermute x69, waiting for transfers between devices, swap(): return lax.ppermute(values, BOTH, pairs)  327 us
    ppermute x69, starting transfers between devices, swap(): return lax.ppermute(values, BOTH, pairs)  132 us
    psum x1, blocking collectives, local(): norm_total = jnp.sqrt(lax.psum(square_local, BOTH))  37.2 us
    unnamed x259, local copies, waits for them, and re-layouts  29 us
    dot_general x5, matrix products, dot_cols(): lax.dot_general(a, b, (((1,), (1,)), ((), ())), preferred_element_type=jn...  27.7 us
    dot_general x8, matrix products, dot_rows(): lax.dot_general(a, b, (((0,), (0,)), ((), ())), preferred_element_type=jn...  25.6 us
    dot_general x5, matrix products, dot_plain(): lax.dot_general(a, b, (((1,), (0,)), ((), ())), preferred_element_type=jn...  16.7 us
    sub x5, other arithmetic, adam_update(): weight_old - rate * (moment_hat / (jnp.sqrt(square_hat) + ADAM_EPS) + dec...  16.6 us
  transfers between devices with their start and end apart: 69, of which 34 were waited for; matrix products, arithmetic and copies ran while one was open for 16% of the time, Pallas kernels for 2%

profile of v2, /device:TPU:0, one launch (start us, length us, event | category | flops | bytes accessed | tf_op | source)
XLA Modules:
  0.0 725.0 jit_solution(14324567147513119166)
XLA Ops:
  4.8 3.6 collective-permute-start.2
  85.5 3.6 collective-permute-done.33
  89.2 5.4 collective-permute-start.11
  97.3 24.1 %collective-permute-done.10 = bf16[256,768]{1,0:T(8,128)(2,1)S(1)} collective-permute-done((bf16[256,768]{1,0:T(8,128)(2,1)S(1)}, bf16[256,768]{1,0:T(8,128)(2,1)S(1)}, u32[]{:S(2)}, u32[]{:S(2)}) %collective-permute-start.10) | collective-permute-done | bytes 393248 | tf_op jit(solution)/shard_map/ppermute | solution.py:33
  123.9 30.4 %collective-permute-done.7 = bf16[2,80,2048]{2,1,0:T(8,128)(2,1)S(1)} collective-permute-done((bf16[2,80,2048]{2,1,0:T(8,128)(2,1)S(1)}, bf16[2,80,2048]{2,1,0:T(8,128)(2,1)S(1)}, u32[]{:S(2)}, u32[]{:S(2)}) %collective-permute-start.7) | collective-permute-done | bytes 655392 | tf_op jit(solution)/shard_map/ppermute | solution.py:33
  157.8 28.1 %collective-permute-done.42 = bf16[4,80,2048]{2,1,0:T(8,128)(2,1)S(1)} collective-permute-done((bf16[4,80,2048]{2,1,0:T(8,128)(2,1)S(1)}, bf16[4,80,2048]{2,1,0:T(8,128)(2,1)S(1)}, u32[]{:S(2)}, u32[]{:S(2)}) %collective-permute-start.42) | collective-permute-done | bytes 1310752 | tf_op jit(solution)/shard_map/ppermute | solution.py:33
  188.0 15.4 %collective-permute-done.25 = bf16[256,1408]{1,0:T(8,128)(2,1)S(1)} collective-permute-done((bf16[256,1408]{1,0:T(8,128)(2,1)S(1)}, bf16[256,1408]{1,0:T(8,128)(2,1)S(1)}, u32[]{:S(2)}, u32[]{:S(2)}) %collective-permute-start.25) | collective-permute-done | bytes 720928 | tf_op jit(solution)/shard_map/ppermute | solution.py:33
  205.7 9.0 %collective-permute-done.36 = bf16[704,256]{1,0:T(8,128)(2,1)S(1)} collective-permute-done((bf16[704,256]{1,0:T(8,128)(2,1)S(1)}, bf16[704,256]{1,0:T(8,128)(2,1)S(1)}, u32[]{:S(2)}, u32[]{:S(2)}) %collective-permute-start.36) | collective-permute-done | bytes 360480 | tf_op jit(solution)/shard_map/ppermute | solution.py:33
  217.0 5.4 collective-permute-done.37
  223.2 6.9 collective-permute-done.35
  230.9 7.7 %collective-permute-done.15 = bf16[256,768]{1,0:T(8,128)(2,1)S(1)} collective-permute-done((bf16[256,768]{1,0:T(8,128)(2,1)S(1)}, bf16[256,768]{1,0:T(8,128)(2,1)S(1)}, u32[]{:S(2)}, u32[]{:S(2)}) %collective-permute-start.15) | collective-permute-done | bytes 393248 | tf_op jit(solution)/shard_map/ppermute | solution.py:33
  239.4 7.6 %collective-permute-done.14 = bf16[256,768]{1,0:T(8,128)(2,1)S(1)} collective-permute-done((bf16[256,768]{1,0:T(8,128)(2,1)S(1)}, bf16[256,768]{1,0:T(8,128)(2,1)S(1)}, u32[]{:S(2)}, u32[]{:S(2)}) %collective-permute-start.14) | collective-permute-done | bytes 393248 | tf_op jit(solution)/shard_map/ppermute | solution.py:33
  247.8 7.6 %collective-permute-done.16 = bf16[256,768]{1,0:T(8,128)(2,1)S(1)} collective-permute-done((bf16[256,768]{1,0:T(8,128)(2,1)S(1)}, bf16[256,768]{1,0:T(8,128)(2,1)S(1)}, u32[]{:S(2)}, u32[]{:S(2)}) %collective-permute-start.16) | collective-permute-done | bytes 393248 | tf_op jit(solution)/shard_map/ppermute | solution.py:33
  256.2 14.6 %collective-permute-done.28 = bf16[256,1408]{1,0:T(8,128)(2,1)S(1)} collective-permute-done((bf16[256,1408]{1,0:T(8,128)(2,1)S(1)}, bf16[256,1408]{1,0:T(8,128)(2,1)S(1)}, u32[]{:S(2)}, u32[]{:S(2)}) %collective-permute-start.28) | collective-permute-done | bytes 720928 | tf_op jit(solution)/shard_map/ppermute | solution.py:33
  270.9 15.4 %collective-permute-done.29 = bf16[256,1408]{1,0:T(8,128)(2,1)S(1)} collective-permute-done((bf16[256,1408]{1,0:T(8,128)(2,1)S(1)}, bf16[256,1408]{1,0:T(8,128)(2,1)S(1)}, u32[]{:S(2)}, u32[]{:S(2)}) %collective-permute-start.29) | collective-permute-done | bytes 720928 | tf_op jit(solution)/shard_map/ppermute | solution.py:33
  286.4 14.3 %collective-permute-done.30 = bf16[256,1408]{1,0:T(8,128)(2,1)S(1)} collective-permute-done((bf16[256,1408]{1,0:T(8,128)(2,1)S(1)}, bf16[256,1408]{1,0:T(8,128)(2,1)S(1)}, u32[]{:S(2)}, u32[]{:S(2)}) %collective-permute-start.30) | collective-permute-done | bytes 720928 | tf_op jit(solution)/shard_map/ppermute | solution.py:33
  307.1 10.4 %units_fore.1 = (f32[1280,1408]{1,0:T(8,128)}, bf16[1280,704]{1,0:T(8,128)(2,1)S(1)}) custom-call(bf16[1280,2048]{1,0:T(8,128)(2,1)S(1)} %bitcast.106, bf16[2048,1408]{1,0:T(8,128)(2,1)S(1)} %bitcast.121), custom_call_target="tpu_custom_call" | custom-call | flops 7381975040 | bytes 14254080 | tf_op jit(solution)/shard_map/units_fore/pallas_call | solution.py:265
  318.8 7.8 %units_back.1 = bf16[1280,1408]{1,0:T(8,128)(2,1)S(1)} custom-call(bf16[1280,2048]{1,0:T(8,128)(2,1)S(1)} %bitcast.101, bf16[704,2048]{1,0:T(8,128)(2,1)S(1)} %copy-done.2, f32[1280,1408]{1,0:T(8,128)} %get-tuple-element.30.packed_ref), custom_call_target="tpu_custom_call" | custom-call | flops 3690987520 | bytes 16056320 | tf_op jit(solution)/shard_map/units_back/pallas_call | solution.py:286
  326.6 6.1 convolution_convert_fusion
  332.8 6.0 fusion.17
  338.7 5.9 fusion.19
  347.8 4.5 fusion.59
  352.4 4.3 fusion.projected_ref
  356.7 8.7 %attention_fore.1 = (bf16[4,4,80,768]{3,2,1,0:T(8,128)(2,1)S(1)}, bf16[4,4,80,256]{3,2,1,0:T(8,128)(2,1)S(1)}) custom-call(f32[4,4,80,768]{3,2,1,0:T(8,128)S(1)} %fusion.projected_ref, f32[3,320,128]{2,1,0:T(8,128)S(1)} %copy-done.6, f32[320,320]{1,0:T(8,128)S(1)} %compare_select_fusion.bias_ref), custom_call_target="tpu_custom_call" | custom-call | flops 629145600 | bytes 6881280 | tf_op jit(solution)/shard_map/attention_fore/pallas_call | solution.py:222
  367.1 16.0 %attention_back.1 = bf16[4,4,80,768]{3,2,1,0:T(8,128)(2,1)S(1)} custom-call(bf16[4,4,80,768]{3,2,1,0:T(8,128)(2,1)S(1)} %get-tuple-element.29.turned_ref, bf16[4,4,80,256]{3,2,1,0:T(8,128)(2,1)S(1)} %bitcast.124, f32[3,320,128]{2,1,0:T(8,128)S(1)} %copy-done.6, f32[320,320]{1,0:T(8,128)S(1)} %compare_select_fusion.bias_ref), custom_call_target="tpu_custom_call" | custom-call | flops 1572864000 | bytes 4915200 | tf_op jit(solution)/shard_map/attention_back/pallas_call | solution.py:243
  387.7 6.2 add_convert_fusion
  393.9 7.2 convolution_add_fusion.1
  401.2 3.3 convolution_add_fusion
  407.9 7.6 %collective-permute-start.52 = (bf16[256,256]{1,0:T(8,128)(2,1)S(1)}, bf16[256,256]{1,0:T(8,128)(2,1)S(1)}, u32[]{:S(2)}, u32[]{:S(2)}) collective-permute-start(bf16[256,256]{1,0:T(8,128)(2,1)S(1)} %get-tuple-element.129), channel_id=1, source_target_pairs={{0,16},{1,17},{2,18},{3,19},{4,20},{5,21},{6,22},{7,23},{8,24},{9,... | collective-permute-start | bytes 393224 | tf_op jit(solution)/shard_map/ppermute | solution.py:33
  421.0 4.2 collective-permute-done.52
  428.1 25.9 %collective-permute-done.59 = bf16[704,1024]{1,0:T(8,128)(2,1)} collective-permute-done((bf16[704,1024]{1,0:T(8,128)(2,1)S(1)}, bf16[704,1024]{1,0:T(8,128)(2,1)}, u32[]{:S(2)}, u32[]{:S(2)}) %collective-permute-start.59) | collective-permute-done | bytes 1441824 | tf_op jit(solution)/shard_map/ppermute | solution.py:33
  454.0 3.5 fusion.98
  457.6 7.6 %collective-permute-start.60 = (bf16[704,256]{1,0:T(8,128)(2,1)S(1)}, bf16[704,256]{1,0:T(8,128)(2,1)S(1)}, u32[]{:S(2)}, u32[]{:S(2)}) collective-permute-start(bf16[704,256]{1,0:T(8,128)(2,1)S(1)} %get-tuple-element.85), channel_id=1, source_target_pairs={{0,16},{1,17},{2,18},{3,19},{4,20},{5,21},{6,22},{7,23},{8,24},{9,... | collective-permute-start | bytes 1081352 | tf_op jit(solution)/shard_map/ppermute | solution.py:33
  470.9 17.1 %collective-permute-done.60 = bf16[704,256]{1,0:T(8,128)(2,1)S(1)} collective-permute-done((bf16[704,256]{1,0:T(8,128)(2,1)S(1)}, bf16[704,256]{1,0:T(8,128)(2,1)S(1)}, u32[]{:S(2)}, u32[]{:S(2)}) %collective-permute-start.60) | collective-permute-done | bytes 360480 | tf_op jit(solution)/shard_map/ppermute | solution.py:33
  488.0 3.8 collective-permute-start.50
  491.9 21.3 %collective-permute-start.49 = (bf16[256,768]{1,0:T(8,128)(2,1)S(1)}, bf16[256,768]{1,0:T(8,128)(2,1)S(1)}, u32[]{:S(2)}, u32[]{:S(2)}) collective-permute-start(bf16[256,768]{1,0:T(8,128)(2,1)S(1)} %get-tuple-element.84), channel_id=1, source_target_pairs={{0,8},{1,9},{2,10},{3,11},{4,12},{5,13},{6,14},{7,15},{8,0},{9,1},... | collective-permute-start | bytes 1179656 | tf_op jit(solution)/shard_map/ppermute | solution.py:33
  515.5 5.5 collective-permute-done.48
  521.0 4.3 collective-permute-done.49
  529.3 7.1 convert_add_fusion.1
  541.1 6.3 fusion.97
  558.8 39.5 %collective-permute-done.56 = bf16[256,1408]{1,0:T(8,128)(2,1)S(1)} collective-permute-done((bf16[256,1408]{1,0:T(8,128)(2,1)S(1)}, bf16[256,1408]{1,0:T(8,128)(2,1)S(1)}, u32[]{:S(2)}, u32[]{:S(2)}) %collective-permute-start.56) | collective-permute-done | bytes 720928 | tf_op jit(solution)/shard_map/ppermute | solution.py:33
  605.0 14.8 %collective-permute-start.46 = (bf16[2,80,2048]{2,1,0:T(8,128)(2,1)S(1)}, bf16[2,80,2048]{2,1,0:T(8,128)(2,1)}, u32[]{:S(2)}, u32[]{:S(2)}) collective-permute-start(bf16[2,80,2048]{2,1,0:T(8,128)(2,1)S(1)} %slice.646), channel_id=1, source_target_pairs={{0,8},{1,9},{2,10},{3,11},{4,12},{5,13},{6,14},{7,15},{8,0},{9,1},... | collective-permute-start | bytes 1966088 | tf_op jit(solution)/shard_map/ppermute | solution.py:33
  625.4 10.0 %collective-permute-done.46 = bf16[2,80,2048]{2,1,0:T(8,128)(2,1)} collective-permute-done((bf16[2,80,2048]{2,1,0:T(8,128)(2,1)S(1)}, bf16[2,80,2048]{2,1,0:T(8,128)(2,1)}, u32[]{:S(2)}, u32[]{:S(2)}) %collective-permute-start.46) | collective-permute-done | bytes 655392 | tf_op jit(solution)/shard_map/ppermute | solution.py:33
  639.4 9.3 %collective-permute-done.40 = bf16[2,80,2048]{2,1,0:T(8,128)(2,1)S(1)} collective-permute-done((bf16[2,80,2048]{2,1,0:T(8,128)(2,1)S(1)}, bf16[2,80,2048]{2,1,0:T(8,128)(2,1)S(1)}, u32[]{:S(2)}, u32[]{:S(2)}) %collective-permute-start.40) | collective-permute-done | bytes 655392 | tf_op jit(solution)/shard_map/ppermute | solution.py:33
  652.1 3.4 collective-permute-start.66
  666.6 37.2 %psum.7 = f32[]{:T(128)} all-reduce(f32[]{:T(128)S(6)} %add.450), channel_id=1, replica_groups=mesh['dp'=8,'tensor'=4] {'dp','tensor'}, use_global_device_ids=true, to_apply=%region_11.12 | all-reduce | flops 1 | bytes 8 | tf_op jit(solution)/shard_map/psum | solution.py:494
  708.4 4.7 multiply_subtract_fusion.2
  718.4 5.0 multiply_subtract_fusion
  (493 shorter events, 192.8 us)
Async XLA Ops:
  1.9 46.5 %collective-permute-start.3 = (bf16[2,256]{1,0:T(2,128)(2,1)}, bf16[2,256]{1,0:T(2,128)(2,1)}, u32[]{:S(2)}, u32[]{:S(2)}) collective-permute-start(bf16[2,256]{1,0:T(2,128)(2,1)} %get-tuple-element.68), channel_id=1, source_target_pairs={{0,4},{1,5},{2,6},{3,7},{4,0},{5,1},{6,2},{7,3},{8,12},{9,13},{10,... | collective-permute-start | bytes 3080 | tf_op jit(solution)/shard_map/ppermute | solution.py:33
  4.8 42.4 %collective-permute-start.2 = (bf16[2,256]{1,0:T(2,128)(2,1)}, bf16[2,256]{1,0:T(2,128)(2,1)}, u32[]{:S(2)}, u32[]{:S(2)}) collective-permute-start(bf16[2,256]{1,0:T(2,128)(2,1)} %get-tuple-element.68), channel_id=1, source_target_pairs={{0,24},{1,25},{2,26},{3,27},{4,28},{5,29},{6,30},{7,31},{8,16},{9,... | collective-permute-start | bytes 3080 | tf_op jit(solution)/shard_map/ppermute | solution.py:33
  8.4 36.6 %collective-permute-start.1 = (bf16[2,256]{1,0:T(2,128)(2,1)}, bf16[2,256]{1,0:T(2,128)(2,1)}, u32[]{:S(2)}, u32[]{:S(2)}) collective-permute-start(bf16[2,256]{1,0:T(2,128)(2,1)} %get-tuple-element.68), channel_id=1, source_target_pairs={{0,16},{1,17},{2,18},{3,19},{4,20},{5,21},{6,22},{7,23},{8,24},{9,... | collective-permute-start | bytes 3080 | tf_op jit(solution)/shard_map/ppermute | solution.py:33
  8.4 33.5 %collective-permute-start = (bf16[2,256]{1,0:T(2,128)(2,1)}, bf16[2,256]{1,0:T(2,128)(2,1)}, u32[]{:S(2)}, u32[]{:S(2)}) collective-permute-start(bf16[2,256]{1,0:T(2,128)(2,1)} %get-tuple-element.68), channel_id=1, source_target_pairs={{0,8},{1,9},{2,10},{3,11},{4,12},{5,13},{6,14},{7,15},{8,0},{9,1},... | collective-permute-start | bytes 3080 | tf_op jit(solution)/shard_map/ppermute | solution.py:33
  11.1 58.0 %collective-permute-start.20 = (bf16[256,256]{1,0:T(8,128)(2,1)}, bf16[256,256]{1,0:T(8,128)(2,1)}, u32[]{:S(2)}, u32[]{:S(2)}) collective-permute-start(bf16[256,256]{1,0:T(8,128)(2,1)} %get-tuple-element.62), channel_id=1, source_target_pairs={{0,4},{1,5},{2,6},{3,7},{4,0},{5,1},{6,2},{7,3},{8,12},{9,13},{10,... | collective-permute-start | bytes 393224 | tf_op jit(solution)/shard_map/ppermute | solution.py:33
  42.0 24.1 %collective-permute-start.18 = (bf16[256,256]{1,0:T(8,128)(2,1)}, bf16[256,256]{1,0:T(8,128)(2,1)S(1)}, u32[]{:S(2)}, u32[]{:S(2)}) collective-permute-start(bf16[256,256]{1,0:T(8,128)(2,1)} %get-tuple-element.62), channel_id=1, source_target_pairs={{0,16},{1,17},{2,18},{3,19},{4,20},{5,21},{6,22},{7,23},{8,24},{9,... | collective-permute-start | bytes 393224 | tf_op jit(solution)/shard_map/ppermute | solution.py:33
  45.0 22.8 %collective-permute-start.19 = (bf16[256,256]{1,0:T(8,128)(2,1)S(1)}, bf16[256,256]{1,0:T(8,128)(2,1)S(1)}, u32[]{:S(2)}, u32[]{:S(2)}) collective-permute-start(bf16[256,256]{1,0:T(8,128)(2,1)S(1)} %copy-done.57), channel_id=1, source_target_pairs={{0,24},{1,25},{2,26},{3,27},{4,28},{5,29},{6,30},{7,31},{8,16},{9,... | collective-permute-start | bytes 393224 | tf_op jit(solution)/shard_map/ppermute | solution.py:33
  59.8 34.8 %collective-permute-start.34 = (bf16[704,256]{1,0:T(8,128)(2,1)}, bf16[704,256]{1,0:T(8,128)(2,1)S(1)}, u32[]{:S(2)}, u32[]{:S(2)}) collective-permute-start(bf16[704,256]{1,0:T(8,128)(2,1)} %get-tuple-element.70), channel_id=1, source_target_pairs={{0,4},{1,5},{2,6},{3,7},{4,0},{5,1},{6,2},{7,3},{8,12},{9,13},{10,... | collective-permute-start | bytes 1081352 | tf_op jit(solution)/shard_map/ppermute | solution.py:33
  63.0 22.5 %collective-permute-start.32 = (bf16[704,256]{1,0:T(8,128)(2,1)}, bf16[704,256]{1,0:T(8,128)(2,1)S(1)}, u32[]{:S(2)}, u32[]{:S(2)}) collective-permute-start(bf16[704,256]{1,0:T(8,128)(2,1)} %get-tuple-element.70), channel_id=1, source_target_pairs={{0,16},{1,17},{2,18},{3,19},{4,20},{5,21},{6,22},{7,23},{8,24},{9,... | collective-permute-start | bytes 1081352 | tf_op jit(solution)/shard_map/ppermute | solution.py:33
  79.2 42.3 %collective-permute-start.41 = (bf16[2,80,2048]{2,1,0:T(8,128)(2,1)S(1)}, bf16[2,80,2048]{2,1,0:T(8,128)(2,1)S(1)}, u32[]{:S(2)}, u32[]{:S(2)}) collective-permute-start(bf16[2,80,2048]{2,1,0:T(8,128)(2,1)S(1)} %copy-done.19), channel_id=1, source_target_pairs={{0,8},{1,9},{2,10},{3,11},{4,12},{5,13},{6,14},{7,15},{8,0},{9,1},... | collective-permute-start | bytes 1966088 | tf_op jit(solution)/shard_map/ppermute | solution.py:33
  81.8 39.6 %collective-permute-start.10 = (bf16[256,768]{1,0:T(8,128)(2,1)S(1)}, bf16[256,768]{1,0:T(8,128)(2,1)S(1)}, u32[]{:S(2)}, u32[]{:S(2)}) collective-permute-start(bf16[256,768]{1,0:T(8,128)(2,1)S(1)} %copy-done.50), channel_id=1, source_target_pairs={{0,8},{1,9},{2,10},{3,11},{4,12},{5,13},{6,14},{7,15},{8,0},{9,1},... | collective-permute-start | bytes 1179656 | tf_op jit(solution)/shard_map/ppermute | solution.py:33
  85.5 71.7 %collective-permute-start.13 = (bf16[256,768]{1,0:T(8,128)(2,1)S(1)}, bf16[256,768]{1,0:T(8,128)(2,1)S(1)}, u32[]{:S(2)}, u32[]{:S(2)}) collective-permute-start(bf16[256,768]{1,0:T(8,128)(2,1)S(1)} %copy-done.49), channel_id=1, source_target_pairs={{0,4},{1,5},{2,6},{3,7},{4,0},{5,1},{6,2},{7,3},{8,12},{9,13},{10,... | collective-permute-start | bytes 1179656 | tf_op jit(solution)/shard_map/ppermute | solution.py:33
  89.2 66.9 %collective-permute-start.11 = (bf16[256,768]{1,0:T(8,128)(2,1)S(1)}, bf16[256,768]{1,0:T(8,128)(2,1)S(1)}, u32[]{:S(2)}, u32[]{:S(2)}) collective-permute-start(bf16[256,768]{1,0:T(8,128)(2,1)S(1)} %copy-done.49), channel_id=1, source_target_pairs={{0,16},{1,17},{2,18},{3,19},{4,20},{5,21},{6,22},{7,23},{8,24},{9,... | collective-permute-start | bytes 1179656 | tf_op jit(solution)/shard_map/ppermute | solution.py:33
  94.6 62.1 %collective-permute-start.12 = (bf16[256,768]{1,0:T(8,128)(2,1)S(1)}, bf16[256,768]{1,0:T(8,128)(2,1)S(1)}, u32[]{:S(2)}, u32[]{:S(2)}) collective-permute-start(bf16[256,768]{1,0:T(8,128)(2,1)S(1)} %copy-done.50), channel_id=1, source_target_pairs={{0,24},{1,25},{2,26},{3,27},{4,28},{5,29},{6,30},{7,31},{8,16},{9,... | collective-permute-start | bytes 1179656 | tf_op jit(solution)/shard_map/ppermute | solution.py:33
  121.4 66.3 %collective-permute-start.24 = (bf16[256,1408]{1,0:T(8,128)(2,1)S(1)}, bf16[256,1408]{1,0:T(8,128)(2,1)S(1)}, u32[]{:S(2)}, u32[]{:S(2)}) collective-permute-start(bf16[256,1408]{1,0:T(8,128)(2,1)S(1)} %copy-done.40), channel_id=1, source_target_pairs={{0,8},{1,9},{2,10},{3,11},{4,12},{5,13},{6,14},{7,15},{8,0},{9,1},... | collective-permute-start | bytes 2162696 | tf_op jit(solution)/shard_map/ppermute | solution.py:33
  121.5 32.8 %collective-permute-start.7 = (bf16[2,80,2048]{2,1,0:T(8,128)(2,1)S(1)}, bf16[2,80,2048]{2,1,0:T(8,128)(2,1)S(1)}, u32[]{:S(2)}, u32[]{:S(2)}) collective-permute-start(bf16[2,80,2048]{2,1,0:T(8,128)(2,1)S(1)} %fusion.45), channel_id=1, source_target_pairs={{0,8},{1,9},{2,10},{3,11},{4,12},{5,13},{6,14},{7,15},{8,0},{9,1},... | collective-permute-start | bytes 1966088 | tf_op jit(solution)/shard_map/ppermute | solution.py:33
  154.2 31.7 %collective-permute-start.42 = (bf16[4,80,2048]{2,1,0:T(8,128)(2,1)S(1)}, bf16[4,80,2048]{2,1,0:T(8,128)(2,1)S(1)}, u32[]{:S(2)}, u32[]{:S(2)}) collective-permute-start(bf16[4,80,2048]{2,1,0:T(8,128)(2,1)S(1)} %pad_maximum_fusion.8), channel_id=1, source_target_pairs={{0,2},{1,3},{2,0},{3,1},{4,6},{5,7},{6,4},{7,5},{8,10},{9,11},{10,... | collective-permute-start | bytes 3932168 | tf_op jit(solution)/shard_map/ppermute | solution.py:33
  156.1 59.3 %collective-permute-start.8 = (bf16[4,80,2048]{2,1,0:T(8,128)(2,1)S(1)}, bf16[4,80,2048]{2,1,0:T(8,128)(2,1)S(1)}, u32[]{:S(2)}, u32[]{:S(2)}) collective-permute-start(bf16[4,80,2048]{2,1,0:T(8,128)(2,1)S(1)} %pad_maximum_fusion.7), channel_id=1, source_target_pairs={{0,2},{1,3},{2,0},{3,1},{4,6},{5,7},{6,4},{7,5},{8,10},{9,11},{10,... | collective-permute-start | bytes 3932168 | tf_op jit(solution)/shard_map/ppermute | solution.py:33
  156.7 46.7 %collective-permute-start.25 = (bf16[256,1408]{1,0:T(8,128)(2,1)S(1)}, bf16[256,1408]{1,0:T(8,128)(2,1)S(1)}, u32[]{:S(2)}, u32[]{:S(2)}) collective-permute-start(bf16[256,1408]{1,0:T(8,128)(2,1)S(1)} %copy-done.39), channel_id=1, source_target_pairs={{0,16},{1,17},{2,18},{3,19},{4,20},{5,21},{6,22},{7,23},{8,24},{9,... | collective-permute-start | bytes 2162696 | tf_op jit(solution)/shard_map/ppermute | solution.py:33
  157.2 66.0 %collective-permute-start.27 = (bf16[256,1408]{1,0:T(8,128)(2,1)S(1)}, bf16[256,1408]{1,0:T(8,128)(2,1)S(1)}, u32[]{:S(2)}, u32[]{:S(2)}) collective-permute-start(bf16[256,1408]{1,0:T(8,128)(2,1)S(1)} %copy-done.39), channel_id=1, source_target_pairs={{0,4},{1,5},{2,6},{3,7},{4,0},{5,1},{6,2},{7,3},{8,12},{9,13},{10,... | collective-permute-start | bytes 2162696 | tf_op jit(solution)/shard_map/ppermute | solution.py:33
  186.0 18.3 %collective-permute-start.26 = (bf16[256,1408]{1,0:T(8,128)(2,1)S(1)}, bf16[256,1408]{1,0:T(8,128)(2,1)S(1)}, u32[]{:S(2)}, u32[]{:S(2)}) collective-permute-start(bf16[256,1408]{1,0:T(8,128)(2,1)S(1)} %copy-done.40), channel_id=1, source_target_pairs={{0,24},{1,25},{2,26},{3,27},{4,28},{5,29},{6,30},{7,31},{8,16},{9,... | collective-permute-start | bytes 2162696 | tf_op jit(solution)/shard_map/ppermute | solution.py:33
  187.7 113.1 %collective-permute-start.43 = (bf16[8,80,2048]{2,1,0:T(8,128)(2,1)S(1)}, bf16[8,80,2048]{2,1,0:T(8,128)(2,1)S(1)}, u32[]{:S(2)}, u32[]{:S(2)}) collective-permute-start(bf16[8,80,2048]{2,1,0:T(8,128)(2,1)S(1)} %pad_maximum_fusion.4), channel_id=1, source_target_pairs={{0,1},{1,0},{2,3},{3,2},{4,5},{5,4},{6,7},{7,6},{8,9},{9,8},{10,11... | collective-permute-start | bytes 7864328 | tf_op jit(solution)/shard_map/ppermute | solution.py:33
  215.4 23.1 %collective-permute-start.15 = (bf16[256,768]{1,0:T(8,128)(2,1)S(1)}, bf16[256,768]{1,0:T(8,128)(2,1)S(1)}, u32[]{:S(2)}, u32[]{:S(2)}) collective-permute-start(bf16[256,768]{1,0:T(8,128)(2,1)S(1)} %collective-permute-done.11), channel_id=1, source_target_pairs={{0,4},{1,5},{2,6},{3,7},{4,0},{5,1},{6,2},{7,3},{8,12},{9,13},{10,... | collective-permute-start | bytes 1179656 | tf_op jit(solution)/shard_map/ppermute | solution.py:33
  222.4 24.6 %collective-permute-start.14 = (bf16[256,768]{1,0:T(8,128)(2,1)S(1)}, bf16[256,768]{1,0:T(8,128)(2,1)S(1)}, u32[]{:S(2)}, u32[]{:S(2)}) collective-permute-start(bf16[256,768]{1,0:T(8,128)(2,1)S(1)} %collective-permute-done.10), channel_id=1, source_target_pairs={{0,4},{1,5},{2,6},{3,7},{4,0},{5,1},{6,2},{7,3},{8,12},{9,13},{10,... | collective-permute-start | bytes 1179656 | tf_op jit(solution)/shard_map/ppermute | solution.py:33
  223.1 82.5 %collective-permute-start.9 = (bf16[8,80,2048]{2,1,0:T(8,128)(2,1)S(1)}, bf16[8,80,2048]{2,1,0:T(8,128)(2,1)S(1)}, u32[]{:S(2)}, u32[]{:S(2)}) collective-permute-start(bf16[8,80,2048]{2,1,0:T(8,128)(2,1)S(1)} %pad_maximum_fusion.3), channel_id=1, source_target_pairs={{0,1},{1,0},{2,3},{3,2},{4,5},{5,4},{6,7},{7,6},{8,9},{9,8},{10,11... | collective-permute-start | bytes 7864328 | tf_op jit(solution)/shard_map/ppermute | solution.py:33
  230.1 25.3 %collective-permute-start.16 = (bf16[256,768]{1,0:T(8,128)(2,1)S(1)}, bf16[256,768]{1,0:T(8,128)(2,1)S(1)}, u32[]{:S(2)}, u32[]{:S(2)}) collective-permute-start(bf16[256,768]{1,0:T(8,128)(2,1)S(1)} %collective-permute-done.12), channel_id=1, source_target_pairs={{0,4},{1,5},{2,6},{3,7},{4,0},{5,1},{6,2},{7,3},{8,12},{9,13},{10,... | collective-permute-start | bytes 1179656 | tf_op jit(solution)/shard_map/ppermute | solution.py:33
  238.5 32.3 %collective-permute-start.28 = (bf16[256,1408]{1,0:T(8,128)(2,1)S(1)}, bf16[256,1408]{1,0:T(8,128)(2,1)S(1)}, u32[]{:S(2)}, u32[]{:S(2)}) collective-permute-start(bf16[256,1408]{1,0:T(8,128)(2,1)S(1)} %collective-permute-done.24), channel_id=1, source_target_pairs={{0,4},{1,5},{2,6},{3,7},{4,0},{5,1},{6,2},{7,3},{8,12},{9,13},{10,... | collective-permute-start | bytes 2162696 | tf_op jit(solution)/shard_map/ppermute | solution.py:33
  247.0 39.3 %collective-permute-start.29 = (bf16[256,1408]{1,0:T(8,128)(2,1)S(1)}, bf16[256,1408]{1,0:T(8,128)(2,1)S(1)}, u32[]{:S(2)}, u32[]{:S(2)}) collective-permute-start(bf16[256,1408]{1,0:T(8,128)(2,1)S(1)} %collective-permute-done.25), channel_id=1, source_target_pairs={{0,4},{1,5},{2,6},{3,7},{4,0},{5,1},{6,2},{7,3},{8,12},{9,13},{10,... | collective-permute-start | bytes 2162696 | tf_op jit(solution)/shard_map/ppermute | solution.py:33
  255.4 45.3 %collective-permute-start.30 = (bf16[256,1408]{1,0:T(8,128)(2,1)S(1)}, bf16[256,1408]{1,0:T(8,128)(2,1)S(1)}, u32[]{:S(2)}, u32[]{:S(2)}) collective-permute-start(bf16[256,1408]{1,0:T(8,128)(2,1)S(1)} %collective-permute-done.26), channel_id=1, source_target_pairs={{0,4},{1,5},{2,6},{3,7},{4,0},{5,1},{6,2},{7,3},{8,12},{9,13},{10,... | collective-permute-start | bytes 2162696 | tf_op jit(solution)/shard_map/ppermute | solution.py:33
  366.3 40.7 %collective-permute-start.51 = (bf16[256,1024]{1,0:T(8,128)(2,1)S(1)}, bf16[256,1024]{1,0:T(8,128)(2,1)S(1)}, u32[]{:S(2)}, u32[]{:S(2)}) collective-permute-start(bf16[256,1024]{1,0:T(8,128)(2,1)S(1)} %fusion.54), channel_id=1, source_target_pairs={{0,4},{1,5},{2,6},{3,7},{4,0},{5,1},{6,2},{7,3},{8,12},{9,13},{10,... | collective-permute-start | bytes 1572872 | tf_op jit(solution)/shard_map/ppermute | solution.py:33
  385.6 82.7 %collective-permute-start.47 = (bf16[1024,768]{1,0:T(8,128)(2,1)S(1)}, bf16[1024,768]{1,0:T(8,128)(2,1)S(1)}, u32[]{:S(2)}, u32[]{:S(2)}) collective-permute-start(bf16[1024,768]{1,0:T(8,128)(2,1)S(1)} %fusion.23), channel_id=1, source_target_pairs={{0,4},{1,5},{2,6},{3,7},{4,0},{5,1},{6,2},{7,3},{8,12},{9,13},{10,... | collective-permute-start | bytes 4718600 | tf_op jit(solution)/shard_map/ppermute | solution.py:33
  386.9 67.1 %collective-permute-start.59 = (bf16[704,1024]{1,0:T(8,128)(2,1)S(1)}, bf16[704,1024]{1,0:T(8,128)(2,1)}, u32[]{:S(2)}, u32[]{:S(2)}) collective-permute-start(bf16[704,1024]{1,0:T(8,128)(2,1)S(1)} %copy-done.74), channel_id=1, source_target_pairs={{0,4},{1,5},{2,6},{3,7},{4,0},{5,1},{6,2},{7,3},{8,12},{9,13},{10,... | collective-permute-start | bytes 4325384 | tf_op jit(solution)/shard_map/ppermute | solution.py:33
  425.2 115.8 %collective-permute-start.55 = (bf16[1024,1408]{1,0:T(8,128)(2,1)}, bf16[1024,1408]{1,0:T(8,128)(2,1)}, u32[]{:S(2)}, u32[]{:S(2)}) collective-permute-start(bf16[1024,1408]{1,0:T(8,128)(2,1)} %convolution_convert_fusion), channel_id=1, source_target_pairs={{0,4},{1,5},{2,6},{3,7},{4,0},{5,1},{6,2},{7,3},{8,12},{9,13},{10,... | collective-permute-start | bytes 8650760 | tf_op jit(solution)/shard_map/ppermute | solution.py:33
  426.5 102.7 %collective-permute-start.44 = (bf16[8,80,2048]{2,1,0:T(8,128)(2,1)}, bf16[8,80,2048]{2,1,0:T(8,128)(2,1)}, u32[]{:S(2)}, u32[]{:S(2)}) collective-permute-start(bf16[8,80,2048]{2,1,0:T(8,128)(2,1)} %bitcast.32), channel_id=1, source_target_pairs={{0,1},{1,0},{2,3},{3,2},{4,5},{5,4},{6,7},{7,6},{8,9},{9,8},{10,11... | collective-permute-start | bytes 7864328 | tf_op jit(solution)/shard_map/ppermute | solution.py:33
  457.6 30.4 %collective-permute-start.60 = (bf16[704,256]{1,0:T(8,128)(2,1)S(1)}, bf16[704,256]{1,0:T(8,128)(2,1)S(1)}, u32[]{:S(2)}, u32[]{:S(2)}) collective-permute-start(bf16[704,256]{1,0:T(8,128)(2,1)S(1)} %get-tuple-element.85), channel_id=1, source_target_pairs={{0,16},{1,17},{2,18},{3,19},{4,20},{5,21},{6,22},{7,23},{8,24},{9,... | collective-permute-start | bytes 1081352 | tf_op jit(solution)/shard_map/ppermute | solution.py:33
  465.2 22.8 %collective-permute-start.62 = (bf16[704,256]{1,0:T(8,128)(2,1)S(1)}, bf16[704,256]{1,0:T(8,128)(2,1)S(1)}, u32[]{:S(2)}, u32[]{:S(2)}) collective-permute-start(bf16[704,256]{1,0:T(8,128)(2,1)S(1)} %get-tuple-element.86), channel_id=1, source_target_pairs={{0,24},{1,25},{2,26},{3,27},{4,28},{5,29},{6,30},{7,31},{8,16},{9,... | collective-permute-start | bytes 1081352 | tf_op jit(solution)/shard_map/ppermute | solution.py:33
  468.3 23.6 %collective-permute-start.61 = (bf16[704,256]{1,0:T(8,128)(2,1)S(1)}, bf16[704,256]{1,0:T(8,128)(2,1)S(1)}, u32[]{:S(2)}, u32[]{:S(2)}) collective-permute-start(bf16[704,256]{1,0:T(8,128)(2,1)S(1)} %get-tuple-element.87), channel_id=1, source_target_pairs={{0,8},{1,9},{2,10},{3,11},{4,12},{5,13},{6,14},{7,15},{8,0},{9,1},... | collective-permute-start | bytes 1081352 | tf_op jit(solution)/shard_map/ppermute | solution.py:33
  488.0 33.0 %collective-permute-start.48 = (bf16[256,768]{1,0:T(8,128)(2,1)S(1)}, bf16[256,768]{1,0:T(8,128)(2,1)S(1)}, u32[]{:S(2)}, u32[]{:S(2)}) collective-permute-start(bf16[256,768]{1,0:T(8,128)(2,1)S(1)} %get-tuple-element.82), channel_id=1, source_target_pairs={{0,16},{1,17},{2,18},{3,19},{4,20},{5,21},{6,22},{7,23},{8,24},{9,... | collective-permute-start | bytes 1179656 | tf_op jit(solution)/shard_map/ppermute | solution.py:33
  488.0 33.0 %collective-permute-start.50 = (bf16[256,768]{1,0:T(8,128)(2,1)S(1)}, bf16[256,768]{1,0:T(8,128)(2,1)S(1)}, u32[]{:S(2)}, u32[]{:S(2)}) collective-permute-start(bf16[256,768]{1,0:T(8,128)(2,1)S(1)} %get-tuple-element.83), channel_id=1, source_target_pairs={{0,24},{1,25},{2,26},{3,27},{4,28},{5,29},{6,30},{7,31},{8,16},{9,... | collective-permute-start | bytes 1179656 | tf_op jit(solution)/shard_map/ppermute | solution.py:33
  491.9 33.5 %collective-permute-start.49 = (bf16[256,768]{1,0:T(8,128)(2,1)S(1)}, bf16[256,768]{1,0:T(8,128)(2,1)S(1)}, u32[]{:S(2)}, u32[]{:S(2)}) collective-permute-start(bf16[256,768]{1,0:T(8,128)(2,1)S(1)} %get-tuple-element.84), channel_id=1, source_target_pairs={{0,8},{1,9},{2,10},{3,11},{4,12},{5,13},{6,14},{7,15},{8,0},{9,1},... | collective-permute-start | bytes 1179656 | tf_op jit(solution)/shard_map/ppermute | solution.py:33
  521.0 30.7 %collective-permute-start.38 = (bf16[8,80,2048]{2,1,0:T(8,128)(2,1)}, bf16[8,80,2048]{2,1,0:T(8,128)(2,1)}, u32[]{:S(2)}, u32[]{:S(2)}) collective-permute-start(bf16[8,80,2048]{2,1,0:T(8,128)(2,1)} %bitcast.26), channel_id=1, source_target_pairs={{0,1},{1,0},{2,3},{3,2},{4,5},{5,4},{6,7},{7,6},{8,9},{9,8},{10,11... | collective-permute-start | bytes 7864328 | tf_op jit(solution)/shard_map/ppermute | solution.py:33
  539.5 62.8 %collective-permute-start.45 = (bf16[4,80,2048]{2,1,0:T(8,128)(2,1)}, bf16[4,80,2048]{2,1,0:T(8,128)(2,1)}, u32[]{:S(2)}, u32[]{:S(2)}) collective-permute-start(bf16[4,80,2048]{2,1,0:T(8,128)(2,1)} %slice.644), channel_id=1, source_target_pairs={{0,2},{1,3},{2,0},{3,1},{4,6},{5,7},{6,4},{7,5},{8,10},{9,11},{10,... | collective-permute-start | bytes 3932168 | tf_op jit(solution)/shard_map/ppermute | solution.py:33
  547.5 50.8 %collective-permute-start.56 = (bf16[256,1408]{1,0:T(8,128)(2,1)S(1)}, bf16[256,1408]{1,0:T(8,128)(2,1)S(1)}, u32[]{:S(2)}, u32[]{:S(2)}) collective-permute-start(bf16[256,1408]{1,0:T(8,128)(2,1)S(1)} %get-tuple-element.77), channel_id=1, source_target_pairs={{0,16},{1,17},{2,18},{3,19},{4,20},{5,21},{6,22},{7,23},{8,24},{9,... | collective-permute-start | bytes 2162696 | tf_op jit(solution)/shard_map/ppermute | solution.py:33
  550.3 47.9 %collective-permute-start.58 = (bf16[256,1408]{1,0:T(8,128)(2,1)S(1)}, bf16[256,1408]{1,0:T(8,128)(2,1)S(1)}, u32[]{:S(2)}, u32[]{:S(2)}) collective-permute-start(bf16[256,1408]{1,0:T(8,128)(2,1)S(1)} %get-tuple-element.78), channel_id=1, source_target_pairs={{0,24},{1,25},{2,26},{3,27},{4,28},{5,29},{6,30},{7,31},{8,16},{9,... | collective-permute-start | bytes 2162696 | tf_op jit(solution)/shard_map/ppermute | solution.py:33
  551.3 47.4 %collective-permute-start.57 = (bf16[256,1408]{1,0:T(8,128)(2,1)S(1)}, bf16[256,1408]{1,0:T(8,128)(2,1)S(1)}, u32[]{:S(2)}, u32[]{:S(2)}) collective-permute-start(bf16[256,1408]{1,0:T(8,128)(2,1)S(1)} %get-tuple-element.79), channel_id=1, source_target_pairs={{0,8},{1,9},{2,10},{3,11},{4,12},{5,13},{6,14},{7,15},{8,0},{9,1},... | collective-permute-start | bytes 2162696 | tf_op jit(solution)/shard_map/ppermute | solution.py:33
  558.3 64.2 %collective-permute-start.39 = (bf16[4,80,2048]{2,1,0:T(8,128)(2,1)}, bf16[4,80,2048]{2,1,0:T(8,128)(2,1)}, u32[]{:S(2)}, u32[]{:S(2)}) collective-permute-start(bf16[4,80,2048]{2,1,0:T(8,128)(2,1)} %slice.645), channel_id=1, source_target_pairs={{0,2},{1,3},{2,0},{3,1},{4,6},{5,7},{6,4},{7,5},{8,10},{9,11},{10,... | collective-permute-start | bytes 3932168 | tf_op jit(solution)/shard_map/ppermute | solution.py:33
  605.0 30.4 %collective-permute-start.46 = (bf16[2,80,2048]{2,1,0:T(8,128)(2,1)S(1)}, bf16[2,80,2048]{2,1,0:T(8,128)(2,1)}, u32[]{:S(2)}, u32[]{:S(2)}) collective-permute-start(bf16[2,80,2048]{2,1,0:T(8,128)(2,1)S(1)} %slice.646), channel_id=1, source_target_pairs={{0,8},{1,9},{2,10},{3,11},{4,12},{5,13},{6,14},{7,15},{8,0},{9,1},... | collective-permute-start | bytes 1966088 | tf_op jit(solution)/shard_map/ppermute | solution.py:33
  625.2 23.5 %collective-permute-start.40 = (bf16[2,80,2048]{2,1,0:T(8,128)(2,1)S(1)}, bf16[2,80,2048]{2,1,0:T(8,128)(2,1)S(1)}, u32[]{:S(2)}, u32[]{:S(2)}) collective-permute-start(bf16[2,80,2048]{2,1,0:T(8,128)(2,1)S(1)} %slice.647), channel_id=1, source_target_pairs={{0,8},{1,9},{2,10},{3,11},{4,12},{5,13},{6,14},{7,15},{8,0},{9,1},... | collective-permute-start | bytes 1966088 | tf_op jit(solution)/shard_map/ppermute | solution.py:33
  (108 other events, 1659.6 us)

commit v3 on v2

--- a/solution.py
+++ b/solution.py
@@ -1,3 +1,4 @@
+import functools
 import math
 
 import jax
@@ -21,6 +22,7 @@
 MASK_FILL = -1e30
 
 BOTH = ("dp", "tensor")
+MESH = pl.DeviceIdType.MESH
 
 
 def swap(values, dp_flip, tensor_flip):
@@ -62,42 +64,331 @@
     )
 
 
-def gather_blocks(mine, other):
-    half = lax.axis_size("dp") // 2
-    near = [mine] + [swap(other if j % 2 else mine, 2 * j, 0) for j in range(1, half)]
-    return near + [swap(block, 1, 0) for block in near]
-
-
-def gather_rows(values):
-    other = flip_blocks(swap(values, 2, 0), values.ndim - 1, lax.axis_size("dp"))
-    pair = jnp.concatenate([values, other], axis=0)
-    four = jnp.concatenate([pair, swap(pair, 0, 2)], axis=0)
-    return jnp.concatenate([four, swap(four, 0, 1)], axis=0)
-
-
-def scatter_rows(partial_of):
-    away = swap(partial_of(1).astype(jnp.bfloat16), 0, 1)
-    four = partial_of(0) + away.astype(jnp.float32)
-    half = four.shape[0] // 2
-    pair = four[:half] + swap(four[half:].astype(jnp.bfloat16), 0, 2).astype(jnp.float32)
-    half //= 2
-    other = swap(pair[half:].astype(jnp.bfloat16), 2, 0).astype(jnp.float32)
-    return pair[:half] + flip_blocks(other, 2, lax.axis_size("dp"))
-
-
-def scatter_blocks(partial_of, axis):
-    half = lax.axis_size("dp") // 2
-    away = swap(partial_of(1).astype(jnp.bfloat16), 1, 0)
-    summed = partial_of(0) + away.astype(jnp.float32)
-    pieces = jnp.split(summed, half, axis=axis)
-    mine, other = pieces[0], None
-    for j in range(1, half):
-        came = swap(pieces[j].astype(jnp.bfloat16), 2 * j, 0).astype(jnp.float32)
-        if j % 2 == 0:
-            mine = mine + came
+def gather_small(block):
+    near = [block] + [swap(block, 2 * j, 0) for j in range(1, lax.axis_size("dp") // 2)]
+    near = jnp.concatenate(near, axis=1)
+    return jnp.concatenate([near, swap(near, 1, 0)], axis=1)
+
+
+def place(dp_flip, tensor_flip):
+    return (lax.axis_index("dp") ^ dp_flip, lax.axis_index("tensor") ^ tensor_flip)
+
+
+def greet(places):
+    barrier = pltpu.get_barrier_semaphore()
+    for there in places:
+        pl.semaphore_signal(barrier, inc=1, device_id=there, device_id_type=MESH)
+    pl.semaphore_wait(barrier, len(places))
+
+
+def send_to(there, source, target, send_sem, recv_sem):
+    return pltpu.make_async_remote_copy(
+        src_ref=source,
+        dst_ref=target,
+        send_sem=send_sem,
+        recv_sem=recv_sem,
+        device_id=there,
+        device_id_type=MESH,
+    )
+
+
+def group_places(half):
+    return [place(2 * j, 0) for j in range(1, half)] + [place(1, 0), place(0, 2), place(0, 1)]
+
+
+def gather_all(half, layout, acts, *refs):
+    n = len(layout)
+    mine, other = refs[:n], refs[n : 2 * n]
+    own_rows = refs[2 * n : 2 * n + acts]
+    flipped_rows = refs[2 * n + acts : 2 * n + 2 * acts]
+    outs = refs[2 * n + 2 * acts : 3 * n + 2 * acts]
+    act_out = refs[3 * n + 2 * acts : 3 * n + 3 * acts]
+    z_send, z_recv, x_send, x_recv, a_send, a_recv, own_sem = refs[3 * n + 3 * acts :]
+    greet(group_places(half))
+
+    def block(c, p):
+        axis, width = layout[c]
+        span = pl.ds(p * width, width)
+        return outs[c].at[span] if axis == 0 else outs[c].at[:, span]
+
+    def z_copy(c, j):
+        source = (other if j % 2 else mine)[c]
+        return send_to(place(2 * j, 0), source, block(c, j), z_send.at[c, j], z_recv.at[c, j])
+
+    def x_copy(c, j):
+        source = block(c, j) if j else mine[c]
+        return send_to(place(1, 0), source, block(c, half + j), x_send.at[c, j], x_recv.at[c, j])
+
+    def own_copy(c):
+        return pltpu.make_async_copy(mine[c], block(c, 0), own_sem.at[c])
+
+    def rows(a, index):
+        each = act_out[a].shape[0] // 8
+        return act_out[a].at[pl.ds(index * each, each)]
+
+    def a_copy(a, k):
+        source = (
+            flipped_rows[a],
+            own_rows[a],
+            rows(a, 1),
+            own_rows[a],
+            rows(a, 1),
+            rows(a, 2),
+            rows(a, 3),
+        )[k]
+        there = place(2, 0) if k == 0 else place(0, 2) if k < 3 else place(0, 1)
+        return send_to(there, source, rows(a, k + 1), a_send.at[a, k], a_recv.at[a, k])
+
+    def own_act(a):
+        return pltpu.make_async_copy(own_rows[a], rows(a, 0), own_sem.at[n + a])
+
+    def act_begin(a):
+        for k in (0, 1, 3):
+            a_copy(a, k).start()
+
+    far = range(1, half)
+    for j in far:
+        z_copy(0, j).start()
+    for c in range(min(2, n)):
+        x_copy(c, 0).start()
+    act_begin(0)
+    for a in range(acts):
+        own_act(a).start()
+    for c in range(n):
+        own_copy(c).start()
+    for c in range(n):
+        for j in far:
+            z_copy(c, j).wait_recv()
+            x_copy(c, j).start()
+            if c + 1 < n:
+                z_copy(c + 1, j).start()
+        if c + 2 < n:
+            x_copy(c + 2, 0).start()
+        if c < acts:
+            a_copy(c, 0).wait_recv()
+            a_copy(c, 2).start()
+            a_copy(c, 4).start()
+            a_copy(c, 1).wait_recv()
+            a_copy(c, 5).start()
+            if c + 1 < acts:
+                act_begin(c + 1)
+        if 1 <= c <= acts:
+            a_copy(c - 1, 2).wait_recv()
+            a_copy(c - 1, 6).start()
+    for c in range(n):
+        own_copy(c).wait()
+        for j in range(half):
+            if j:
+                z_copy(c, j).wait_send()
+            x_copy(c, j).wait()
+    for a in range(acts):
+        own_act(a).wait()
+        for k in range(7):
+            a_copy(a, k).wait_send()
+            if k >= 3:
+                a_copy(a, k).wait_recv()
+
+
+def run_gather(half, chunks, acts):
+    layout, shapes = [], []
+    for mine, _, axis in chunks:
+        layout.append((axis, mine.shape[axis]))
+        shape = list(mine.shape)
+        shape[axis] *= 2 * half
+        shapes.append(jax.ShapeDtypeStruct(tuple(shape), mine.dtype))
+    shapes += [jax.ShapeDtypeStruct((a.shape[0] * 8,) + a.shape[1:], a.dtype) for a in acts]
+    n, m = len(chunks), len(acts)
+    ins = [c[0] for c in chunks] + [c[1] for c in chunks] + acts
+    ins += [flip_blocks(a, a.ndim - 1, 2 * half) for a in acts]
+    anywhere = pl.BlockSpec(memory_space=pl.ANY)
+    sem = pltpu.SemaphoreType.DMA
+    return pl.pallas_call(
+        functools.partial(gather_all, half, layout, m),
+        out_shape=shapes,
+        in_specs=[anywhere] * len(ins),
+        out_specs=[anywhere] * len(shapes),
+        scratch_shapes=[sem((n, half))] * 4 + [sem((m, 7))] * 2 + [sem((n + m,))],
+        compiler_params=pltpu.CompilerParams(collective_id=0, has_side_effects=True),
+        name="gather_all",
+    )(*ins)
+
+
+def add_rows(out_ref, *terms):
+    rows = out_ref.shape[0]
+    step = 32 if rows % 32 == 0 else 16
+
+    def body(i, carry):
+        span = pl.ds(pl.multiple_of(i * step, step), step)
+        total = terms[0][span].astype(jnp.float32)
+        for term in terms[1:]:
+            total = total + term[span].astype(jnp.float32)
+        out_ref[span] = total.astype(out_ref.dtype)
+        return carry
+
+    lax.fori_loop(0, rows // step, body, 0)
+
+
+def scatter_all(half, axes, acts, window, *refs):
+    n = len(axes)
+
+    def take(count):
+        nonlocal refs
+        head, refs = refs[:count], refs[count:]
+        return head
+
+    away, near, act_away, act_close = take(n), take(n), take(acts), take(acts)
+    mine, other, act_sum, act_far = take(n), take(n), take(acts), take(acts)
+    x_in, x_own, z_in = take(n), take(n), take(n)
+    a_near, a_core, a_y, a_out = take(acts), take(acts), take(acts), take(acts)
+    x_send, x_recv, z_send, z_recv, own_sem, a_send, a_recv, a_own = refs
+    greet(group_places(half))
+
+    def piece(ref, c, j):
+        width = ref.shape[axes[c]] // half
+        span = pl.ds(j * width, width)
+        return ref.at[span] if axes[c] == 0 else ref.at[:, span]
+
+    def x_copy(c, j):
+        return send_to(place(1, 0), piece(away[c], c, j), x_in[c].at[j], x_send.at[c, j], x_recv.at[c, j])
+
+    def z_copy(c, j):
+        return send_to(place(2 * j, 0), x_in[c].at[j], z_in[c].at[j], z_send.at[c, j], z_recv.at[c, j])
+
+    def own_copy(c, j):
+        return pltpu.make_async_copy(piece(near[c], c, j), x_own[c].at[j], own_sem.at[c, j])
+
+    def a_copy(a, s):
+        source = (act_away[a], a_out[a].at[pl.ds(0, 4)], a_out[a].at[pl.ds(4, 2)])[s]
+        target = (a_core[a], a_y[a], act_far[a])[s]
+        there = (place(0, 1), place(0, 2), place(2, 0))[s]
+        return send_to(there, source, target, a_send.at[a, s], a_recv.at[a, s])
+
+    def a_load(a):
+        return pltpu.make_async_copy(act_close[a], a_near[a], a_own.at[a])
+
+    def a_step(a, s):
+        if s == 0:
+            a_load(a).wait()
+            a_copy(a, 0).wait_recv()
+            for i in range(4):
+                add_rows(a_out[a].at[i], a_near[a].at[4 + i], a_core[a].at[4 + i])
+            a_copy(a, 1).start()
         else:
-            other = came if other is None else other + came
-    return mine, other
+            a_copy(a, 1).wait_recv()
+            for i in range(2):
+                add_rows(a_out[a].at[4 + i], *[part[a].at[2 + i] for part in (a_near, a_core, a_y)])
+            a_copy(a, 2).start()
+            for i in range(2):
+                add_rows(act_sum[a].at[i], *[part[a].at[i] for part in (a_near, a_core, a_y)])
+
+    order = [(c, j) for c in range(n) for j in range(half - 1, -1, -1)]
+    for c, j in order[:window]:
+        x_copy(c, j).start()
+    for a in range(acts):
+        a_copy(a, 0).start()
+        a_load(a).start()
+    for c, j in order:
+        own_copy(c, j).start()
+    steps = [(a, s) for s in range(2) for a in range(acts)]
+    for i, (c, j) in enumerate(order):
+        x_copy(c, j).wait_recv()
+        if i + window < len(order):
+            x_copy(*order[i + window]).start()
+        own_copy(c, j).wait()
+        if j:
+            add_rows(x_in[c].at[j], x_in[c].at[j], x_own[c].at[j])
+            z_copy(c, j).start()
+        else:
+            add_rows(mine[c], x_in[c].at[j], x_own[c].at[j])
+        if steps and i % 2 == 1:
+            a_step(*steps.pop(0))
+    for c in range(n):
+        for j in range(1, half):
+            z_copy(c, j).wait_recv()
+        add_rows(other[c], *[z_in[c].at[j] for j in range(1, half, 2)])
+        add_rows(mine[c], mine[c], *[z_in[c].at[j] for j in range(2, half, 2)])
+    for c in range(n):
+        for j in range(half):
+            x_copy(c, j).wait_send()
+            if j:
+                z_copy(c, j).wait_send()
+    for a in range(acts):
+        for s in range(3):
+            a_copy(a, s).wait_send()
+        a_copy(a, 2).wait_recv()
+
+
+def run_scatter(half, chunks, acts, window=2):
+    n, m = len(chunks), len(acts)
+    axes = [c[2] for c in chunks]
+    pieces = []
+    for away, _, axis in chunks:
+        shape = list(away.shape)
+        shape[axis] //= half
+        pieces.append(tuple(shape))
+    anywhere = pl.BlockSpec(memory_space=pl.ANY)
+    vmem = pl.BlockSpec(memory_space=pltpu.VMEM)
+    ins = [c[k] for k in range(2) for c in chunks] + [a[k] for k in range(2) for a in acts]
+    low = jnp.bfloat16
+
+    def part(a, top, bottom):
+        return (a.shape[0] * top // bottom,) + a.shape[1:]
+
+    shapes = [jax.ShapeDtypeStruct(p, jnp.float32) for p in pieces] * 2
+    shapes += [jax.ShapeDtypeStruct(part(a, 1, 4), kind) for kind in (jnp.float32, low) for a, _ in acts]
+    scratch = [pltpu.VMEM((half,) + p, low) for p in pieces] * 3
+    scratch += [pltpu.VMEM(part(a, *share), low) for share in ((1, 1), (1, 1), (1, 2), (3, 4)) for a, _ in acts]
+    sem = pltpu.SemaphoreType.DMA
+    scratch += [sem((n, half))] * 5 + [sem((m, 3))] * 2 + [sem((m,))]
+    outs = pl.pallas_call(
+        functools.partial(scatter_all, half, axes, m, window),
+        out_shape=shapes,
+        in_specs=[anywhere] * len(ins),
+        out_specs=[vmem] * (2 * n + m) + [anywhere] * m,
+        scratch_shapes=scratch,
+        compiler_params=pltpu.CompilerParams(
+            collective_id=1, has_side_effects=True, vmem_limit_bytes=60 * 1024 * 1024
+        ),
+        name="scatter_all",
+    )(*ins)
+    totals = [
+        outs[2 * n + a] + flip_blocks(outs[2 * n + m + a].astype(jnp.float32), 2, 2 * half) for a in range(m)
+    ]
+    return list(zip(outs[:n], outs[n : 2 * n])), totals
+
+
+def sum_kernel(rounds, in_ref, out_ref, sent, came, send_sem, recv_sem):
+    places = [place(*flips) for flips in rounds]
+    greet(places)
+    out_ref[...] = in_ref[...]
+    for k, there in enumerate(places):
+        sent[k] = out_ref[...]
+        copy = send_to(there, sent.at[k], came.at[k], send_sem.at[k], recv_sem.at[k])
+        copy.start()
+        copy.wait()
+        out_ref[...] = out_ref[...] + came[k]
+
+
+def sum_everywhere(value):
+    rounds = []
+    for axis, size in enumerate((lax.axis_size("dp"), lax.axis_size("tensor"))):
+        flip = 1
+        while flip < size:
+            rounds.append((0, flip) if axis else (flip, 0))
+            flip *= 2
+    vmem = pl.BlockSpec(memory_space=pltpu.VMEM)
+    tile = (8, 128)
+    sem = pltpu.SemaphoreType.DMA
+    total = pl.pallas_call(
+        functools.partial(sum_kernel, rounds),
+        out_shape=jax.ShapeDtypeStruct(tile, jnp.float32),
+        in_specs=[vmem],
+        out_specs=vmem,
+        scratch_shapes=[pltpu.VMEM((len(rounds),) + tile, jnp.float32)] * 2 + [sem((len(rounds),))] * 2,
+        compiler_params=pltpu.CompilerParams(collective_id=2, has_side_effects=True),
+        name="sum_everywhere",
+    )(jnp.full(tile, value))
+    return total[0, 0]
 
 
 def dot_plain(a, b):
@@ -366,17 +657,11 @@
     def down_half(s):
         return jnp.concatenate([down_weight[span] for span in unit_spans(s)], axis=0)
 
-    def gather_half(half_of, axis):
-        return jnp.concatenate(gather_blocks(*halves(half_of(0), half_of(1))), axis=axis)
+    by_columns = rows_each % 128 == 0
 
     norm_low = norm_params.astype(jnp.bfloat16)
-    norm_full = jnp.concatenate(gather_blocks(norm_low, norm_low), axis=1).astype(jnp.float32)
+    norm_full = gather_small(norm_low).astype(jnp.float32)
     gain, shift = norm_full[0], norm_full[1]
-
-    w_project = gather_half(project_half, 0)
-    w_gate_up = gather_half(gate_up_half, 0)
-    w_down = gather_half(down_half, 1)
-    w_output = gather_half(output_half, 1)
 
     tok_rows = relative(tokens, 2, me, count).astype(jnp.float32)
     row_mean = jnp.mean(tok_rows, axis=2, keepdims=True)
@@ -386,8 +671,21 @@
     normed = (unit_rows * gain + shift).astype(jnp.bfloat16)
     cot_low = relative(cotangent, 2, me, count)
 
-    all_normed = gather_rows(normed).reshape(rows_all, D)
-    all_cot = gather_rows(cot_low).reshape(rows_all, D)
+    def chunk(half_of, columns):
+        pair = halves(half_of(0), half_of(1))
+        if columns and not by_columns:
+            return (pair[0].T, pair[1].T, 0)
+        return (*pair, int(columns))
+
+    gathered = run_gather(
+        blocks_half,
+        [chunk(project_half, False), chunk(gate_up_half, False), chunk(down_half, True), chunk(output_half, True)],
+        [normed, cot_low],
+    )
+    w_project, w_gate_up, w_down, w_output = gathered[:4]
+    if not by_columns:
+        w_down, w_output = w_down.T, w_output.T
+    all_normed, all_cot = [rows.reshape(rows_all, D) for rows in gathered[4:]]
 
     order = jnp.array([0, 2, 1, 3])
     positions = ((spot ^ order)[:, None] * piece + jnp.arange(piece)[None, :]).reshape(-1)
@@ -418,29 +716,42 @@
     def core_of(values, c):
         return values[c * (rows_all // 2) : (c + 1) * (rows_all // 2)]
 
-    grad_down = scatter_blocks(lambda i: dot_rows(hidden, side_of(all_cot, i)), 1)
-    grad_output = scatter_blocks(lambda i: dot_rows(attended, side_of(all_cot, i)), 1)
+    def by_side(left_of, right_of, columns=False):
+        def one(i):
+            if columns and not by_columns:
+                return dot_rows(right_of(i), left_of(i)).astype(jnp.bfloat16)
+            return dot_rows(left_of(i), right_of(i)).astype(jnp.bfloat16)
+
+        return (one(1), one(0), int(columns and by_columns))
+
+    def split_rows(values):
+        return values.astype(jnp.bfloat16).reshape(-1, piece, D)
+
+    cot_of = functools.partial(side_of, all_cot)
+    normed_of = functools.partial(side_of, all_normed)
+    down_parts = by_side(lambda i: hidden, cot_of, True)
+    output_parts = by_side(lambda i: attended, cot_of, True)
 
     d_packed = run_units_back(all_cot, w_down, packed)
-    grad_gate_up = scatter_blocks(lambda i: dot_rows(side_of(all_normed, i), d_packed), 0)
+    gate_up_parts = by_side(normed_of, lambda i: d_packed)
 
     d_att = dot_cols(all_cot, w_output).astype(jnp.bfloat16).reshape(spots, seqs, piece, head_cols)
     d_project = run_attention_back(turned, d_att, tables, bias).reshape(rows_all, 3 * head_cols)
-    grad_project = scatter_blocks(lambda i: dot_rows(side_of(all_normed, i), d_project), 0)
-
-    def split_rows(values):
-        return values.reshape(-1, piece, D)
-
-    d_normed = scatter_rows(
-        lambda c: split_rows(
-            dot_cols(core_of(d_project, c), w_project) + dot_cols(core_of(d_packed, c), w_gate_up)
-        )
-    )
-    summed = scatter_rows(
-        lambda c: split_rows(
-            dot_plain(core_of(attended, c), w_output) + dot_plain(core_of(hidden, c), w_down)
-        )
-    )
+    project_parts = by_side(normed_of, lambda i: d_project)
+
+    out_parts = [
+        split_rows(dot_plain(core_of(attended, c), w_output) + dot_plain(core_of(hidden, c), w_down))
+        for c in (1, 0)
+    ]
+    back_parts = [
+        split_rows(dot_cols(core_of(d_project, c), w_project) + dot_cols(core_of(d_packed, c), w_gate_up))
+        for c in (1, 0)
+    ]
+    (grad_down, grad_output, grad_gate_up, grad_project), (d_normed, summed) = run_scatter(
+        blocks_half, [down_parts, output_parts, gate_up_parts, project_parts], [back_parts, out_parts]
+    )
+    if not by_columns:
+        grad_down, grad_output = [tuple(g.T for g in pair) for pair in (grad_down, grad_output)]
     layer_out = from_relative((tok_rows + summed).astype(jnp.bfloat16), 2, me, count)
 
     d_unit = d_normed * gain
@@ -491,7 +802,7 @@
         norm_grad,
     )
     square_local = sum(jnp.sum(g * g) for g in grads[:4]) + jnp.sum(norm_grad * norm_grad) / spots
-    norm_total = jnp.sqrt(lax.psum(square_local, BOTH))
+    norm_total = jnp.sqrt(sum_everywhere(square_local))
     limit = 0.03 * math.sqrt((4 * D * D + 3 * D * FF + 2 * D) * micro_count * count * SEQ)
     factor = jnp.minimum(1.0, limit / (norm_total + 1e-06))
     rates = (

time: 730 us -> 594 us (0.81)
  Pallas kernels: 42.9 us -> 392 us
  waiting for transfers between devices: 327 us -> 1.78 us
  starting transfers between devices: 132 us -> 12.3 us
  blocking collectives: 37.2 us -> 0 us
  other arithmetic: 58.4 us -> 46.5 us
  local copies, waits for them, and re-layouts: 49.5 us -> 57.1 us
    pallas_call x0 -> x3, Pallas kernels: none -> 348 us  [the longest x1 176 us: run_scatter(): pl.pallas_call(functools.partial(scatter_all, half, axes, m, window), out...]
    ppermute x69 -> x10, waiting for transfers between devices: 327 us -> 1.78 us  [swap(): return lax.ppermute(values, BOTH, pairs)]
    ppermute x69 -> x10, starting transfers between devices: 132 us -> 12.3 us  [swap(): return lax.ppermute(values, BOTH, pairs)]
    psum x1 -> x0, blocking collectives: 37.2 us -> none  [local(): norm_total = jnp.sqrt(lax.psum(square_local, BOTH))]
    add x4 -> x0, other arithmetic: 15.1 us -> none  [the longest x2 10 us: scatter_rows(): four = partial_of(0) + away.astype(jnp.float32)]
    unnamed x259 -> x182, local copies, waits for them, and re-layouts: 29 us -> 33.9 us
  transfers between devices with their start and end apart: 69 -> 10, of which waited for: 34 -> 1; matrix products, arithmetic and copies ran while one was open for 16% -> 9% of each run, Pallas kernels for 2% -> 0%
where the time goes in v3:
time: 594 us; the launch traced here: 590 us
  Pallas kernels  392 us (66%)
  matrix products  72.4 us (12%)
  local copies, waits for them, and re-layouts  57.1 us (10%)
  other arithmetic  46.5 us (8%)
  starting transfers between devices  12.3 us (2%)
  between operations  7.41 us (1%)
    pallas_call x1, Pallas kernels, run_scatter(): pl.pallas_call(functools.partial(scatter_all, half, axes, m, window), out...  176 us
    pallas_call x1, Pallas kernels, run_gather(): pl.pallas_call(functools.partial(gather_all, half, layout, m), out_shape=...  157 us
    unnamed x182, local copies, waits for them, and re-layouts  33.9 us
    dot_general x8, matrix products, dot_rows(): lax.dot_general(a, b, (((0,), (0,)), ((), ())), preferred_element_type=jn...  28.1 us
    dot_general x5, matrix products, dot_cols(): lax.dot_general(a, b, (((1,), (1,)), ((), ())), preferred_element_type=jn...  25.9 us
    dot_general x5, matrix products, dot_plain(): lax.dot_general(a, b, (((1,), (0,)), ((), ())), preferred_element_type=jn...  18.3 us
    sub x5, other arithmetic, adam_update(): weight_old - rate * (moment_hat / (jnp.sqrt(square_hat) + ADAM_EPS) + dec...  17.7 us
    pallas_call x1, Pallas kernels, run_attention_back(): pl.pallas_call(attention_back, grid=(seqs,), in_specs=[block(width), bloc...  16.1 us
  transfers between devices with their start and end apart: 10, of which 1 were waited for; matrix products, arithmetic and copies ran while one was open for 9% of the time, Pallas kernels for 0%

profile of v3, /device:TPU:0, one launch (start us, length us, event | category | flops | bytes accessed | tf_op | source)
XLA Modules:
  0.0 589.6 jit_solution(10763979234290896205)
XLA Ops:
  1.9 3.0 collective-permute-start
  4.9 2.6 collective-permute-start.1
  7.5 2.0 convert.61
  16.3 1.7 constant_dynamic-update-slice_fusion.32
  18.0 1.6 constant_dynamic-update-slice_fusion.31
  19.6 1.6 constant_dynamic-update-slice_fusion.30
  21.2 1.6 constant_dynamic-update-slice_fusion.29
  31.1 1.6 concatenate.89
  36.3 2.0 broadcast_select_fusion.10
  40.0 1.8 collective-permute-start.3
  45.4 157.0 %gather_all.1 = (bf16[2048,768]{1,0:T(8,128)(2,1)}, bf16[2048,1408]{1,0:T(8,128)(2,1)}, bf16[704,2048]{1,0:T(8,128)(2,1)}, bf16[256,2048]{1,0:T(8,128)(2,1)}, bf...) custom-call(bf16[256,768]{1,0:T(8,128)(2,1)} %get-tuple-element.132.refs_0_, ...), custom_call_target="tpu_custom_call" | custom-call | tf_op jit(solution)/shard_map/gather_all/pallas_call | solution.py:205
  202.4 2.6 copy-done.2
  205.1 2.5 copy-done.3
  207.6 10.6 %units_fore.1 = (f32[1280,1408]{1,0:T(8,128)}, bf16[1280,704]{1,0:T(8,128)(2,1)S(1)}) custom-call(bf16[1280,2048]{1,0:T(8,128)(2,1)S(1)} %bitcast.113, bf16[2048,1408]{1,0:T(8,128)(2,1)S(1)} %copy-done.2), custom_call_target="tpu_custom_call" | custom-call | flops 7381975040 | bytes 14254080 | tf_op jit(solution)/shard_map/units_fore/pallas_call | solution.py:556
  218.2 3.2 fusion.25.refs_0_
  221.3 3.2 fusion.28.refs_4_
  224.5 4.3 fusion.projected_ref
  228.8 8.9 %attention_fore.1 = (bf16[4,4,80,768]{3,2,1,0:T(8,128)(2,1)S(1)}, bf16[4,4,80,256]{3,2,1,0:T(8,128)(2,1)S(1)}) custom-call(f32[4,4,80,768]{3,2,1,0:T(8,128)S(1)} %fusion.projected_ref, f32[3,320,128]{2,1,0:T(8,128)S(1)} %pad_maximum_fusion.4.tables_ref, f32[320,320]{1,0:T(8,128)S(1)} %compare_select_fusion.bias_ref), custom_call_target="tpu_custom_call" | custom-call | flops 629145600 | bytes 6881280 | tf_op jit(solution)/shard_map/attention_fore/pallas_call | solution.py:513
  237.7 1.7 fusion.49.refs_1_
  239.4 1.7 fusion.52.refs_5_
  241.2 8.2 %units_back.1 = bf16[1280,1408]{1,0:T(8,128)(2,1)S(1)} custom-call(bf16[1280,2048]{1,0:T(8,128)(2,1)S(1)} %bitcast.105, bf16[704,2048]{1,0:T(8,128)(2,1)S(1)} %copy-done.1, f32[1280,1408]{1,0:T(8,128)} %get-tuple-element.52.packed_ref), custom_call_target="tpu_custom_call" | custom-call | flops 3690987520 | bytes 16056320 | tf_op jit(solution)/shard_map/units_back/pallas_call | solution.py:577
  249.4 5.7 convolution_convert_fusion.1.refs_2_
  255.1 5.7 convolution_convert_fusion.refs_6_
  260.8 1.6 convolution_convert_fusion.2
  262.4 16.1 %attention_back.1 = bf16[4,4,80,768]{3,2,1,0:T(8,128)(2,1)S(1)} custom-call(bf16[4,4,80,768]{3,2,1,0:T(8,128)(2,1)S(1)} %get-tuple-element.53.turned_ref, bf16[4,4,80,256]{3,2,1,0:T(8,128)(2,1)S(1)} %bitcast.121, f32[3,320,128]{2,1,0:T(8,128)S(1)} %pad_maximum_fusion.4.tables_ref, f32[320,320]{1,0:T(8,128)S(1)} %compare_select_fusion.bias_ref), custom_call_target="tpu_custom_call" | custom-call | flops 1572864000 | bytes 4915200 | tf_op jit(solution)/shard_map/attention_back/pallas_call | solution.py:534
  278.5 3.5 fusion.19.refs_3_
  282.0 3.5 fusion.22.refs_7_
  285.7 4.5 fusion.57
  290.3 2.2 fusion.55
  292.5 4.5 fusion.83
  297.0 7.5 %add_convert_fusion.3 = bf16[640,2048]{1,0:T(8,128)(2,1)} fusion(f32[640,2048]{1,0:T(8,128)} %fusion.83, bf16[2048,1408]{1,0:T(8,128)(2,1)S(1)} %bitcast.112, bf16[1280,1408]{1,0:T(8,128)(2,1)S(1)} %units_back.1), kind=kOutput, calls=%fused_computation.3 | convolution fusion | flops 3693608960 | bytes 15433728 | tf_op jit(solution)/shard_map/dot_general | solution.py:403
  304.5 4.6 fusion.84
  309.1 7.8 %add_convert_fusion.1 = bf16[640,2048]{1,0:T(8,128)(2,1)} fusion(f32[640,2048]{1,0:T(8,128)} %fusion.84, bf16[2048,1408]{1,0:T(8,128)(2,1)S(1)} %bitcast.112, bf16[1280,1408]{1,0:T(8,128)(2,1)S(1)} %units_back.1), kind=kOutput, calls=%fused_computation.1 | convolution fusion | flops 3693608960 | bytes 15433728 | tf_op jit(solution)/shard_map/dot_general | solution.py:403
  316.9 4.9 add_convert_fusion.2
  321.7 2.4 add_convert_fusion
  324.1 175.7 %scatter_all.1 = (f32[704,256]{1,0:T(8,128)}, f32[256,256]{1,0:T(8,128)}, f32[256,1408]{1,0:T(8,128)}, f32[256,768]{1,0:T(8,128)}, f32[704,256]{1,0:T(8,128)}, /...) custom-call(bf16[704,1024]{1,0:T(8,128)(2,1)} %fusion.25.refs_0_, ...), custom_call_target="tpu_custom_call" | custom-call | tf_op jit(solution)/shard_map/scatter_all/pallas_call | solution.py:343
  499.8 2.0 broadcast_select_fusion
  510.1 1.9 fusion.45
  527.0 3.3 multiply_reduce_fusion
  530.3 2.1 multiply_reduce_fusion.1
  532.5 2.0 multiply_reduce_fusion.2
  537.6 2.9 collective-permute-start.5
  544.0 1.7 collective-permute-done.8
  545.7 1.5 constant_dynamic-update-slice_fusion.45
  551.7 15.7 %sum_everywhere.1 = f32[8,128]{1,0:T(8,128)} custom-call(f32[8,128]{1,0:T(8,128)} %broadcast_in_dim.29.in_ref), custom_call_target="tpu_custom_call" | custom-call | tf_op jit(solution)/shard_map/sum_everywhere/pallas_call | solution.py:382
  569.5 6.1 %multiply_subtract_fusion.1 = (f32[3,256,512]{2,1,0:T(8,128)}, f32[3,256,512]{2,1,0:T(8,128)}, f32[3,256,512]{2,1,0:T(8,128)}) fusion(f32[3,256,512]{2,1,0:T(8,128)} %param.20, f32[3,256,512]{2,1,0:T(8,128)} %get-tuple-element.95, f32[]{:T(128)S(6)} %min.3, f32[3,256,512]{2,1,0:T(8,128)} %param.25, f32[3,256,512]{2,1,0:T(8,128)} %param.30), kind=kLoop, calls=%fused_computation.42 | loop fusion | flops 6291456 | bytes 11010052 | tf_op jit(solution)/shard_map/sub | solution.py:597
  578.0 5.0 multiply_subtract_fusion
  583.1 4.6 multiply_subtract_fusion.2
  (277 shorter events, 60.1 us)
Async XLA Ops:
  1.9 37.4 %collective-permute-start = (bf16[2,256]{1,0:T(2,128)(2,1)}, bf16[2,256]{1,0:T(2,128)(2,1)}, u32[]{:S(2)}, u32[]{:S(2)}) collective-permute-start(bf16[2,256]{1,0:T(2,128)(2,1)} %get-tuple-element.98), channel_id=1, source_target_pairs={{0,8},{1,9},{2,10},{3,11},{4,12},{5,13},{6,14},{7,15},{8,0},{9,1},... | collective-permute-start | bytes 3080 | tf_op jit(solution)/shard_map/ppermute | solution.py:35
  4.9 34.4 %collective-permute-start.1 = (bf16[2,256]{1,0:T(2,128)(2,1)}, bf16[2,256]{1,0:T(2,128)(2,1)}, u32[]{:S(2)}, u32[]{:S(2)}) collective-permute-start(bf16[2,256]{1,0:T(2,128)(2,1)} %get-tuple-element.98), channel_id=1, source_target_pairs={{0,16},{1,17},{2,18},{3,19},{4,20},{5,21},{6,22},{7,23},{8,24},{9,... | collective-permute-start | bytes 3080 | tf_op jit(solution)/shard_map/ppermute | solution.py:35
  7.5 31.8 %collective-permute-start.2 = (bf16[2,256]{1,0:T(2,128)(2,1)}, bf16[2,256]{1,0:T(2,128)(2,1)}, u32[]{:S(2)}, u32[]{:S(2)}) collective-permute-start(bf16[2,256]{1,0:T(2,128)(2,1)} %get-tuple-element.98), channel_id=1, source_target_pairs={{0,24},{1,25},{2,26},{3,27},{4,28},{5,29},{6,30},{7,31},{8,16},{9,... | collective-permute-start | bytes 3080 | tf_op jit(solution)/shard_map/ppermute | solution.py:35
  11.3 3.3 copy-start.37
  15.5 28.4 %copy-start.4 = (bf16[2,80,2048]{2,1,0:T(8,128)(2,1)}, bf16[2,80,2048]{2,1,0:T(8,128)(2,1)S(1)}, u32[]{:S(2)}) copy-start(bf16[2,80,2048]{2,1,0:T(8,128)(2,1)S(1)} %constant_dynamic-update-slice_fusion) | copy-start | bytes 1966084
  16.3 10.1 %copy-start.8 = (f32[3,256,512]{2,1,0:T(8,128)S(1)}, f32[3,256,512]{2,1,0:T(8,128)}, u32[]{:S(2)}) copy-start(f32[3,256,512]{2,1,0:T(8,128)} %param.20) | copy-start | bytes 4718596
  27.5 3.6 copy-start.28
  27.5 3.6 copy-start.29
  35.1 3.2 copy-start.41
  35.1 3.2 copy-start.42
  35.1 3.2 copy-start.43
  35.1 3.2 copy-start.44
  35.1 3.2 copy-start.45
  40.0 3.8 collective-permute-start.3
  207.6 10.6 %copy-start = (bf16[16,80,2048]{2,1,0:T(8,128)(2,1)S(1)}, bf16[16,80,2048]{2,1,0:T(8,128)(2,1)}, u32[]{:S(2)}) copy-start(bf16[16,80,2048]{2,1,0:T(8,128)(2,1)} %get-tuple-element.48) | copy-start | bytes 15728644
  239.4 10.0 %slice-start.2 = ((s8[5242880]{0:T(1024)(128)(4,1)}), s8[4194304]{0:T(1024)(128)(4,1)S(1)}, s32[]{:S(2)}) async-start(s8[5242880]{0:T(1024)(128)(4,1)} %bitcast.115), calls=%async_computation.2 | async-start | bytes 8388608
  241.2 8.2 %slice-start.3 = ((s8[5242880]{0:T(1024)(128)(4,1)}), s8[1048576]{0:T(1024)(128)(4,1)S(1)}, s32[]{:S(2)}) async-start(s8[5242880]{0:T(1024)(128)(4,1)} %bitcast.115), calls=%async_computation.3 | async-start | bytes 2097152
  255.1 5.7 copy-start.13
  290.2 6.8 %slice-start = ((s8[5767168]{0:T(1024)(128)(4,1)}), s8[1572864]{0:T(1024)(128)(4,1)S(1)}, s32[]{:S(2)}) async-start(s8[5767168]{0:T(1024)(128)(4,1)} %bitcast.111), calls=%async_computation | async-start | bytes 3145728
  292.5 4.5 slice-start.1
  297.0 7.5 %copy-start.59 = (bf16[2048,768]{1,0:T(8,128)(2,1)S(1)}, bf16[2048,768]{1,0:T(8,128)(2,1)}, u32[]{:S(2)}) copy-start(bf16[2048,768]{1,0:T(8,128)(2,1)} %get-tuple-element.49) | copy-start | bytes 9437188
  309.1 7.8 %copy-start.14 = (bf16[256,2048]{1,0:T(8,128)(2,1)S(1)}, bf16[256,2048]{1,0:T(8,128)(2,1)}, u32[]{:S(2)}) copy-start(bf16[256,2048]{1,0:T(8,128)(2,1)} %get-tuple-element.54) | copy-start | bytes 3145732
  511.9 7.9 %copy-start.20 = (bf16[2,80,2048]{2,1,0:T(8,128)(2,1)}, bf16[2,80,2048]{2,1,0:T(8,128)(2,1)S(1)}, u32[]{:S(2)}) copy-start(bf16[2,80,2048]{2,1,0:T(8,128)(2,1)S(1)} %get-tuple-element.145) | copy-start | bytes 1966084
  511.9 7.9 %copy-start.21 = (bf16[2,80,2048]{2,1,0:T(8,128)(2,1)}, bf16[2,80,2048]{2,1,0:T(8,128)(2,1)S(1)}, u32[]{:S(2)}) copy-start(bf16[2,80,2048]{2,1,0:T(8,128)(2,1)S(1)} %get-tuple-element.146) | copy-start | bytes 1966084
  512.0 7.8 %copy-start.33 = (f32[256,768]{1,0:T(8,128)S(1)}, f32[256,768]{1,0:T(8,128)}, u32[]{:S(2)}) copy-start(f32[256,768]{1,0:T(8,128)} %get-tuple-element.59) | copy-start | bytes 2359300
  512.0 7.8 %copy-start.34 = (f32[256,768]{1,0:T(8,128)S(1)}, f32[256,768]{1,0:T(8,128)}, u32[]{:S(2)}) copy-start(f32[256,768]{1,0:T(8,128)} %get-tuple-element.60) | copy-start | bytes 2359300
  520.0 16.0 %collective-permute-start.4 = (f32[2,1024]{1,0:T(2,128)S(1)}, f32[2,1024]{1,0:T(2,128)S(1)}, u32[]{:S(2)}, u32[]{:S(2)}) collective-permute-start(f32[2,1024]{1,0:T(2,128)S(1)} %pad_maximum_fusion.9), channel_id=1, source_target_pairs={{0,4},{1,5},{2,6},{3,7},{4,0},{5,1},{6,2},{7,3},{8,12},{9,13},{10,... | collective-permute-start | bytes 24584 | tf_op jit(solution)/shard_map/ppermute | solution.py:35
  526.9 3.3 copy-start.24
  526.9 3.3 copy-start.25
  527.0 3.3 copy-start.26
  530.2 46.8 %copy-start.7 = (f32[2,256,1408]{2,1,0:T(8,128)}, f32[2,256,1408]{2,1,0:T(8,128)S(1)}, u32[]{:S(2)}) copy-start(f32[2,256,1408]{2,1,0:T(8,128)S(1)} %get-tuple-element.91) | copy-start | bytes 8650756
  536.1 6.0 %collective-permute-start.7 = (f32[2,256]{1,0:T(2,128)S(1)}, f32[2,256]{1,0:T(2,128)S(1)}, u32[]{:S(2)}, u32[]{:S(2)}) collective-permute-start(f32[2,256]{1,0:T(2,128)S(1)} %get-tuple-element.168), channel_id=1, source_target_pairs={{0,24},{1,25},{2,26},{3,27},{4,28},{5,29},{6,30},{7,31},{8,16},{9,... | collective-permute-start | bytes 6152 | tf_op jit(solution)/shard_map/ppermute | solution.py:35
  537.6 4.5 collective-permute-start.6
  537.6 4.5 collective-permute-start.5
  542.1 3.6 collective-permute-start.8
  545.7 4.1 collective-permute-start.9
  550.5 37.2 %copy-start.54 = (f32[2,256]{1,0:T(2,128)}, f32[2,256]{1,0:T(2,128)S(1)}, u32[]{:S(2)}) copy-start(f32[2,256]{1,0:T(2,128)S(1)} %get-tuple-element.87) | copy-start | bytes 6148
  569.4 6.2 %copy-start.23 = (f32[512,256]{1,0:T(8,128)S(1)}, f32[512,256]{1,0:T(8,128)}, u32[]{:S(2)}) copy-start(f32[512,256]{1,0:T(8,128)} %param.21) | copy-start | bytes 1572868
  569.4 6.2 %copy-start.27 = (f32[512,256]{1,0:T(8,128)S(1)}, f32[512,256]{1,0:T(8,128)}, u32[]{:S(2)}) copy-start(f32[512,256]{1,0:T(8,128)} %get-tuple-element.93) | copy-start | bytes 1572868
  569.4 6.2 %copy-start.46 = (f32[512,256]{1,0:T(8,128)S(1)}, f32[512,256]{1,0:T(8,128)}, u32[]{:S(2)}) copy-start(f32[512,256]{1,0:T(8,128)} %param.26) | copy-start | bytes 1572868
  569.5 6.2 %copy-start.47 = (f32[512,256]{1,0:T(8,128)S(1)}, f32[512,256]{1,0:T(8,128)}, u32[]{:S(2)}) copy-start(f32[512,256]{1,0:T(8,128)} %param.31) | copy-start | bytes 1572868
  569.5 7.6 %copy-start.15 = (f32[2,256,1408]{2,1,0:T(8,128)S(1)}, f32[2,256,1408]{2,1,0:T(8,128)}, u32[]{:S(2)}) copy-start(f32[2,256,1408]{2,1,0:T(8,128)} %param.27) | copy-start | bytes 8650756
  569.5 7.6 %copy-start.16 = (f32[2,256,1408]{2,1,0:T(8,128)S(1)}, f32[2,256,1408]{2,1,0:T(8,128)}, u32[]{:S(2)}) copy-start(f32[2,256,1408]{2,1,0:T(8,128)} %param.32) | copy-start | bytes 8650756
  578.0 5.0 copy-start.11
  578.0 5.0 copy-start.12
  583.1 4.6 copy-start.53
  583.1 4.6 copy-start.55
  583.1 4.6 copy-start.56
  (27 other events, 52.6 us)

commit v4 on v3

--- a/solution.py
+++ b/solution.py
@@ -213,148 +213,303 @@
     )(*ins)
 
 
-def add_rows(out_ref, *terms):
-    rows = out_ref.shape[0]
-    step = 32 if rows % 32 == 0 else 16
-
-    def body(i, carry):
-        span = pl.ds(pl.multiple_of(i * step, step), step)
-        total = terms[0][span].astype(jnp.float32)
-        for term in terms[1:]:
-            total = total + term[span].astype(jnp.float32)
-        out_ref[span] = total.astype(out_ref.dtype)
-        return carry
-
-    lax.fori_loop(0, rows // step, body, 0)
-
-
-def scatter_all(half, axes, acts, window, *refs):
-    n = len(axes)
-
+def flat(ref):
+    value = ref[...]
+    return value.reshape(-1, value.shape[-1])
+
+
+def put(ref, value):
+    ref[...] = value.astype(ref.dtype).reshape(ref.shape)
+
+
+def blocked(shape, *index):
+    return pl.BlockSpec(shape, lambda g: tuple(i(g) if callable(i) else i for i in index))
+
+
+def step(offset=0):
+    return lambda g: g + offset
+
+
+def backward(half, by_columns, window, *refs):
     def take(count):
         nonlocal refs
         head, refs = refs[:count], refs[count:]
         return head
 
-    away, near, act_away, act_close = take(n), take(n), take(acts), take(acts)
-    mine, other, act_sum, act_far = take(n), take(n), take(acts), take(acts)
-    x_in, x_own, z_in = take(n), take(n), take(n)
-    a_near, a_core, a_y, a_out = take(acts), take(acts), take(acts), take(acts)
-    x_send, x_recv, z_send, z_recv, own_sem, a_send, a_recv, a_own = refs
+    cot, normed, packed, hidden, attended, turned = take(6)
+    w_project, w_gate_up, w_down, w_output, tables, bias = take(6)
+    d_packed, d_att, d_project = take(3)
+    stage, x_in, z_out, z_in, mine = take(4), take(4), take(4), take(4), take(4)
+    act_away, act_near, core_in, y_out, y_in, far_out, act_far, act_sum = [take(2) for _ in range(8)]
+    x_send, x_recv, z_send, z_recv, a_send, a_recv = refs
     greet(group_places(half))
 
-    def piece(ref, c, j):
-        width = ref.shape[axes[c]] // half
-        span = pl.ds(j * width, width)
-        return ref.at[span] if axes[c] == 0 else ref.at[:, span]
-
-    def x_copy(c, j):
-        return send_to(place(1, 0), piece(away[c], c, j), x_in[c].at[j], x_send.at[c, j], x_recv.at[c, j])
+    spots, seqs, piece, _ = cot.shape
+    units, heads = hidden.shape[-1], attended.shape[-1]
+    groups = stage[0].shape[0]
+    per = half // groups
+    wide = D // (2 * groups)
+    every = lambda ref: pl.BlockSpec(ref.shape, lambda g: (0,) * len(ref.shape))
+
+    left = (cot, cot, normed, normed)
+    right = (hidden, attended, d_packed, d_project)
+
+    def product(c, left_ref, right_ref):
+        value = dot_rows(flat(left_ref), flat(right_ref))
+        return value.T if c < 2 and by_columns else value
+
+    def columns_of(side, g=None):
+        first = side * groups + (0 if g is None else g)
+        return blocked((spots, seqs, piece, wide), 0, 0, 0, step(first) if g is None else first)
+
+    def x_copy(c, g):
+        return send_to(place(1, 0), stage[c].at[g], x_in[c].at[g], x_send.at[c, g], x_recv.at[c, g])
 
     def z_copy(c, j):
-        return send_to(place(2 * j, 0), x_in[c].at[j], z_in[c].at[j], z_send.at[c, j], z_recv.at[c, j])
-
-    def own_copy(c, j):
-        return pltpu.make_async_copy(piece(near[c], c, j), x_own[c].at[j], own_sem.at[c, j])
+        source = z_out[c].at[j // per]
+        if per > 1:
+            rows = z_in[c].shape[1]
+            source = source.at[pl.ds((j % per) * rows, rows)]
+        return send_to(place(2 * j, 0), source, z_in[c].at[j], z_send.at[c, j], z_recv.at[c, j])
 
     def a_copy(a, s):
-        source = (act_away[a], a_out[a].at[pl.ds(0, 4)], a_out[a].at[pl.ds(4, 2)])[s]
-        target = (a_core[a], a_y[a], act_far[a])[s]
+        source = (act_away[a], y_out[a], far_out[a])[s]
+        target = (core_in[a], y_in[a], act_far[a])[s]
         there = (place(0, 1), place(0, 2), place(2, 0))[s]
         return send_to(there, source, target, a_send.at[a, s], a_recv.at[a, s])
 
-    def a_load(a):
-        return pltpu.make_async_copy(act_close[a], a_near[a], a_own.at[a])
-
-    def a_step(a, s):
-        if s == 0:
-            a_load(a).wait()
-            a_copy(a, 0).wait_recv()
-            for i in range(4):
-                add_rows(a_out[a].at[i], a_near[a].at[4 + i], a_core[a].at[4 + i])
-            a_copy(a, 1).start()
-        else:
-            a_copy(a, 1).wait_recv()
-            for i in range(2):
-                add_rows(a_out[a].at[4 + i], *[part[a].at[2 + i] for part in (a_near, a_core, a_y)])
-            a_copy(a, 2).start()
-            for i in range(2):
-                add_rows(act_sum[a].at[i], *[part[a].at[i] for part in (a_near, a_core, a_y)])
-
-    order = [(c, j) for c in range(n) for j in range(half - 1, -1, -1)]
-    for c, j in order[:window]:
-        x_copy(c, j).start()
-    for a in range(acts):
-        a_copy(a, 0).start()
-        a_load(a).start()
-    for c, j in order:
-        own_copy(c, j).start()
-    steps = [(a, s) for s in range(2) for a in range(acts)]
-    for i, (c, j) in enumerate(order):
-        x_copy(c, j).wait_recv()
-        if i + window < len(order):
-            x_copy(*order[i + window]).start()
-        own_copy(c, j).wait()
-        if j:
-            add_rows(x_in[c].at[j], x_in[c].at[j], x_own[c].at[j])
-            z_copy(c, j).start()
-        else:
-            add_rows(mine[c], x_in[c].at[j], x_own[c].at[j])
-        if steps and i % 2 == 1:
-            a_step(*steps.pop(0))
-    for c in range(n):
+    order = [(c, g) for c in range(4) for g in range(groups - 1, -1, -1)]
+    started, served = [0], [0]
+
+    def start_x(up_to):
+        while started[0] < min(up_to, len(order)):
+            x_copy(*order[started[0]]).start()
+            started[0] += 1
+
+    def away_products(chunks):
+        def body(*refs):
+            count = len(chunks)
+            for k, c in enumerate(chunks):
+                put(refs[1 + count + k], product(c, refs[0], refs[1 + k]))
+
+        pltpu.emit_pipeline(
+            body,
+            grid=(groups,),
+            in_specs=[columns_of(1)] + [every(right[c]) for c in chunks],
+            out_specs=[blocked((1,) + stage[c].shape[1:], step(), 0, 0) for c in chunks],
+        )(left[chunks[0]], *[right[c] for c in chunks], *[stage[c] for c in chunks])
+
+    def own_product(c, g):
+        out = mine[c] if g == 0 else z_out[c]
+
+        def body(left_ref, right_ref, came_ref, *out_refs):
+            total = product(c, left_ref, right_ref) + came_ref[0].astype(jnp.float32)
+            for out_ref in out_refs:
+                put(out_ref, total)
+
+        outs = ([mine[c]] if g == 0 else []) + ([z_out[c]] if g > 0 or per > 1 else [])
+        one = (1,) + stage[c].shape[1:]
+        pltpu.emit_pipeline(
+            body,
+            grid=(1,),
+            in_specs=[columns_of(0, g), every(right[c]), blocked(one, g, 0, 0)],
+            out_specs=[blocked(one, 0 if out is mine[c] else g, 0, 0) for out in outs],
+        )(left[c], right[c], x_in[c], *outs)
+
+    def serve(count):
+        for _ in range(count):
+            c, g = order[served[0]]
+            x_copy(c, g).wait_recv()
+            served[0] += 1
+            start_x(served[0] + window)
+            own_product(c, g)
+            for j in range(g * per, (g + 1) * per):
+                if j:
+                    z_copy(c, j).start()
+
+    def units_step():
+        tile = (1, seqs, piece)
+
+        def body(cot_ref, down_ref, output_ref, packed_ref, d_packed_ref, d_att_ref):
+            rows = flat(cot_ref)
+            d_packed_ref[...] = units_back(rows, down_ref[...], flat(packed_ref)).reshape(d_packed_ref.shape)
+            put(d_att_ref, dot_cols(rows, output_ref[...]))
+
+        pltpu.emit_pipeline(
+            body,
+            grid=(spots,),
+            in_specs=[
+                blocked(tile + (D,), step(), 0, 0, 0),
+                every(w_down),
+                every(w_output),
+                blocked(tile + (2 * units,), step(), 0, 0, 0),
+            ],
+            out_specs=[
+                blocked(tile + (2 * units,), step(), 0, 0, 0),
+                blocked(tile + (heads,), step(), 0, 0, 0),
+            ],
+        )(cot, w_down, w_output, packed, d_packed, d_att)
+
+    def attention_step(first, count):
+        block = lambda width: blocked((spots, 1, piece, width), 0, step(first), 0, 0)
+        pltpu.emit_pipeline(
+            attention_back,
+            grid=(count,),
+            in_specs=[block(3 * heads), block(heads), every(tables), every(bias)],
+            out_specs=[block(3 * heads)],
+        )(turned, d_att, tables, bias, d_project)
+
+    def rows_of(width, core):
+        return blocked((spots // 2, seqs, piece, width), core, 0, 0, 0)
+
+    def normed_step(core):
+        def body(d_project_ref, d_packed_ref, project_ref, gate_up_ref, out_ref):
+            total = dot_cols(flat(d_project_ref), project_ref[...])
+            put(out_ref, total + dot_cols(flat(d_packed_ref), gate_up_ref[...]))
+
+        pltpu.emit_pipeline(
+            body,
+            grid=(D // 256,),
+            in_specs=[
+                rows_of(3 * heads, core),
+                rows_of(2 * units, core),
+                blocked((256, 3 * heads), step(), 0),
+                blocked((256, 2 * units), step(), 0),
+            ],
+            out_specs=[blocked((spots // 2, seqs, piece, 256), 0, 0, 0, step())],
+        )(d_project, d_packed, w_project, w_gate_up, (act_away if core else act_near)[0])
+
+    def out_step(core):
+        def body(attended_ref, hidden_ref, output_ref, down_ref, out_ref):
+            total = dot_plain(flat(attended_ref), output_ref[...])
+            put(out_ref, total + dot_plain(flat(hidden_ref), down_ref[...]))
+
+        pltpu.emit_pipeline(
+            body,
+            grid=(D // 256,),
+            in_specs=[
+                rows_of(heads, core),
+                rows_of(units, core),
+                blocked((heads, 256), 0, step()),
+                blocked((units, 256), 0, step()),
+            ],
+            out_specs=[blocked((spots // 2, seqs, piece, 256), 0, 0, 0, step())],
+        )(attended, hidden, w_output, w_down, (act_away if core else act_near)[1])
+
+    def add_terms(*refs):
+        *terms, out_ref = refs
+        put(out_ref, sum(flat(term).astype(jnp.float32) for term in terms))
+
+    half_seqs = seqs // 2
+    row = lambda *index: blocked((1, 1, piece, D), *index, 0, 0)
+    line = lambda index: blocked((1, piece, D), index, 0, 0)
+
+    def core_arrived(a):
+        a_copy(a, 0).wait_recv()
+        pltpu.emit_pipeline(
+            add_terms,
+            grid=(seqs,),
+            in_specs=[row(1, step()), row(1, step())],
+            out_specs=[line(step())],
+        )(act_near[a], core_in[a], y_out[a])
+        a_copy(a, 1).start()
+
+    def y_arrived(a):
+        a_copy(a, 1).wait_recv()
+        for first, out in ((half_seqs, far_out[a]), (0, act_sum[a])):
+            pltpu.emit_pipeline(
+                add_terms,
+                grid=(half_seqs,),
+                in_specs=[row(0, step(first)), row(0, step(first)), line(step(first))],
+                out_specs=[line(step())],
+            )(act_near[a], core_in[a], y_in[a], out)
+            if first:
+                a_copy(a, 2).start()
+
+    away_products((0, 1))
+    start_x(window)
+    units_step()
+    away_products((2,))
+    serve(1)
+    attention_step(0, seqs // 2)
+    serve(1)
+    attention_step(seqs // 2, seqs - seqs // 2)
+    away_products((3,))
+    serve(2)
+    normed_step(1)
+    a_copy(0, 0).start()
+    serve(2)
+    normed_step(0)
+    core_arrived(0)
+    serve(2)
+    out_step(1)
+    a_copy(1, 0).start()
+    out_step(0)
+    serve(1)
+    core_arrived(1)
+    y_arrived(0)
+    serve(1)
+    y_arrived(1)
+    serve(len(order) - served[0])
+    for c in range(4):
         for j in range(1, half):
-            z_copy(c, j).wait_recv()
-        add_rows(other[c], *[z_in[c].at[j] for j in range(1, half, 2)])
-        add_rows(mine[c], mine[c], *[z_in[c].at[j] for j in range(2, half, 2)])
-    for c in range(n):
-        for j in range(half):
-            x_copy(c, j).wait_send()
-            if j:
-                z_copy(c, j).wait_send()
-    for a in range(acts):
+            z_copy(c, j).wait()
+        for g in range(groups):
+            x_copy(c, g).wait_send()
+    for a in range(2):
         for s in range(3):
             a_copy(a, s).wait_send()
         a_copy(a, 2).wait_recv()
 
 
-def run_scatter(half, chunks, acts, window=2):
-    n, m = len(chunks), len(acts)
-    axes = [c[2] for c in chunks]
-    pieces = []
-    for away, _, axis in chunks:
-        shape = list(away.shape)
-        shape[axis] //= half
-        pieces.append(tuple(shape))
+def run_backward(half, by_columns, rows, weights, tables, bias, window=3):
+    cot, _, packed, hidden, attended, turned = rows
+    low, full = jnp.bfloat16, jnp.float32
+    spots, seqs, piece, _ = cot.shape
+    each = D // (2 * half)
+    groups = min(half, 4)
+    wide = D // (2 * groups)
+    widths = (hidden.shape[-1], attended.shape[-1], packed.shape[-1], turned.shape[-1])
+    columns = [by_columns and c < 2 for c in range(4)]
+    if by_columns and groups != half:
+        columns = [False] * 4
+
+    def shape_of(count, block, kind):
+        return [
+            jax.ShapeDtypeStruct((count, w, block) if flip else (count, block, w), kind)
+            for w, flip in zip(widths, columns)
+        ]
+
+    def row_shape(*lead, kind=low):
+        return [jax.ShapeDtypeStruct(lead + (piece, D), kind)] * 2
+
+    shapes = [jax.ShapeDtypeStruct(r.shape, low) for r in (packed, attended, turned)]
+    shapes += shape_of(groups, wide, low) * 3 + shape_of(half, each, low) + shape_of(1, wide, full)
+    shapes += row_shape(spots // 2, seqs) * 3 + row_shape(seqs) * 2 + row_shape(seqs // 2) * 2
+    shapes += row_shape(seqs // 2, kind=full)
     anywhere = pl.BlockSpec(memory_space=pl.ANY)
-    vmem = pl.BlockSpec(memory_space=pltpu.VMEM)
-    ins = [c[k] for k in range(2) for c in chunks] + [a[k] for k in range(2) for a in acts]
-    low = jnp.bfloat16
-
-    def part(a, top, bottom):
-        return (a.shape[0] * top // bottom,) + a.shape[1:]
-
-    shapes = [jax.ShapeDtypeStruct(p, jnp.float32) for p in pieces] * 2
-    shapes += [jax.ShapeDtypeStruct(part(a, 1, 4), kind) for kind in (jnp.float32, low) for a, _ in acts]
-    scratch = [pltpu.VMEM((half,) + p, low) for p in pieces] * 3
-    scratch += [pltpu.VMEM(part(a, *share), low) for share in ((1, 1), (1, 1), (1, 2), (3, 4)) for a, _ in acts]
+    ins = [*rows, *weights, tables, bias]
     sem = pltpu.SemaphoreType.DMA
-    scratch += [sem((n, half))] * 5 + [sem((m, 3))] * 2 + [sem((m,))]
     outs = pl.pallas_call(
-        functools.partial(scatter_all, half, axes, m, window),
+        functools.partial(backward, half, columns[0], window),
         out_shape=shapes,
         in_specs=[anywhere] * len(ins),
-        out_specs=[vmem] * (2 * n + m) + [anywhere] * m,
-        scratch_shapes=scratch,
+        out_specs=[anywhere] * len(shapes),
+        scratch_shapes=[sem((4, groups))] * 2 + [sem((4, half))] * 2 + [sem((2, 3))] * 2,
         compiler_params=pltpu.CompilerParams(
-            collective_id=1, has_side_effects=True, vmem_limit_bytes=60 * 1024 * 1024
+            collective_id=1, has_side_effects=True, vmem_limit_bytes=56 * 1024 * 1024
         ),
-        name="scatter_all",
+        name="backward",
     )(*ins)
-    totals = [
-        outs[2 * n + a] + flip_blocks(outs[2 * n + m + a].astype(jnp.float32), 2, 2 * half) for a in range(m)
-    ]
-    return list(zip(outs[:n], outs[n : 2 * n])), totals
+    z_in, own = outs[15:19], outs[19:23]
+    act_far, act_sum = outs[-4:-2], outs[-2:]
+    pairs = []
+    for c in range(4):
+        came = [z_in[c][j].astype(full) for j in range(half)]
+        first = own[c][0] if columns[c] else own[c][0, :each]
+        pairs.append((first + sum(came[2::2]), sum(came[1::2])))
+    totals = [near + flip_blocks(far.astype(full), 2, 2 * half) for near, far in zip(act_sum, act_far)]
+    return pairs, totals
 
 
 def sum_kernel(rounds, in_ref, out_ref, sent, came, send_sem, recv_sem):
@@ -483,20 +638,19 @@
     hidden_ref[...] = (gate * jax.nn.sigmoid(gate) * up).astype(jnp.bfloat16)[:, :units]
 
 
-def units_back(cot_ref, weight_ref, packed_ref, d_packed_ref):
-    units = weight_ref.shape[0]
+def units_back(cot, down, packed):
+    units = down.shape[0]
     whole = units - 64
-    d_hid = dot_cols(cot_ref[...], weight_ref[...]).astype(jnp.bfloat16).astype(jnp.float32)
+    d_hid = dot_cols(cot, down).astype(jnp.bfloat16).astype(jnp.float32)
     d_hid = jnp.concatenate([d_hid, jnp.zeros((d_hid.shape[0], 64), jnp.float32)], axis=1)
-    gate, up = join_gate_up(packed_ref[...], whole)
+    gate, up = join_gate_up(packed, whole)
     sigmoid_gate = jax.nn.sigmoid(gate)
     d_gate = d_hid * up * (sigmoid_gate * (1.0 + gate * (1.0 - sigmoid_gate)))
     d_up = d_hid * (gate * sigmoid_gate)
     first = lax.broadcasted_iota(jnp.int32, (gate.shape[0], 128), 1) < 64
     last = jnp.where(first, d_gate[:, whole:], pltpu.roll(d_up[:, whole:], 64, 1))
-    d_packed_ref[:, :whole] = d_gate[:, :whole].astype(jnp.bfloat16)
-    d_packed_ref[:, whole : 2 * whole] = d_up[:, :whole].astype(jnp.bfloat16)
-    d_packed_ref[:, 2 * whole :] = last.astype(jnp.bfloat16)
+    parts = [d_gate[:, :whole], d_up[:, :whole], last]
+    return jnp.concatenate([part.astype(jnp.bfloat16) for part in parts], axis=1)
 
 
 def whole_block(shape):
@@ -527,24 +681,6 @@
     )(projected, tables, bias)
 
 
-def run_attention_back(turned, d_att, tables, bias):
-    spots, seqs, piece, width = turned.shape
-    block = lambda w: pl.BlockSpec((spots, 1, piece, w), lambda s: (0, s, 0, 0))
-    rows = spots * piece
-    return pl.pallas_call(
-        attention_back,
-        grid=(seqs,),
-        in_specs=[block(width), block(width // 3), whole_block(tables.shape), whole_block(bias.shape)],
-        out_specs=block(width),
-        out_shape=jax.ShapeDtypeStruct((spots, seqs, piece, width), jnp.bfloat16),
-        compiler_params=KERNEL_PARAMS,
-        cost_estimate=pl.CostEstimate(
-            flops=seqs * rows * rows * width * 5, bytes_accessed=seqs * rows * width * 5, transcendentals=0
-        ),
-        name="attention_back",
-    )(turned, d_att, tables, bias)
-
-
 def row_tile(rows):
     return 256 if rows % 256 == 0 else rows // 8
 
@@ -568,24 +704,6 @@
         ),
         name="units_fore",
     )(normed, weight)
-
-
-def run_units_back(cot, weight, packed):
-    rows, units = cot.shape[0], weight.shape[0]
-    tile = row_tile(rows)
-    block = lambda w: pl.BlockSpec((tile, w), lambda r: (r, 0))
-    return pl.pallas_call(
-        units_back,
-        grid=(rows // tile,),
-        in_specs=[block(D), whole_block(weight.shape), block(2 * units)],
-        out_specs=block(2 * units),
-        out_shape=jax.ShapeDtypeStruct((rows, 2 * units), jnp.bfloat16),
-        compiler_params=KERNEL_PARAMS,
-        cost_estimate=pl.CostEstimate(
-            flops=rows * D * units * 2, bytes_accessed=rows * (D * 2 + units * 12), transcendentals=0
-        ),
-        name="units_back",
-    )(cot, weight, packed)
 
 
 def adam_update(weight_old, gradient, moment_old, square_old, factor, rate, decay):
@@ -709,46 +827,10 @@
     packed, hidden = run_units_fore(all_normed, w_gate_up)
 
     half_d = D // 2
-
-    def side_of(values, i):
-        return values[:, i * half_d : (i + 1) * half_d]
-
-    def core_of(values, c):
-        return values[c * (rows_all // 2) : (c + 1) * (rows_all // 2)]
-
-    def by_side(left_of, right_of, columns=False):
-        def one(i):
-            if columns and not by_columns:
-                return dot_rows(right_of(i), left_of(i)).astype(jnp.bfloat16)
-            return dot_rows(left_of(i), right_of(i)).astype(jnp.bfloat16)
-
-        return (one(1), one(0), int(columns and by_columns))
-
-    def split_rows(values):
-        return values.astype(jnp.bfloat16).reshape(-1, piece, D)
-
-    cot_of = functools.partial(side_of, all_cot)
-    normed_of = functools.partial(side_of, all_normed)
-    down_parts = by_side(lambda i: hidden, cot_of, True)
-    output_parts = by_side(lambda i: attended, cot_of, True)
-
-    d_packed = run_units_back(all_cot, w_down, packed)
-    gate_up_parts = by_side(normed_of, lambda i: d_packed)
-
-    d_att = dot_cols(all_cot, w_output).astype(jnp.bfloat16).reshape(spots, seqs, piece, head_cols)
-    d_project = run_attention_back(turned, d_att, tables, bias).reshape(rows_all, 3 * head_cols)
-    project_parts = by_side(normed_of, lambda i: d_project)
-
-    out_parts = [
-        split_rows(dot_plain(core_of(attended, c), w_output) + dot_plain(core_of(hidden, c), w_down))
-        for c in (1, 0)
-    ]
-    back_parts = [
-        split_rows(dot_cols(core_of(d_project, c), w_project) + dot_cols(core_of(d_packed, c), w_gate_up))
-        for c in (1, 0)
-    ]
-    (grad_down, grad_output, grad_gate_up, grad_project), (d_normed, summed) = run_scatter(
-        blocks_half, [down_parts, output_parts, gate_up_parts, project_parts], [back_parts, out_parts]
+    row_shape = (spots, seqs, piece, -1)
+    rows = [values.reshape(row_shape) for values in (all_cot, all_normed, packed, hidden, attended, turned)]
+    (grad_down, grad_output, grad_gate_up, grad_project), (d_normed, summed) = run_backward(
+        blocks_half, by_columns, rows, (w_project, w_gate_up, w_down, w_output), tables, bias
     )
     if not by_columns:
         grad_down, grad_output = [tuple(g.T for g in pair) for pair in (grad_down, grad_output)]

time: 594 us -> 584 us (0.983)
  matrix products: 72.4 us -> 7.31 us
  Pallas kernels: 392 us -> 446 us
    pallas_call x3 -> x1, Pallas kernels: 200 us -> 255 us  [run_backward(): pl.pallas_call(functools.partial(backward, half, columns[0], window), out...]
    dot_general x13 -> x0, matrix products: 54.1 us -> none  [the longest x8 28.1 us: dot_rows(): lax.dot_general(a, b, (((0,), (0,)), ((), ())), preferred_element_type=jn...]
    dot_general x5 -> x1, matrix products: 18.3 us -> 7.31 us  [dot_plain(): lax.dot_general(a, b, (((1,), (0,)), ((), ())), preferred_element_type=jn...]
    unnamed x182 -> x200, local copies, waits for them, and re-layouts: 33.9 us -> 34.5 us
  transfers between devices with their start and end apart: 10 -> 10, of which waited for: 1 -> 3; matrix products, arithmetic and copies ran while one was open for 9% -> 11% of each run, Pallas kernels for 0% -> 0%
where the time goes in v4:
time: 584 us; the launch traced here: 578 us
  Pallas kernels  446 us (76%)
  local copies, waits for them, and re-layouts  60.3 us (10%)
  other arithmetic  42.7 us (7%)
  starting transfers between devices  11.4 us (2%)
  matrix products  7.31 us (1%)
  between operations  7.17 us (1%)
    pallas_call x1, Pallas kernels, run_backward(): pl.pallas_call(functools.partial(backward, half, columns[0], window), out...  255 us
    pallas_call x1, Pallas kernels, run_gather(): pl.pallas_call(functools.partial(gather_all, half, layout, m), out_shape=...  157 us
    unnamed x200, local copies, waits for them, and re-layouts  34.5 us
    sub x5, other arithmetic, adam_update(): weight_old - rate * (moment_hat / (jnp.sqrt(square_hat) + ADAM_EPS) + dec...  16.3 us
    pallas_call x1, Pallas kernels, sum_everywhere(): pl.pallas_call(functools.partial(sum_kernel, rounds), out_shape=jax.Shape...  14.7 us
  transfers between devices with their start and end apart: 10, of which 3 were waited for; matrix products, arithmetic and copies ran while one was open for 11% of the time, Pallas kernels for 0%

profile of v4, /device:TPU:0, one launch (start us, length us, event | category | flops | bytes accessed | tf_op | source)
XLA Modules:
  0.0 577.5 jit_solution(10511237549809176259)
XLA Ops:
  0.7 1.2 constant_dynamic-update-slice_fusion.12
  1.9 5.0 collective-permute-start.2
  8.5 1.6 convert.62
  12.5 1.1 slice_bitcast_fusion.2
  18.3 0.9 constant_dynamic-update-slice_fusion.35
  19.2 0.9 constant_dynamic-update-slice_fusion.34
  21.9 0.9 constant_dynamic-update-slice_fusion.5
  22.8 0.9 constant_dynamic-update-slice_fusion.4
  23.7 0.9 constant_dynamic-update-slice_fusion.3
  24.6 0.9 constant_dynamic-update-slice_fusion.2
  25.5 0.9 constant_dynamic-update-slice_fusion.1
  26.4 0.9 constant_dynamic-update-slice_fusion
  32.0 1.5 concatenate.89
  33.5 1.9 concatenate.88
  35.5 2.4 broadcast_select_fusion
  38.1 1.0 broadcast_select_fusion.4
  39.6 1.0 broadcast_select_fusion.2
  41.3 1.8 collective-permute-start.3
  46.7 156.6 %gather_all.1 = (bf16[2048,768]{1,0:T(8,128)(2,1)}, bf16[2048,1408]{1,0:T(8,128)(2,1)}, bf16[704,2048]{1,0:T(8,128)(2,1)}, bf16[256,2048]{1,0:T(8,128)(2,1)}, bf...) custom-call(bf16[256,768]{1,0:T(8,128)(2,1)} %get-tuple-element.132.refs_0_, ...), custom_call_target="tpu_custom_call" | custom-call | tf_op jit(solution)/shard_map/gather_all/pallas_call | solution.py:205
  203.3 7.3 %fusion.projected_ref = f32[4,4,80,768]{3,2,1,0:T(8,128)S(1)} fusion(bf16[4,4,80,2048]{3,2,1,0:T(8,128)(2,1)} %bitcast.90, bf16[2048,768]{1,0:T(8,128)(2,1)} %get-tuple-element.50.refs_6_), kind=kOutput, calls=%fused_computation.1 | convolution fusion | flops 4026531840 | bytes 12320768 | tf_op jit(solution)/shard_map/dot_general | solution.py:550
  210.6 10.5 %units_fore.1 = (f32[1280,1408]{1,0:T(8,128)}, bf16[1280,704]{1,0:T(8,128)(2,1)S(1)}) custom-call(bf16[1280,2048]{1,0:T(8,128)(2,1)S(1)} %bitcast.92, bf16[2048,1408]{1,0:T(8,128)(2,1)S(1)} %copy-done), custom_call_target="tpu_custom_call" | custom-call | flops 7381975040 | bytes 14254080 | tf_op jit(solution)/shard_map/units_fore/pallas_call | solution.py:692
  221.1 8.7 %attention_fore.1 = (bf16[4,4,80,768]{3,2,1,0:T(8,128)(2,1)S(1)}, bf16[4,4,80,256]{3,2,1,0:T(8,128)(2,1)S(1)}) custom-call(f32[4,4,80,768]{3,2,1,0:T(8,128)S(1)} %fusion.projected_ref, f32[3,320,128]{2,1,0:T(8,128)S(1)} %pad_maximum_fusion.4.tables_ref.refs_10_, f32[320,320]{1,0:T(8,128)S(1)} %compare_select_fusion.bias_ref.refs_11_), custom_call_target="tpu_custom_call" | custom-call | flops 629145600 | bytes 6881280 | tf_op jit(solution)/shard_map/attention_fore/pallas_call | solution.py:667
  229.9 1.3 copy-done.5
  232.0 255.5 %backward.1 = (bf16[4,4,80,1408]{3,2,1,0:T(8,128)(2,1)}, bf16[4,4,80,256]{3,2,1,0:T(8,128)(2,1)}, bf16[4,4,80,768]{3,2,1,0:T(8,128)(2,1)}, bf16[4,704,256]{2,1,0...) custom-call(bf16[4,4,80,2048]{3,2,1,0:T(8,128)(2,1)} %bitcast.97, ...), custom_call_target="tpu_custom_call" | custom-call | tf_op jit(solution)/shard_map/backward/pallas_call | solution.py:493
  487.4 1.7 fusion.22
  494.2 1.0 copy-done.45
  495.8 1.1 copy-done.34
  510.0 1.5 multiply_reduce_fusion.4
  511.4 1.3 concatenate.108
  512.7 1.5 concatenate.109
  514.3 3.2 multiply_reduce_fusion
  517.7 1.0 copy-done.37
  518.7 2.1 multiply_reduce_fusion.1
  520.9 2.0 multiply_reduce_fusion.2
  522.9 1.5 constant_dynamic-update-slice_fusion.46
  525.2 1.7 collective-permute-start.7
  526.9 1.8 collective-permute-start.6
  528.7 1.5 constant_dynamic-update-slice_fusion.38
  531.9 1.5 constant_dynamic-update-slice_fusion.45
  533.4 1.6 collective-permute-done.8
  535.0 1.5 constant_dynamic-update-slice_fusion.37
  541.0 14.7 %sum_everywhere.1 = f32[8,128]{1,0:T(8,128)} custom-call(f32[8,128]{1,0:T(8,128)} %broadcast_in_dim.29.in_ref), custom_call_target="tpu_custom_call" | custom-call | tf_op jit(solution)/shard_map/sum_everywhere/pallas_call | solution.py:537
  555.6 1.2 slice.367
  558.2 2.9 multiply_subtract_fusion.3
  561.1 4.7 multiply_subtract_fusion.2
  565.9 3.1 multiply_subtract_fusion.1
  569.0 1.3 copy-done.18
  571.1 5.0 multiply_subtract_fusion
  (272 shorter events, 44.5 us)
Async XLA Ops:
  1.9 38.7 %collective-permute-start.2 = (bf16[2,256]{1,0:T(2,128)(2,1)}, bf16[2,256]{1,0:T(2,128)(2,1)}, u32[]{:S(2)}, u32[]{:S(2)}) collective-permute-start(bf16[2,256]{1,0:T(2,128)(2,1)} %get-tuple-element.98), channel_id=1, source_target_pairs={{0,24},{1,25},{2,26},{3,27},{4,28},{5,29},{6,30},{7,31},{8,16},{9,... | collective-permute-start | bytes 3080 | tf_op jit(solution)/shard_map/ppermute | solution.py:35
  7.0 33.6 %collective-permute-start.1 = (bf16[2,256]{1,0:T(2,128)(2,1)}, bf16[2,256]{1,0:T(2,128)(2,1)}, u32[]{:S(2)}, u32[]{:S(2)}) collective-permute-start(bf16[2,256]{1,0:T(2,128)(2,1)} %get-tuple-element.98), channel_id=1, source_target_pairs={{0,16},{1,17},{2,18},{3,19},{4,20},{5,21},{6,22},{7,23},{8,24},{9,... | collective-permute-start | bytes 3080 | tf_op jit(solution)/shard_map/ppermute | solution.py:35
  7.0 33.6 %collective-permute-start = (bf16[2,256]{1,0:T(2,128)(2,1)}, bf16[2,256]{1,0:T(2,128)(2,1)}, u32[]{:S(2)}, u32[]{:S(2)}) collective-permute-start(bf16[2,256]{1,0:T(2,128)(2,1)} %get-tuple-element.98), channel_id=1, source_target_pairs={{0,8},{1,9},{2,10},{3,11},{4,12},{5,13},{6,14},{7,15},{8,0},{9,1},... | collective-permute-start | bytes 3080 | tf_op jit(solution)/shard_map/ppermute | solution.py:35
  8.5 212.7 %copy-start.2 = (f32[320,320]{1,0:T(8,128)}, f32[320,320]{1,0:T(8,128)S(1)}, u32[]{:S(2)}) copy-start(f32[320,320]{1,0:T(8,128)S(1)} %compare_select_fusion.bias_ref.refs_11_) | copy-start | bytes 1228804
  8.5 3.1 copy-start.7
  13.6 2.8 copy-start.25
  16.5 2.7 copy-start.20
  27.5 17.7 %copy-start.66 = (f32[2,80]{1,0:T(2,128)}, f32[2,80]{1,0:T(2,128)S(1)}, u32[]{:S(2)}) copy-start(f32[2,80]{1,0:T(2,128)S(1)} %broadcast_multiply_fusion.2) | copy-start | bytes 1924
  27.8 17.3 %copy-start.68 = (f32[2,80]{1,0:T(2,128)}, f32[2,80]{1,0:T(2,128)S(1)}, u32[]{:S(2)}) copy-start(f32[2,80]{1,0:T(2,128)S(1)} %add_rsqrt_fusion) | copy-start | bytes 1924
  29.8 3.7 copy-start.32
  29.8 3.7 copy-start.63
  31.2 4.2 copy-start.16
  38.0 183.1 %copy-start.3 = (f32[3,320,128]{2,1,0:T(8,128)}, f32[3,320,128]{2,1,0:T(8,128)S(1)}, u32[]{:S(2)}) copy-start(f32[3,320,128]{2,1,0:T(8,128)S(1)} %pad_maximum_fusion.4.tables_ref.refs_10_) | copy-start | bytes 1474564
  41.3 3.8 collective-permute-start.3
  203.3 7.3 %copy-start = (bf16[2048,1408]{1,0:T(8,128)(2,1)S(1)}, bf16[2048,1408]{1,0:T(8,128)(2,1)}, u32[]{:S(2)}) copy-start(bf16[2048,1408]{1,0:T(8,128)(2,1)} %get-tuple-element.47.weight_ref.refs_7_) | copy-start | bytes 17301508
  203.3 7.3 %copy-start.1 = (bf16[16,80,2048]{2,1,0:T(8,128)(2,1)S(1)}, bf16[16,80,2048]{2,1,0:T(8,128)(2,1)}, u32[]{:S(2)}) copy-start(bf16[16,80,2048]{2,1,0:T(8,128)(2,1)} %get-tuple-element.46) | copy-start | bytes 15728644
  221.1 8.7 %copy-start.4 = (bf16[1280,704]{1,0:T(8,128)(2,1)}, bf16[1280,704]{1,0:T(8,128)(2,1)S(1)}, u32[]{:S(2)}) copy-start(bf16[1280,704]{1,0:T(8,128)(2,1)S(1)} %get-tuple-element.49) | copy-start | bytes 5406724
  487.4 4.7 copy-start.30
  489.1 3.0 copy-start.27
  498.3 26.1 %collective-permute-start.4 = (f32[2,1024]{1,0:T(2,128)}, f32[2,1024]{1,0:T(2,128)}, u32[]{:S(2)}, u32[]{:S(2)}) collective-permute-start(f32[2,1024]{1,0:T(2,128)} %pad_maximum_fusion.9), channel_id=1, source_target_pairs={{0,4},{1,5},{2,6},{3,7},{4,0},{5,1},{6,2},{7,3},{8,12},{9,13},{10,... | collective-permute-start | bytes 24584 | tf_op jit(solution)/shard_map/ppermute | solution.py:35
  499.2 8.6 %copy-start.43 = (f32[1,256,768]{2,1,0:T(8,128)S(1)}, f32[1,256,768]{2,1,0:T(8,128)}, u32[]{:S(2)}) copy-start(f32[1,256,768]{2,1,0:T(8,128)} %get-tuple-element.59) | copy-start | bytes 2359300
  500.0 8.0 %copy-start.23 = (bf16[2,80,2048]{2,1,0:T(8,128)(2,1)}, bf16[2,80,2048]{2,1,0:T(8,128)(2,1)S(1)}, u32[]{:S(2)}) copy-start(bf16[2,80,2048]{2,1,0:T(8,128)(2,1)S(1)} %get-tuple-element.146) | copy-start | bytes 1966084
  500.1 8.0 %copy-start.24 = (bf16[2,80,2048]{2,1,0:T(8,128)(2,1)}, bf16[2,80,2048]{2,1,0:T(8,128)(2,1)S(1)}, u32[]{:S(2)}) copy-start(bf16[2,80,2048]{2,1,0:T(8,128)(2,1)S(1)} %get-tuple-element.145) | copy-start | bytes 1966084
  500.1 7.8 %copy-start.40 = (bf16[4,256,768]{2,1,0:T(8,128)(2,1)S(1)}, bf16[4,256,768]{2,1,0:T(8,128)(2,1)}, u32[]{:S(2)}) copy-start(bf16[4,256,768]{2,1,0:T(8,128)(2,1)} %get-tuple-element.60) | copy-start | bytes 4718596
  514.2 3.3 copy-start.36
  514.2 3.3 copy-start.39
  514.3 3.3 copy-start.35
  514.3 3.3 copy-start.38
  517.5 51.5 %copy-start.9 = (f32[2,256,1408]{2,1,0:T(8,128)}, f32[2,256,1408]{2,1,0:T(8,128)S(1)}, u32[]{:S(2)}) copy-start(f32[2,256,1408]{2,1,0:T(8,128)S(1)} %get-tuple-element.91) | copy-start | bytes 8650756
  520.8 36.7 %copy-start.70 = (f32[2,256]{1,0:T(2,128)S(1)}, f32[2,256]{1,0:T(2,128)}, u32[]{:S(2)}) copy-start(f32[2,256]{1,0:T(2,128)} %param.24) | copy-start | bytes 6148
  520.8 36.7 %copy-start.72 = (f32[2,256]{1,0:T(2,128)S(1)}, f32[2,256]{1,0:T(2,128)}, u32[]{:S(2)}) copy-start(f32[2,256]{1,0:T(2,128)} %param.29) | copy-start | bytes 6148
  520.9 36.7 %copy-start.73 = (f32[2,256]{1,0:T(2,128)S(1)}, f32[2,256]{1,0:T(2,128)}, u32[]{:S(2)}) copy-start(f32[2,256]{1,0:T(2,128)} %param.34) | copy-start | bytes 6148
  520.9 37.3 %copy-start.26 = (f32[512,256]{1,0:T(8,128)S(1)}, f32[512,256]{1,0:T(8,128)}, u32[]{:S(2)}) copy-start(f32[512,256]{1,0:T(8,128)} %param.21) | copy-start | bytes 1572868
  525.1 5.1 collective-permute-start.5
  525.2 5.4 collective-permute-start.7
  526.9 4.5 collective-permute-start.6
  531.4 3.6 collective-permute-start.8
  535.0 4.1 collective-permute-start.9
  539.7 21.4 %copy-start.71 = (f32[2,256]{1,0:T(2,128)}, f32[2,256]{1,0:T(2,128)S(1)}, u32[]{:S(2)}) copy-start(f32[2,256]{1,0:T(2,128)S(1)} %get-tuple-element.87) | copy-start | bytes 6148
  558.2 2.9 copy-start.14
  558.2 2.9 copy-start.15
  561.1 4.8 copy-start.11
  561.1 4.8 copy-start.12
  561.1 4.8 copy-start.28
  561.1 4.7 copy-start.29
  565.9 3.1 copy-start.8
  565.9 4.4 copy-start.18
  565.9 5.2 copy-start.19
  (36 other events, 58.0 us)

commit v5 on v4

--- a/solution.py
+++ b/solution.py
@@ -236,12 +236,14 @@
         head, refs = refs[:count], refs[count:]
         return head
 
-    cot, normed, packed, hidden, attended, turned = take(6)
+    cot, packed, hidden, attended, turned = take(5)
+    normed_t, attended_t_all, hidden_t_all = take(3)
     w_project, w_gate_up, w_down, w_output, tables, bias = take(6)
-    d_packed, d_att, d_project = take(3)
-    stage, x_in, z_out, z_in, mine = take(4), take(4), take(4), take(4), take(4)
+    z_in, mine = take(4), take(4)
     act_away, act_near, core_in, y_out, y_in, far_out, act_far, act_sum = [take(2) for _ in range(8)]
-    x_send, x_recv, z_send, z_recv, a_send, a_recv = refs
+    stage, x_in = take(4), take(4)
+    d_packed, d_att, d_project, attended_t, hidden_t, normed_block, cot_block = take(7)
+    x_send, x_recv, z_send, z_recv, a_send, a_recv, load_sem, block_sem = refs
     greet(group_places(half))
 
     spots, seqs, piece, _ = cot.shape
@@ -251,22 +253,28 @@
     wide = D // (2 * groups)
     every = lambda ref: pl.BlockSpec(ref.shape, lambda g: (0,) * len(ref.shape))
 
-    left = (cot, cot, normed, normed)
-    right = (hidden, attended, d_packed, d_project)
-
-    def product(c, left_ref, right_ref):
-        value = dot_rows(flat(left_ref), flat(right_ref))
-        return value.T if c < 2 and by_columns else value
-
-    def columns_of(side, g=None):
-        first = side * groups + (0 if g is None else g)
-        return blocked((spots, seqs, piece, wide), 0, 0, 0, step(first) if g is None else first)
+    whole = (attended_t, hidden_t, d_packed, d_project)
+
+    def product(c, block, whole_ref):
+        if c >= 2:
+            return dot_plain(block, flat(whole_ref))
+        value = dot_plain(whole_ref[...], block)
+        return value if by_columns else value.T
+
+    def block_copy(index):
+        c, g = order[index]
+        span, slot = pl.ds(g * wide, wide), index % 2
+        if c >= 2:
+            source, target = normed_t.at[span], normed_block.at[slot]
+        else:
+            source, target = cot.at[:, :, :, span], cot_block.at[slot]
+        return pltpu.make_async_copy(source, target, block_sem.at[slot])
 
     def x_copy(c, g):
         return send_to(place(1, 0), stage[c].at[g], x_in[c].at[g], x_send.at[c, g], x_recv.at[c, g])
 
     def z_copy(c, j):
-        source = z_out[c].at[j // per]
+        source = x_in[c].at[j // per]
         if per > 1:
             rows = z_in[c].shape[1]
             source = source.at[pl.ds((j % per) * rows, rows)]
@@ -278,51 +286,50 @@
         there = (place(0, 1), place(0, 2), place(2, 0))[s]
         return send_to(there, source, target, a_send.at[a, s], a_recv.at[a, s])
 
-    order = [(c, g) for c in range(4) for g in range(groups - 1, -1, -1)]
-    started, served = [0], [0]
-
-    def start_x(up_to):
-        while started[0] < min(up_to, len(order)):
+    order = [(0, 3), (0, 2), (1, 3), (1, 2), (1, 1), (0, 1)]
+    order += [(c, g) for c in (2, 3) for g in (3, 2, 1)] + [(c, 0) for c in (2, 1, 3, 0)]
+    started, served, ready = [0], [0], set()
+
+    def start_x():
+        while started[0] < min(served[0] + window, len(order)) and order[started[0]][0] in ready:
             x_copy(*order[started[0]]).start()
             started[0] += 1
 
     def away_products(chunks):
-        def body(*refs):
+        def body(block_ref, *refs):
             count = len(chunks)
             for k, c in enumerate(chunks):
-                put(refs[1 + count + k], product(c, refs[0], refs[1 + k]))
-
+                put(refs[count + k], product(c, flat(block_ref), refs[k]))
+
+        if chunks[0] >= 2:
+            source, block = normed_t, blocked((wide, normed_t.shape[1]), step(groups), 0)
+        else:
+            source, block = cot, blocked((spots, seqs, piece, wide), 0, 0, 0, step(groups))
         pltpu.emit_pipeline(
             body,
             grid=(groups,),
-            in_specs=[columns_of(1)] + [every(right[c]) for c in chunks],
+            in_specs=[block] + [every(whole[c]) for c in chunks],
             out_specs=[blocked((1,) + stage[c].shape[1:], step(), 0, 0) for c in chunks],
-        )(left[chunks[0]], *[right[c] for c in chunks], *[stage[c] for c in chunks])
-
-    def own_product(c, g):
-        out = mine[c] if g == 0 else z_out[c]
-
-        def body(left_ref, right_ref, came_ref, *out_refs):
-            total = product(c, left_ref, right_ref) + came_ref[0].astype(jnp.float32)
-            for out_ref in out_refs:
-                put(out_ref, total)
-
-        outs = ([mine[c]] if g == 0 else []) + ([z_out[c]] if g > 0 or per > 1 else [])
-        one = (1,) + stage[c].shape[1:]
-        pltpu.emit_pipeline(
-            body,
-            grid=(1,),
-            in_specs=[columns_of(0, g), every(right[c]), blocked(one, g, 0, 0)],
-            out_specs=[blocked(one, 0 if out is mine[c] else g, 0, 0) for out in outs],
-        )(left[c], right[c], x_in[c], *outs)
+        )(source, *[whole[c] for c in chunks], *[stage[c] for c in chunks])
+        ready.update(chunks)
+        start_x()
 
     def serve(count):
         for _ in range(count):
-            c, g = order[served[0]]
+            index = served[0]
+            c, g = order[index]
+            served[0] += 1
+            block_copy(index).wait()
+            if served[0] < len(order):
+                block_copy(served[0]).start()
             x_copy(c, g).wait_recv()
-            served[0] += 1
-            start_x(served[0] + window)
-            own_product(c, g)
+            start_x()
+            block = flat((normed_block if c >= 2 else cot_block).at[index % 2])
+            total = product(c, block, whole[c]) + x_in[c][g].astype(jnp.float32)
+            if g == 0:
+                mine[c][0] = total
+            if g > 0 or per > 1:
+                put(x_in[c].at[g], total)
             for j in range(g * per, (g + 1) * per):
                 if j:
                     z_copy(c, j).start()
@@ -359,97 +366,111 @@
             out_specs=[block(3 * heads)],
         )(turned, d_att, tables, bias, d_project)
 
-    def rows_of(width, core):
-        return blocked((spots // 2, seqs, piece, width), core, 0, 0, 0)
-
-    def normed_step(core):
-        def body(d_project_ref, d_packed_ref, project_ref, gate_up_ref, out_ref):
+    def two_cores(away_ref, near_ref, total):
+        middle = total.shape[0] // 2
+        put(near_ref, total[:middle])
+        put(away_ref, total[middle:])
+
+    core_block = blocked((spots // 2, seqs, piece, 256), 0, 0, 0, step())
+
+    def normed_step():
+        def body(d_project_ref, d_packed_ref, project_ref, gate_up_ref, away_ref, near_ref):
             total = dot_cols(flat(d_project_ref), project_ref[...])
-            put(out_ref, total + dot_cols(flat(d_packed_ref), gate_up_ref[...]))
+            two_cores(away_ref, near_ref, total + dot_cols(flat(d_packed_ref), gate_up_ref[...]))
 
         pltpu.emit_pipeline(
             body,
             grid=(D // 256,),
             in_specs=[
-                rows_of(3 * heads, core),
-                rows_of(2 * units, core),
+                every(d_project),
+                every(d_packed),
                 blocked((256, 3 * heads), step(), 0),
                 blocked((256, 2 * units), step(), 0),
             ],
-            out_specs=[blocked((spots // 2, seqs, piece, 256), 0, 0, 0, step())],
-        )(d_project, d_packed, w_project, w_gate_up, (act_away if core else act_near)[0])
-
-    def out_step(core):
-        def body(attended_ref, hidden_ref, output_ref, down_ref, out_ref):
+            out_specs=[core_block, core_block],
+        )(d_project, d_packed, w_project, w_gate_up, act_away[0], act_near[0])
+
+    def out_step():
+        def body(attended_ref, hidden_ref, output_ref, down_ref, away_ref, near_ref):
             total = dot_plain(flat(attended_ref), output_ref[...])
-            put(out_ref, total + dot_plain(flat(hidden_ref), down_ref[...]))
+            two_cores(away_ref, near_ref, total + dot_plain(flat(hidden_ref), down_ref[...]))
 
         pltpu.emit_pipeline(
             body,
             grid=(D // 256,),
             in_specs=[
-                rows_of(heads, core),
-                rows_of(units, core),
+                every(attended),
+                every(hidden),
                 blocked((heads, 256), 0, step()),
                 blocked((units, 256), 0, step()),
             ],
-            out_specs=[blocked((spots // 2, seqs, piece, 256), 0, 0, 0, step())],
-        )(attended, hidden, w_output, w_down, (act_away if core else act_near)[1])
+            out_specs=[core_block, core_block],
+        )(attended, hidden, w_output, w_down, act_away[1], act_near[1])
 
     def add_terms(*refs):
         *terms, out_ref = refs
         put(out_ref, sum(flat(term).astype(jnp.float32) for term in terms))
 
     half_seqs = seqs // 2
-    row = lambda *index: blocked((1, 1, piece, D), *index, 0, 0)
-    line = lambda index: blocked((1, piece, D), index, 0, 0)
 
     def core_arrived(a):
         a_copy(a, 0).wait_recv()
+        rows = blocked((1, half_seqs, piece, D), 1, step(), 0, 0)
         pltpu.emit_pipeline(
             add_terms,
-            grid=(seqs,),
-            in_specs=[row(1, step()), row(1, step())],
-            out_specs=[line(step())],
+            grid=(2,),
+            in_specs=[rows, rows],
+            out_specs=[blocked((half_seqs, piece, D), step(), 0, 0)],
         )(act_near[a], core_in[a], y_out[a])
         a_copy(a, 1).start()
 
     def y_arrived(a):
+        def body(*refs):
+            add_terms(*refs[:3], refs[6])
+            add_terms(*refs[3:6], refs[7])
+
+        def both(shape, *lead):
+            return [blocked(shape, *lead, step(first), 0, 0) for first in (half_seqs, 0)]
+
+        rows, lines = both((1, 1, piece, D), 0), both((1, piece, D))
         a_copy(a, 1).wait_recv()
-        for first, out in ((half_seqs, far_out[a]), (0, act_sum[a])):
-            pltpu.emit_pipeline(
-                add_terms,
-                grid=(half_seqs,),
-                in_specs=[row(0, step(first)), row(0, step(first)), line(step(first))],
-                out_specs=[line(step())],
-            )(act_near[a], core_in[a], y_in[a], out)
-            if first:
-                a_copy(a, 2).start()
-
+        pltpu.emit_pipeline(
+            body,
+            grid=(half_seqs,),
+            in_specs=[rows[0], rows[0], lines[0], rows[1], rows[1], lines[1]],
+            out_specs=[blocked((1, piece, D), step(), 0, 0)] * 2,
+        )(*[act_near[a], core_in[a], y_in[a]] * 2, far_out[a], act_sum[a])
+        a_copy(a, 2).start()
+
+    loads = [
+        pltpu.make_async_copy(attended_t_all, attended_t, load_sem.at[0]),
+        pltpu.make_async_copy(hidden_t_all, hidden_t, load_sem.at[1]),
+    ]
+    for load in loads:
+        load.start()
+    block_copy(0).start()
+    for load in loads:
+        load.wait()
     away_products((0, 1))
-    start_x(window)
+    out_step()
+    a_copy(1, 0).start()
+    serve(2)
     units_step()
+    core_arrived(1)
     away_products((2,))
-    serve(1)
+    serve(2)
     attention_step(0, seqs // 2)
-    serve(1)
+    serve(2)
     attention_step(seqs // 2, seqs - seqs // 2)
     away_products((3,))
-    serve(2)
-    normed_step(1)
-    a_copy(0, 0).start()
-    serve(2)
-    normed_step(0)
-    core_arrived(0)
-    serve(2)
-    out_step(1)
-    a_copy(1, 0).start()
-    out_step(0)
-    serve(1)
-    core_arrived(1)
-    y_arrived(0)
     serve(1)
     y_arrived(1)
+    normed_step()
+    a_copy(0, 0).start()
+    serve(1)
+    core_arrived(0)
+    serve(4)
+    y_arrived(0)
     serve(len(order) - served[0])
     for c in range(4):
         for j in range(1, half):
@@ -462,46 +483,48 @@
         a_copy(a, 2).wait_recv()
 
 
-def run_backward(half, by_columns, rows, weights, tables, bias, window=3):
-    cot, _, packed, hidden, attended, turned = rows
+def run_backward(half, by_columns, rows, transposed, weights, tables, bias, window=3):
+    cot, packed, hidden, attended, turned = rows
     low, full = jnp.bfloat16, jnp.float32
     spots, seqs, piece, _ = cot.shape
     each = D // (2 * half)
     groups = min(half, 4)
     wide = D // (2 * groups)
-    widths = (hidden.shape[-1], attended.shape[-1], packed.shape[-1], turned.shape[-1])
-    columns = [by_columns and c < 2 for c in range(4)]
-    if by_columns and groups != half:
-        columns = [False] * 4
-
-    def shape_of(count, block, kind):
-        return [
-            jax.ShapeDtypeStruct((count, w, block) if flip else (count, block, w), kind)
-            for w, flip in zip(widths, columns)
-        ]
+    widths = (attended.shape[-1], hidden.shape[-1], packed.shape[-1], turned.shape[-1])
+    columns = [by_columns and groups == half and c < 2 for c in range(4)]
+
+    def shape_of(count, block):
+        return [(count, w, block) if flip else (count, block, w) for w, flip in zip(widths, columns)]
 
     def row_shape(*lead, kind=low):
         return [jax.ShapeDtypeStruct(lead + (piece, D), kind)] * 2
 
-    shapes = [jax.ShapeDtypeStruct(r.shape, low) for r in (packed, attended, turned)]
-    shapes += shape_of(groups, wide, low) * 3 + shape_of(half, each, low) + shape_of(1, wide, full)
+    shapes = [jax.ShapeDtypeStruct(shape, low) for shape in shape_of(half, each)]
+    shapes += [jax.ShapeDtypeStruct(shape, full) for shape in shape_of(1, wide)]
     shapes += row_shape(spots // 2, seqs) * 3 + row_shape(seqs) * 2 + row_shape(seqs // 2) * 2
     shapes += row_shape(seqs // 2, kind=full)
     anywhere = pl.BlockSpec(memory_space=pl.ANY)
-    ins = [*rows, *weights, tables, bias]
+    vmem = pl.BlockSpec(memory_space=pltpu.VMEM)
+    ins = [*rows, *transposed, *weights, tables, bias]
     sem = pltpu.SemaphoreType.DMA
+    rows_all = spots * seqs * piece
+    scratch = [pltpu.VMEM(shape, low) for shape in shape_of(groups, wide)] * 2
+    scratch += [pltpu.VMEM(r.shape, low) for r in (packed, attended, turned)]
+    scratch += [pltpu.VMEM(t.shape, low) for t in transposed[1:]]
+    scratch += [pltpu.VMEM((2, wide, rows_all), low), pltpu.VMEM((2, spots, seqs, piece, wide), low)]
+    scratch += [sem((4, groups))] * 2 + [sem((4, half))] * 2 + [sem((2, 3))] * 2 + [sem((2,))] * 2
     outs = pl.pallas_call(
         functools.partial(backward, half, columns[0], window),
         out_shape=shapes,
         in_specs=[anywhere] * len(ins),
-        out_specs=[anywhere] * len(shapes),
-        scratch_shapes=[sem((4, groups))] * 2 + [sem((4, half))] * 2 + [sem((2, 3))] * 2,
+        out_specs=[anywhere] * 4 + [vmem] * 4 + [anywhere] * (len(shapes) - 8),
+        scratch_shapes=scratch,
         compiler_params=pltpu.CompilerParams(
-            collective_id=1, has_side_effects=True, vmem_limit_bytes=56 * 1024 * 1024
+            collective_id=1, has_side_effects=True, vmem_limit_bytes=60 * 1024 * 1024
         ),
         name="backward",
     )(*ins)
-    z_in, own = outs[15:19], outs[19:23]
+    z_in, own = outs[:4], outs[4:8]
     act_far, act_sum = outs[-4:-2], outs[-2:]
     pairs = []
     for c in range(4):
@@ -828,9 +851,15 @@
 
     half_d = D // 2
     row_shape = (spots, seqs, piece, -1)
-    rows = [values.reshape(row_shape) for values in (all_cot, all_normed, packed, hidden, attended, turned)]
-    (grad_down, grad_output, grad_gate_up, grad_project), (d_normed, summed) = run_backward(
-        blocks_half, by_columns, rows, (w_project, w_gate_up, w_down, w_output), tables, bias
+    rows = [values.reshape(row_shape) for values in (all_cot, packed, hidden, attended, turned)]
+    (grad_output, grad_down, grad_gate_up, grad_project), (d_normed, summed) = run_backward(
+        blocks_half,
+        by_columns,
+        rows,
+        (all_normed.T, attended.T, hidden.T),
+        (w_project, w_gate_up, w_down, w_output),
+        tables,
+        bias,
     )
     if not by_columns:
         grad_down, grad_output = [tuple(g.T for g in pair) for pair in (grad_down, grad_output)]

time: 584 us -> 527 us (0.902)
  Pallas kernels: 446 us -> 373 us
  local copies, waits for them, and re-layouts: 60.3 us -> 76.4 us
    pallas_call x1, Pallas kernels: 255 us -> 182 us  [run_backward(): pl.pallas_call(functools.partial(backward, half, columns[0], window), out...]
    reshape x0 -> x2, local copies, waits for them, and re-layouts: none -> 8.97 us  [the longest x1 7.89 us: local(): all_normed, all_cot = [rows.reshape(rows_all, D) for rows in gathered[4:]]]
    unnamed x200 -> x192, local copies, waits for them, and re-layouts: 34.5 us -> 39.1 us
  transfers between devices with their start and end apart: 10 -> 10, of which waited for: 3 -> 3; matrix products, arithmetic and copies ran while one was open for 11% -> 12% of each run, Pallas kernels for 0% -> 0%
where the time goes in v5:
time: 527 us; the launch traced here: 522 us
  Pallas kernels  373 us (71%)
  local copies, waits for them, and re-layouts  76.4 us (14%)
  other arithmetic  43.5 us (8%)
  starting transfers between devices  12.5 us (2%)
  matrix products  7.16 us (1%)
  between operations  7.01 us (1%)
    pallas_call x1, Pallas kernels, run_backward(): pl.pallas_call(functools.partial(backward, half, columns[0], window), out...  182 us
    pallas_call x1, Pallas kernels, run_gather(): pl.pallas_call(functools.partial(gather_all, half, layout, m), out_shape=...  157 us
    unnamed x192, local copies, waits for them, and re-layouts  39.1 us
    sub x5, other arithmetic, adam_update(): weight_old - rate * (moment_hat / (jnp.sqrt(square_hat) + ADAM_EPS) + dec...  17.2 us
    pallas_call x1, Pallas kernels, sum_everywhere(): pl.pallas_call(functools.partial(sum_kernel, rounds), out_shape=jax.Shape...  15.3 us
    ppermute x10, starting transfers between devices, swap(): return lax.ppermute(values, BOTH, pairs)  12.5 us
  transfers between devices with their start and end apart: 10, of which 3 were waited for; matrix products, arithmetic and copies ran while one was open for 12% of the time, Pallas kernels for 0%

profile of v5, /device:TPU:0, one launch (start us, length us, event | category | flops | bytes accessed | tf_op | source)
XLA Modules:
  0.0 522.1 jit_solution(660444431071628620)
XLA Ops:
  0.7 1.2 constant_dynamic-update-slice_fusion.12
  1.9 5.0 collective-permute-start.2
  8.5 1.6 convert.62
  12.5 1.1 slice_bitcast_fusion.2
  18.3 0.9 constant_dynamic-update-slice_fusion.35
  19.2 0.9 constant_dynamic-update-slice_fusion.34
  31.9 1.5 concatenate.89
  33.4 1.9 concatenate.88
  35.3 2.4 broadcast_select_fusion
  37.9 1.0 broadcast_select_fusion.4
  39.4 1.0 broadcast_select_fusion.2
  41.1 1.8 collective-permute-start.3
  46.6 156.6 %gather_all.1 = (bf16[2048,768]{1,0:T(8,128)(2,1)}, bf16[2048,1408]{1,0:T(8,128)(2,1)}, bf16[704,2048]{1,0:T(8,128)(2,1)}, bf16[256,2048]{1,0:T(8,128)(2,1)}, bf...) custom-call(bf16[256,768]{1,0:T(8,128)(2,1)} %get-tuple-element.132.refs_0_, ...), custom_call_target="tpu_custom_call" | custom-call | tf_op jit(solution)/shard_map/gather_all/pallas_call | solution.py:205
  203.2 7.2 %fusion.projected_ref = f32[4,4,80,768]{3,2,1,0:T(8,128)S(1)} fusion(bf16[4,4,80,2048]{3,2,1,0:T(8,128)(2,1)} %bitcast.95, bf16[2048,768]{1,0:T(8,128)(2,1)} %get-tuple-element.50.refs_8_), kind=kOutput, calls=%fused_computation.1 | convolution fusion | flops 4026531840 | bytes 12320768 | tf_op jit(solution)/shard_map/dot_general | solution.py:573
  210.4 8.7 %attention_fore.1 = (bf16[4,4,80,768]{3,2,1,0:T(8,128)(2,1)S(1)}, bf16[4,4,80,256]{3,2,1,0:T(8,128)(2,1)S(1)}) custom-call(f32[4,4,80,768]{3,2,1,0:T(8,128)S(1)} %fusion.projected_ref, f32[3,320,128]{2,1,0:T(8,128)S(1)} %pad_maximum_fusion.4.tables_ref.refs_12_, f32[320,320]{1,0:T(8,128)S(1)} %compare_select_fusion.bias_ref.refs_13_), custom_call_target="tpu_custom_call" | custom-call | flops 629145600 | bytes 6881280 | tf_op jit(solution)/shard_map/attention_fore/pallas_call | solution.py:690
  219.1 1.3 copy-done.6
  220.3 1.1 copy.49
  221.4 7.9 %copy.48 = bf16[1280,2048]{0,1:T(8,128)(2,1)} copy(bf16[1280,2048]{1,0:T(8,128)(2,1)} %bitcast.96) | data formatting | bytes 10485760 | tf_op jit(solution)/shard_map/reshape | solution.py:829
  229.3 2.6 copy-done.1
  231.9 2.5 copy-done.2
  234.4 10.5 %units_fore.1 = (f32[1280,1408]{1,0:T(8,128)}, bf16[1280,704]{1,0:T(8,128)(2,1)S(1)}) custom-call(bf16[1280,2048]{1,0:T(8,128)(2,1)S(1)} %bitcast.97, bf16[2048,1408]{1,0:T(8,128)(2,1)S(1)} %copy-done.1), custom_call_target="tpu_custom_call" | custom-call | flops 7381975040 | bytes 14254080 | tf_op jit(solution)/shard_map/units_fore/pallas_call | solution.py:715
  244.9 2.5 copy.50
  247.4 182.1 %backward.1 = (bf16[4,256,256]{2,1,0:T(8,128)(2,1)}, bf16[4,704,256]{2,1,0:T(8,128)(2,1)}, bf16[4,256,1408]{2,1,0:T(8,128)(2,1)}, bf16[4,256,768]{2,1,0:T(8,128)...) custom-call(bf16[4,4,80,2048]{3,2,1,0:T(8,128)(2,1)} %bitcast.104, ...), custom_call_target="tpu_custom_call" | custom-call | tf_op jit(solution)/shard_map/backward/pallas_call | solution.py:516
  429.5 1.7 fusion.22
  435.4 1.0 copy-done.46
  451.4 1.5 multiply_reduce_fusion.4
  452.9 2.2 concatenate.108
  455.0 1.5 concatenate.109
  456.5 3.2 multiply_reduce_fusion
  459.9 0.9 copy-done.35
  461.2 2.1 multiply_reduce_fusion.1
  463.3 2.0 multiply_reduce_fusion.2
  465.3 1.5 constant_dynamic-update-slice_fusion.46
  467.8 2.2 collective-permute-start.7
  470.0 1.2 collective-permute-start.6
  471.1 1.5 constant_dynamic-update-slice_fusion.38
  473.2 1.3 collective-permute-done.6
  474.5 1.5 collective-permute-start.8
  476.0 1.5 constant_dynamic-update-slice_fusion.45
  478.0 1.5 constant_dynamic-update-slice_fusion.37
  484.0 15.3 %sum_everywhere.1 = f32[8,128]{1,0:T(8,128)} custom-call(f32[8,128]{1,0:T(8,128)} %broadcast_in_dim.29.in_ref), custom_call_target="tpu_custom_call" | custom-call | tf_op jit(solution)/shard_map/sum_everywhere/pallas_call | solution.py:560
  499.4 1.2 slice.367
  501.3 1.3 multiply_subtract_fusion.4
  502.6 3.1 multiply_subtract_fusion.3
  505.8 4.7 multiply_subtract_fusion.2
  510.5 3.1 multiply_subtract_fusion.1
  513.6 1.3 copy-done.20
  515.7 5.0 multiply_subtract_fusion
  (267 shorter events, 48.6 us)
Async XLA Ops:
  1.9 38.5 %collective-permute-start.2 = (bf16[2,256]{1,0:T(2,128)(2,1)}, bf16[2,256]{1,0:T(2,128)(2,1)}, u32[]{:S(2)}, u32[]{:S(2)}) collective-permute-start(bf16[2,256]{1,0:T(2,128)(2,1)} %get-tuple-element.98), channel_id=1, source_target_pairs={{0,24},{1,25},{2,26},{3,27},{4,28},{5,29},{6,30},{7,31},{8,16},{9,... | collective-permute-start | bytes 3080 | tf_op jit(solution)/shard_map/ppermute | solution.py:35
  7.0 33.5 %collective-permute-start.1 = (bf16[2,256]{1,0:T(2,128)(2,1)}, bf16[2,256]{1,0:T(2,128)(2,1)}, u32[]{:S(2)}, u32[]{:S(2)}) collective-permute-start(bf16[2,256]{1,0:T(2,128)(2,1)} %get-tuple-element.98), channel_id=1, source_target_pairs={{0,16},{1,17},{2,18},{3,19},{4,20},{5,21},{6,22},{7,23},{8,24},{9,... | collective-permute-start | bytes 3080 | tf_op jit(solution)/shard_map/ppermute | solution.py:35
  7.0 33.5 %collective-permute-start = (bf16[2,256]{1,0:T(2,128)(2,1)}, bf16[2,256]{1,0:T(2,128)(2,1)}, u32[]{:S(2)}, u32[]{:S(2)}) collective-permute-start(bf16[2,256]{1,0:T(2,128)(2,1)} %get-tuple-element.98), channel_id=1, source_target_pairs={{0,8},{1,9},{2,10},{3,11},{4,12},{5,13},{6,14},{7,15},{8,0},{9,1},... | collective-permute-start | bytes 3080 | tf_op jit(solution)/shard_map/ppermute | solution.py:35
  8.5 201.9 %copy-start.3 = (f32[320,320]{1,0:T(8,128)}, f32[320,320]{1,0:T(8,128)S(1)}, u32[]{:S(2)}) copy-start(f32[320,320]{1,0:T(8,128)S(1)} %compare_select_fusion.bias_ref.refs_13_) | copy-start | bytes 1228804
  8.5 3.0 copy-start.9
  13.6 2.8 copy-start.26
  16.5 2.7 copy-start.22
  27.2 17.8 %copy-start.7 = (bf16[2,80,2048]{2,1,0:T(8,128)(2,1)}, bf16[2,80,2048]{2,1,0:T(8,128)(2,1)S(1)}, u32[]{:S(2)}) copy-start(bf16[2,80,2048]{2,1,0:T(8,128)(2,1)S(1)} %constant_dynamic-update-slice_fusion) | copy-start | bytes 1966084
  27.4 17.6 %copy-start.65 = (f32[2,80]{1,0:T(2,128)}, f32[2,80]{1,0:T(2,128)S(1)}, u32[]{:S(2)}) copy-start(f32[2,80]{1,0:T(2,128)S(1)} %broadcast_multiply_fusion.2) | copy-start | bytes 1924
  27.8 17.2 %copy-start.67 = (f32[2,80]{1,0:T(2,128)}, f32[2,80]{1,0:T(2,128)S(1)}, u32[]{:S(2)}) copy-start(f32[2,80]{1,0:T(2,128)S(1)} %add_rsqrt_fusion) | copy-start | bytes 1924
  29.8 3.6 copy-start.32
  29.8 3.6 copy-start.62
  31.1 4.1 copy-start.18
  35.3 2.5 copy-start.48
  35.3 2.6 copy-start.31
  35.3 2.6 copy-start.63
  35.3 2.6 copy-start.64
  37.9 172.5 %copy-start.4 = (f32[3,320,128]{2,1,0:T(8,128)}, f32[3,320,128]{2,1,0:T(8,128)S(1)}, u32[]{:S(2)}) copy-start(f32[3,320,128]{2,1,0:T(8,128)S(1)} %pad_maximum_fusion.4.tables_ref.refs_12_) | copy-start | bytes 1474564
  41.1 3.8 collective-permute-start.3
  220.3 9.0 %copy-start.5 = (bf16[4,4,80,256]{3,2,1,0:T(8,128)(2,1)}, bf16[4,4,80,256]{3,2,1,0:T(8,128)(2,1)S(1)}, u32[]{:S(2)}) copy-start(bf16[4,4,80,256]{3,2,1,0:T(8,128)(2,1)S(1)} %get-tuple-element.51.refs_3_) | copy-start | bytes 1966084
  229.3 2.6 copy-start.1
  231.9 2.5 copy-start.2
  429.5 3.9 copy-start.30
  439.8 27.1 %collective-permute-start.4 = (f32[2,1024]{1,0:T(2,128)}, f32[2,1024]{1,0:T(2,128)}, u32[]{:S(2)}, u32[]{:S(2)}) collective-permute-start(f32[2,1024]{1,0:T(2,128)} %pad_maximum_fusion.9), channel_id=1, source_target_pairs={{0,4},{1,5},{2,6},{3,7},{4,0},{5,1},{6,2},{7,3},{8,12},{9,13},{10,... | collective-permute-start | bytes 24584 | tf_op jit(solution)/shard_map/ppermute | solution.py:35
  440.6 8.6 %copy-start.44 = (f32[1,256,768]{2,1,0:T(8,128)S(1)}, f32[1,256,768]{2,1,0:T(8,128)}, u32[]{:S(2)}) copy-start(f32[1,256,768]{2,1,0:T(8,128)} %get-tuple-element.59) | copy-start | bytes 2359300
  441.5 8.0 %copy-start.24 = (bf16[2,80,2048]{2,1,0:T(8,128)(2,1)}, bf16[2,80,2048]{2,1,0:T(8,128)(2,1)S(1)}, u32[]{:S(2)}) copy-start(bf16[2,80,2048]{2,1,0:T(8,128)(2,1)S(1)} %get-tuple-element.146) | copy-start | bytes 1966084
  441.5 8.0 %copy-start.25 = (bf16[2,80,2048]{2,1,0:T(8,128)(2,1)}, bf16[2,80,2048]{2,1,0:T(8,128)(2,1)S(1)}, u32[]{:S(2)}) copy-start(bf16[2,80,2048]{2,1,0:T(8,128)(2,1)S(1)} %get-tuple-element.145) | copy-start | bytes 1966084
  441.5 7.8 %copy-start.41 = (bf16[4,256,768]{2,1,0:T(8,128)(2,1)S(1)}, bf16[4,256,768]{2,1,0:T(8,128)(2,1)}, u32[]{:S(2)}) copy-start(bf16[4,256,768]{2,1,0:T(8,128)(2,1)} %get-tuple-element.60) | copy-start | bytes 4718596
  456.5 3.2 copy-start.37
  456.5 3.3 copy-start.40
  456.5 3.3 copy-start.36
  456.5 3.3 copy-start.39
  459.8 53.9 %copy-start.11 = (f32[2,256,1408]{2,1,0:T(8,128)}, f32[2,256,1408]{2,1,0:T(8,128)S(1)}, u32[]{:S(2)}) copy-start(f32[2,256,1408]{2,1,0:T(8,128)S(1)} %get-tuple-element.91) | copy-start | bytes 8650756
  467.6 5.1 collective-permute-start.5
  467.8 5.4 %collective-permute-start.7 = (f32[2,256]{1,0:T(2,128)S(1)}, f32[2,256]{1,0:T(2,128)S(1)}, u32[]{:S(2)}, u32[]{:S(2)}) collective-permute-start(f32[2,256]{1,0:T(2,128)S(1)} %get-tuple-element.164), channel_id=1, source_target_pairs={{0,24},{1,25},{2,26},{3,27},{4,28},{5,29},{6,30},{7,31},{8,16},{9,... | collective-permute-start | bytes 6152 | tf_op jit(solution)/shard_map/ppermute | solution.py:35
  470.0 4.5 collective-permute-start.6
  474.5 3.6 collective-permute-start.8
  478.0 4.1 collective-permute-start.9
  482.8 22.9 %copy-start.69 = (f32[2,256]{1,0:T(2,128)}, f32[2,256]{1,0:T(2,128)S(1)}, u32[]{:S(2)}) copy-start(f32[2,256]{1,0:T(2,128)S(1)} %get-tuple-element.87) | copy-start | bytes 6148
  502.6 3.1 copy-start.16
  502.6 3.1 copy-start.17
  505.7 4.8 copy-start.13
  505.7 4.8 copy-start.14
  505.7 4.8 copy-start.28
  505.7 4.7 copy-start.29
  510.5 3.1 copy-start.10
  510.5 4.4 copy-start.20
  510.5 5.2 %copy-start.21 = (f32[2,256,1408]{2,1,0:T(8,128)S(1)}, f32[2,256,1408]{2,1,0:T(8,128)}, u32[]{:S(2)}) copy-start(f32[2,256,1408]{2,1,0:T(8,128)} %param.32) | copy-start | bytes 8650756
  (32 other events, 51.2 us)

commit v6 on v5

--- a/solution.py
+++ b/solution.py
@@ -524,49 +524,182 @@
         ),
         name="backward",
     )(*ins)
-    z_in, own = outs[:4], outs[4:8]
-    act_far, act_sum = outs[-4:-2], outs[-2:]
     pairs = []
     for c in range(4):
-        came = [z_in[c][j].astype(full) for j in range(half)]
-        first = own[c][0] if columns[c] else own[c][0, :each]
-        pairs.append((first + sum(came[2::2]), sum(came[1::2])))
-    totals = [near + flip_blocks(far.astype(full), 2, 2 * half) for near, far in zip(act_sum, act_far)]
-    return pairs, totals
-
-
-def sum_kernel(rounds, in_ref, out_ref, sent, came, send_sem, recv_sem):
+        own = outs[4 + c][0] if columns[c] else outs[4 + c][0, :each]
+        pairs.append((own, outs[c]))
+    return pairs, outs[-4:]
+
+
+def flip_lanes(values, width):
+    lanes = values.shape[1]
+    even = (lax.broadcasted_iota(jnp.int32, values.shape, 1) // width) % 2 == 0
+    return jnp.where(even, pltpu.roll(values, lanes - width, 1), pltpu.roll(values, width, 1))
+
+
+def norm_rows(tok_rows):
+    centered = tok_rows - jnp.mean(tok_rows, axis=1, keepdims=True)
+    row_scale = lax.rsqrt(jnp.mean(centered * centered, axis=1, keepdims=True) + NORM_EPS)
+    return centered * row_scale, row_scale
+
+
+def finish_rows(each, in_place, far_ref, far_out_ref, sum_ref, sum_out_ref, tok_ref, cot_ref, gain_ref, out_ref, input_ref, grad_ref):
+    d_normed = flat(sum_ref) + flip_lanes(flat(far_ref).astype(jnp.float32), each)
+    summed = flat(sum_out_ref) + flip_lanes(flat(far_out_ref).astype(jnp.float32), each)
+    tok_rows, cot_rows = flat(tok_ref).astype(jnp.float32), flat(cot_ref).astype(jnp.float32)
+    unit_rows, row_scale = norm_rows(tok_rows)
+    d_unit = d_normed * gain_ref[0:1]
+    d_input = row_scale * (
+        d_unit
+        - jnp.mean(d_unit, axis=1, keepdims=True)
+        - unit_rows * jnp.mean(d_unit * unit_rows, axis=1, keepdims=True)
+    )
+    me = lax.axis_index("dp")
+    for ref, value in ((out_ref, tok_rows + summed), (input_ref, cot_rows + d_input)):
+        value = value.astype(jnp.bfloat16)
+        if in_place:
+            for p, r in enumerate(block_order(D // each)):
+                span = pl.ds(pl.multiple_of((me ^ r) * each, each), each)
+                ref[0, :, span] = value[:, p * each : (p + 1) * each]
+        else:
+            ref[0] = value
+    share = jnp.concatenate(
+        [
+            jnp.sum(d_normed * unit_rows, axis=0, keepdims=True),
+            jnp.sum(d_normed, axis=0, keepdims=True),
+            jnp.zeros((6, D), jnp.float32),
+        ],
+        axis=0,
+    )
+
+    @pl.when(pl.program_id(0) == 0)
+    def _():
+        grad_ref[...] = share
+
+    @pl.when(pl.program_id(0) > 0)
+    def _():
+        grad_ref[...] = grad_ref[...] + share
+
+
+def run_finish_rows(each, totals, tokens, cot, gain):
+    in_place = each % 128 == 0
+    count, piece, _ = tokens.shape
+    block = pl.BlockSpec((1, piece, D), lambda s: (s, 0, 0))
+    fixed = pl.BlockSpec((8, D), lambda s: (0, 0))
+    rows = jax.ShapeDtypeStruct(tokens.shape, jnp.bfloat16)
+    return pl.pallas_call(
+        functools.partial(finish_rows, each, in_place),
+        grid=(count,),
+        in_specs=[block] * 6 + [fixed],
+        out_specs=[block, block, fixed],
+        out_shape=[rows, rows, jax.ShapeDtypeStruct((8, D), jnp.float32)],
+        compiler_params=KERNEL_PARAMS,
+        name="finish_rows",
+    )(*totals, tokens, cot, gain)
+
+
+def join_grads(half, spans, *refs):
+    own, came = refs[0:8:2], refs[1:8:2]
+    output_ref, down_ref, gate_up_ref, project_ref, square_ref = refs[8:]
+    side = (lax.axis_index("dp") // 2) % 2
+    heads, whole = spans
+    squares = jnp.float32(0.0)
+
+    def halves(c, rows, columns):
+        nonlocal squares
+        pick = lambda j: came[c][j, rows, columns].astype(jnp.float32)
+        mine = own[c][rows, columns] + sum(pick(j) for j in range(2, half, 2))
+        other = sum(pick(j) for j in range(1, half, 2))
+        squares = squares + jnp.sum(mine * mine) + jnp.sum(other * other)
+        return mine, other
+
+    def places(width, start=0):
+        return [pl.ds(start + pl.multiple_of(s * width, width), width) for s in (side, 1 - side)]
+
+    every = slice(None)
+    for value, span in zip(halves(0, every, every), places(heads)):
+        output_ref[span] = value
+    for value, span in zip(halves(1, slice(0, whole), every), places(whole)):
+        down_ref[span] = value
+    for value, span in zip(halves(1, slice(whole, whole + 64), every), places(64, 2 * whole)):
+        down_ref[span] = value
+    for k in range(3):
+        for value, span in zip(halves(3, every, slice(k * heads, (k + 1) * heads)), places(heads)):
+            project_ref[k, :, span] = value
+    for k in range(2):
+        for value, span in zip(halves(2, every, slice(k * whole, (k + 1) * whole)), places(whole)):
+            gate_up_ref[k, :, span] = value
+    mine, other = halves(2, every, slice(2 * whole, 2 * whole + 128))
+    zero, one = jnp.where(side == 0, mine, other), jnp.where(side == 0, other, mine)
+    first = lax.broadcasted_iota(jnp.int32, zero.shape, 1) < 64
+    gate_up_ref[0, :, 2 * whole :] = jnp.where(first, zero, pltpu.roll(one, 64, 1))
+    gate_up_ref[1, :, 2 * whole :] = jnp.where(first, pltpu.roll(zero, 64, 1), one)
+    square_ref[...] = jnp.full(square_ref.shape, squares)
+
+
+def run_join_grads(half, pairs, shapes, spans):
+    vmem = pl.BlockSpec(memory_space=pltpu.VMEM)
+    return pl.pallas_call(
+        functools.partial(join_grads, half, spans),
+        in_specs=[vmem] * 8,
+        out_specs=[vmem] * 5,
+        out_shape=[jax.ShapeDtypeStruct(shape, jnp.float32) for shape in shapes + [(8, 128)]],
+        compiler_params=pltpu.CompilerParams(vmem_limit_bytes=48 * 1024 * 1024),
+        name="join_grads",
+    )(*[part for pair in pairs for part in pair])
+
+
+def sum_kernel(rounds, half, in_ref, out_ref, total_ref, sent, came, send_sem, recv_sem):
     places = [place(*flips) for flips in rounds]
     greet(places)
+    count = in_ref.shape[0]
     out_ref[...] = in_ref[...]
-    for k, there in enumerate(places):
+    for k, (dp_flip, _) in enumerate(rounds):
         sent[k] = out_ref[...]
-        copy = send_to(there, sent.at[k], came.at[k], send_sem.at[k], recv_sem.at[k])
+        copy = send_to(places[k], sent.at[k], came.at[k], send_sem.at[k], recv_sem.at[k])
         copy.start()
         copy.wait()
-        out_ref[...] = out_ref[...] + came[k]
-
-
-def sum_everywhere(value):
+        move = (dp_flip % 2) * half + dp_flip // 2
+        for p in range(count):
+            out_ref[p] = out_ref[p] + came[k, p ^ move]
+    rows, lanes = in_ref.shape[1:]
+    me = lax.axis_index("dp")
+    used = lax.broadcasted_iota(jnp.int32, (rows, lanes), 0) < rows - 1
+    total = out_ref[0, rows - 1 :, :]
+    for g in range(count):
+        there = me ^ g
+        value = out_ref[(there % 2) * half + there // 2]
+        total = total + jnp.sum(jnp.where(used, value * value, 0.0))
+    total_ref[...] = jnp.broadcast_to(total, total_ref.shape)
+
+
+def sum_everywhere(shares, square):
+    dp_size = lax.axis_size("dp")
     rounds = []
-    for axis, size in enumerate((lax.axis_size("dp"), lax.axis_size("tensor"))):
+    for axis, size in enumerate((dp_size, lax.axis_size("tensor"))):
         flip = 1
         while flip < size:
             rounds.append((0, flip) if axis else (flip, 0))
             flip *= 2
+    each = D // dp_size
+    lanes = 128 if each % 128 == 0 else each
+    used = 2 * each // lanes
+    parts = shares.reshape(2, dp_size, each // lanes, lanes).transpose(1, 0, 2, 3).reshape(dp_size, used, lanes)
+    filler = jnp.zeros((dp_size, 7 - used, lanes), jnp.float32)
+    last = jnp.broadcast_to(square, (dp_size, 1, lanes))
+    parts = jnp.concatenate([parts, filler, last], axis=1)
     vmem = pl.BlockSpec(memory_space=pltpu.VMEM)
-    tile = (8, 128)
     sem = pltpu.SemaphoreType.DMA
-    total = pl.pallas_call(
-        functools.partial(sum_kernel, rounds),
-        out_shape=jax.ShapeDtypeStruct(tile, jnp.float32),
+    summed, total = pl.pallas_call(
+        functools.partial(sum_kernel, rounds, dp_size // 2),
+        out_shape=[jax.ShapeDtypeStruct(shape, jnp.float32) for shape in (parts.shape, (8, lanes))],
         in_specs=[vmem],
-        out_specs=vmem,
-        scratch_shapes=[pltpu.VMEM((len(rounds),) + tile, jnp.float32)] * 2 + [sem((len(rounds),))] * 2,
+        out_specs=[vmem, vmem],
+        scratch_shapes=[pltpu.VMEM((len(rounds),) + parts.shape, jnp.float32)] * 2 + [sem((len(rounds),))] * 2,
         compiler_params=pltpu.CompilerParams(collective_id=2, has_side_effects=True),
         name="sum_everywhere",
-    )(jnp.full(tile, value))
-    return total[0, 0]
+    )(parts)
+    return summed[0, :used].reshape(2, each), total[0, 0]
 
 
 def dot_plain(a, b):
@@ -804,13 +937,10 @@
     norm_full = gather_small(norm_low).astype(jnp.float32)
     gain, shift = norm_full[0], norm_full[1]
 
-    tok_rows = relative(tokens, 2, me, count).astype(jnp.float32)
-    row_mean = jnp.mean(tok_rows, axis=2, keepdims=True)
-    centered = tok_rows - row_mean
-    row_scale = lax.rsqrt(jnp.mean(centered * centered, axis=2, keepdims=True) + NORM_EPS)
-    unit_rows = centered * row_scale
-    normed = (unit_rows * gain + shift).astype(jnp.bfloat16)
+    tok_rel = relative(tokens, 2, me, count)
     cot_low = relative(cotangent, 2, me, count)
+    unit_rows, _ = norm_rows(tok_rel.astype(jnp.float32).reshape(-1, D))
+    normed = (unit_rows * gain + shift).astype(jnp.bfloat16).reshape(tokens.shape)
 
     def chunk(half_of, columns):
         pair = halves(half_of(0), half_of(1))
@@ -849,10 +979,9 @@
     attended = attended.reshape(rows_all, head_cols)
     packed, hidden = run_units_fore(all_normed, w_gate_up)
 
-    half_d = D // 2
     row_shape = (spots, seqs, piece, -1)
     rows = [values.reshape(row_shape) for values in (all_cot, packed, hidden, attended, turned)]
-    (grad_output, grad_down, grad_gate_up, grad_project), (d_normed, summed) = run_backward(
+    pairs, totals = run_backward(
         blocks_half,
         by_columns,
         rows,
@@ -862,58 +991,21 @@
         bias,
     )
     if not by_columns:
-        grad_down, grad_output = [tuple(g.T for g in pair) for pair in (grad_down, grad_output)]
-    layer_out = from_relative((tok_rows + summed).astype(jnp.bfloat16), 2, me, count)
-
-    d_unit = d_normed * gain
-    d_input = row_scale * (
-        d_unit
-        - jnp.mean(d_unit, axis=2, keepdims=True)
-        - unit_rows * jnp.mean(d_unit * unit_rows, axis=2, keepdims=True)
-    )
-    input_grad = from_relative((cot_low.astype(jnp.float32) + d_input).astype(jnp.bfloat16), 2, me, count)
-
-    grad_norm = jnp.stack(
-        [jnp.sum(d_normed * unit_rows, axis=(0, 1)), jnp.sum(d_normed, axis=(0, 1))]
-    )
-    grad_norm = grad_norm[:, :half_d] + swap(grad_norm[:, half_d:], 1, 0)
-    grad_norm = grad_norm.reshape(2, blocks_half, rows_each)
-    norm_grad = grad_norm[:, 0]
-    for j in range(1, blocks_half):
-        norm_grad = norm_grad + swap(grad_norm[:, j], 2 * j, 0)
-    norm_grad = norm_grad + swap(norm_grad, 0, 2)
-    norm_grad = norm_grad + swap(norm_grad, 0, 1)
-
-    def in_order(pair):
-        mine, other = pair
-        return jnp.where(side == 0, mine, other), jnp.where(side == 0, other, mine)
-
-    project_pair = in_order(grad_project)
-    gate_up_pair = in_order(grad_gate_up)
-    down_pair = in_order(grad_down)
-    grads = (
-        jnp.stack(
-            [
-                jnp.concatenate([g[:, k * head_cols : (k + 1) * head_cols] for g in project_pair], axis=1)
-                for k in range(3)
-            ]
-        ),
-        jnp.concatenate(in_order(grad_output), axis=0),
-        jnp.stack(
-            [
-                jnp.concatenate(
-                    [g[:, k * whole : (k + 1) * whole] for g in gate_up_pair]
-                    + [g[:, 2 * whole + 64 * k : 2 * whole + 64 * (k + 1)] for g in gate_up_pair],
-                    axis=1,
-                )
-                for k in range(2)
-            ]
-        ),
-        jnp.concatenate([g[:whole] for g in down_pair] + [g[whole:] for g in down_pair], axis=0),
-        norm_grad,
-    )
-    square_local = sum(jnp.sum(g * g) for g in grads[:4]) + jnp.sum(norm_grad * norm_grad) / spots
-    norm_total = jnp.sqrt(sum_everywhere(square_local))
+        pairs[:2] = [(own.T, came.swapaxes(1, 2)) for own, came in pairs[:2]]
+    *weight_grads, squares = run_join_grads(
+        blocks_half,
+        pairs,
+        [output_weight.shape, down_weight.shape, gate_up_weight.shape, project_weight.shape],
+        (head_cols, whole),
+    )
+    layer_out, input_grad, shares = run_finish_rows(
+        rows_each, totals, tok_rel, cot_low, jnp.broadcast_to(gain[None], (8, D))
+    )
+    if rows_each % 128:
+        layer_out, input_grad = [from_relative(r, 2, me, count) for r in (layer_out, input_grad)]
+    norm_grad, square_total = sum_everywhere(shares[:2], squares[0, 0])
+    grads = (weight_grads[3], weight_grads[0], weight_grads[2], weight_grads[1], norm_grad)
+    norm_total = jnp.sqrt(square_total)
     limit = 0.03 * math.sqrt((4 * D * D + 3 * D * FF + 2 * D) * micro_count * count * SEQ)
     factor = jnp.minimum(1.0, limit / (norm_total + 1e-06))
     rates = (

time: 527 us -> 499 us (0.947)
  other arithmetic: 43.5 us -> 29.3 us
  local copies, waits for them, and re-layouts: 76.4 us -> 65.3 us
  Pallas kernels: 373 us -> 381 us
    pallas_call x1 -> x3, Pallas kernels: 15.3 us -> 25 us  [the longest x1 15.8 us: sum_everywhere(): pl.pallas_call(functools.partial(sum_kernel, rounds, dp_size // 2), out_s...]
    reduce_sum x8 -> x2, other arithmetic: 10.7 us -> 2.78 us  [the longest x1 1.41 us: norm_rows(): jnp.mean(centered * centered, axis=1, keepdims=True) + NORM_EPS]
    concatenate x4 -> x2, local copies, waits for them, and re-layouts: 6.7 us -> 0.79 us  [sum_everywhere(): parts = jnp.concatenate([parts, filler, last], axis=1)]
    ppermute x10 -> x4, starting transfers between devices: 12.5 us -> 7.39 us  [swap(): return lax.ppermute(values, BOTH, pairs)]
    unnamed x192 -> x149, local copies, waits for them, and re-layouts: 39.1 us -> 37.4 us
  transfers between devices with their start and end apart: 10 -> 4, of which waited for: 3 -> 0; matrix products, arithmetic and copies ran while one was open for 12% -> 9% of each run, Pallas kernels for 0% -> 0%
where the time goes in v6:
time: 499 us; the launch traced here: 493 us
  Pallas kernels  381 us (76%)
  local copies, waits for them, and re-layouts  65.3 us (13%)
  other arithmetic  29.3 us (6%)
  starting transfers between devices  7.39 us (1%)
  matrix products  7.16 us (1%)
    pallas_call x1, Pallas kernels, run_backward(): pl.pallas_call(functools.partial(backward, half, columns[0], window), out...  179 us
    pallas_call x1, Pallas kernels, run_gather(): pl.pallas_call(functools.partial(gather_all, half, layout, m), out_shape=...  157 us
    unnamed x149, local copies, waits for them, and re-layouts  37.4 us
    sub x5, other arithmetic, adam_update(): weight_old - rate * (moment_hat / (jnp.sqrt(square_hat) + ADAM_EPS) + dec...  16.8 us
    pallas_call x1, Pallas kernels, sum_everywhere(): pl.pallas_call(functools.partial(sum_kernel, rounds, dp_size // 2), out_s...  15.8 us
    pallas_call x1, Pallas kernels, run_units_fore(): pl.pallas_call(units_fore, grid=(rows // tile,), in_specs=[block(D), whol...  10.5 us
  transfers between devices with their start and end apart: 4, of which 0 were waited for; matrix products, arithmetic and copies ran while one was open for 9% of the time, Pallas kernels for 0%

profile of v6, /device:TPU:0, one launch (start us, length us, event | category | flops | bytes accessed | tf_op | source)
XLA Modules:
  0.0 493.5 jit_solution(6952876673828724663)
XLA Ops:
  0.7 1.2 constant_dynamic-update-slice_fusion.20
  1.9 3.0 collective-permute-start
  4.9 2.6 collective-permute-start.1
  7.5 2.0 convert.61
  9.5 1.1 slice_bitcast_fusion
  13.3 1.0 constant_dynamic-update-slice_fusion.7
  14.4 1.0 constant_dynamic-update-slice_fusion.6
  16.0 0.9 constant_dynamic-update-slice_fusion.5
  16.9 0.9 constant_dynamic-update-slice_fusion.4
  26.0 1.4 convert_reduce_fusion
  27.4 1.4 fusion.6
  28.8 1.6 constant_dynamic-update-slice_fusion.41
  30.4 1.6 constant_dynamic-update-slice_fusion.40
  32.0 1.6 constant_dynamic-update-slice_fusion.39
  33.6 1.6 constant_dynamic-update-slice_fusion.38
  35.1 1.6 constant_dynamic-update-slice_fusion.37
  41.6 1.6 concatenate.77
  43.2 1.3 concatenate.78
  44.6 1.2 broadcast_select_fusion
  46.1 1.0 broadcast_select_fusion.4
  47.2 1.0 broadcast_select_fusion.2
  50.0 1.8 collective-permute-start.3
  55.4 157.0 %gather_all.1 = (bf16[2048,768]{1,0:T(8,128)(2,1)}, bf16[2048,1408]{1,0:T(8,128)(2,1)}, bf16[704,2048]{1,0:T(8,128)(2,1)}, bf16[256,2048]{1,0:T(8,128)(2,1)}, bf...) custom-call(bf16[256,768]{1,0:T(8,128)(2,1)} %get-tuple-element.131.refs_0_, ...), custom_call_target="tpu_custom_call" | custom-call | tf_op jit(solution)/shard_map/gather_all/pallas_call | solution.py:205
  212.4 7.2 %fusion.projected_ref = f32[4,4,80,768]{3,2,1,0:T(8,128)S(1)} fusion(bf16[4,4,80,2048]{3,2,1,0:T(8,128)(2,1)} %bitcast.68, bf16[2048,768]{1,0:T(8,128)(2,1)} %get-tuple-element.60.refs_8_), kind=kOutput, calls=%fused_computation.1 | convolution fusion | flops 4026531840 | bytes 12320768 | tf_op jit(solution)/shard_map/dot_general | solution.py:706
  219.6 8.7 %attention_fore.1 = (bf16[4,4,80,768]{3,2,1,0:T(8,128)(2,1)S(1)}, bf16[4,4,80,256]{3,2,1,0:T(8,128)(2,1)S(1)}) custom-call(f32[4,4,80,768]{3,2,1,0:T(8,128)S(1)} %fusion.projected_ref, f32[3,320,128]{2,1,0:T(8,128)S(1)} %pad_maximum_fusion.tables_ref.refs_12_, f32[320,320]{1,0:T(8,128)S(1)} %compare_select_fusion.bias_ref.refs_13_), custom_call_target="tpu_custom_call" | custom-call | flops 629145600 | bytes 6881280 | tf_op jit(solution)/shard_map/attention_fore/pallas_call | solution.py:823
  228.3 1.3 copy-done.10
  229.6 1.1 copy.50
  230.7 7.9 %copy.49 = bf16[1280,2048]{0,1:T(8,128)(2,1)} copy(bf16[1280,2048]{1,0:T(8,128)(2,1)} %bitcast.69) | data formatting | bytes 10485760 | tf_op jit(solution)/shard_map/reshape | solution.py:959
  238.6 2.6 copy-done.1
  241.2 2.5 copy-done.2
  243.7 10.5 %units_fore.1 = (f32[1280,1408]{1,0:T(8,128)}, bf16[1280,704]{1,0:T(8,128)(2,1)S(1)}) custom-call(bf16[1280,2048]{1,0:T(8,128)(2,1)S(1)} %bitcast.70, bf16[2048,1408]{1,0:T(8,128)(2,1)S(1)} %copy-done.1), custom_call_target="tpu_custom_call" | custom-call | flops 7381975040 | bytes 14254080 | tf_op jit(solution)/shard_map/units_fore/pallas_call | solution.py:848
  254.2 2.5 copy.51
  256.6 179.5 %backward.1 = (bf16[4,256,256]{2,1,0:T(8,128)(2,1)}, bf16[4,704,256]{2,1,0:T(8,128)(2,1)}, bf16[4,256,1408]{2,1,0:T(8,128)(2,1)}, bf16[4,256,768]{2,1,0:T(8,128)...) custom-call(bf16[4,4,80,2048]{3,2,1,0:T(8,128)(2,1)} %bitcast.79, ...), custom_call_target="tpu_custom_call" | custom-call | tf_op jit(solution)/shard_map/backward/pallas_call | solution.py:516
  436.1 1.4 copy-done.11
  437.5 1.4 copy-done.12
  438.9 1.1 copy-done.15
  440.0 1.1 copy-done.16
  441.1 1.0 copy-done.19
  442.1 0.9 copy-done.20
  443.1 6.3 %join_grads.1 = (f32[512,256]{1,0:T(8,128)}, f32[1408,256]{1,0:T(8,128)}, f32[2,256,1408]{2,1,0:T(8,128)}, f32[3,256,512]{2,1,0:T(8,128)}, f32[8,128]{1,0:T(8,128)S(1)}) custom-call(f32[256,256]{1,0:T(8,128)S(1)} %bitcast.75, bf16[4,256,256]{2,1,0:T(8,128)(2,1)S(1)} %copy-done.19, f32[704,256]{1,0:T(8,128)S(1)} %bitcast.74, ...), custom_call_target="tpu_custom_call" | custom-call | tf_op jit(solution)/shard_map/join_grads/pallas_call | solution.py:642
  450.7 3.0 finish_rows.1
  454.5 15.8 %sum_everywhere.1 = (f32[8,8,128]{2,1,0:T(8,128)}, f32[8,128]{1,0:T(8,128)}) custom-call(f32[8,8,128]{2,1,0:T(8,128)} %maximum_maximum_fusion.3.in_ref), custom_call_target="tpu_custom_call" | custom-call | tf_op jit(solution)/shard_map/sum_everywhere/pallas_call | solution.py:693
  470.9 1.2 slice.155
  473.5 4.7 multiply_subtract_fusion.2
  478.2 1.2 copy-done.28
  479.5 7.0 %multiply_subtract_fusion = (f32[2,256,1408]{2,1,0:T(8,128)}, f32[2,256,1408]{2,1,0:T(8,128)}, f32[2,256,1408]{2,1,0:T(8,128)}) fusion(f32[2,256,1408]{2,1,0:T(8,128)S(1)} %copy-done.21, f32[2,256,1408]{2,1,0:T(8,128)} %get-tuple-element.36, f32[]{:T(128)S(6)} %min.3, f32[2,256,1408]{2,1,0:T(8,128)S(1)} %copy-done.27, f32[2,256,1408]{2,1,0:T(8,128)S(1)} %copy-done.28), kind=kLoop, calls=%fused_computation.4 | loop fusion | flops 11534336 | bytes 20185092 | tf_op jit(solution)/shard_map/sub | solution.py:871
  486.6 1.4 multiply_subtract_fusion.3
  489.0 3.1 multiply_subtract_fusion.1
  (188 shorter events, 26.4 us)
Async XLA Ops:
  1.9 47.4 %collective-permute-start = (bf16[2,256]{1,0:T(2,128)(2,1)}, bf16[2,256]{1,0:T(2,128)(2,1)}, u32[]{:S(2)}, u32[]{:S(2)}) collective-permute-start(bf16[2,256]{1,0:T(2,128)(2,1)} %get-tuple-element.103), channel_id=1, source_target_pairs={{0,8},{1,9},{2,10},{3,11},{4,12},{5,13},{6,14},{7,15},{8,0},{9,1},... | collective-permute-start | bytes 3080 | tf_op jit(solution)/shard_map/ppermute | solution.py:35
  4.9 44.4 %collective-permute-start.1 = (bf16[2,256]{1,0:T(2,128)(2,1)}, bf16[2,256]{1,0:T(2,128)(2,1)}, u32[]{:S(2)}, u32[]{:S(2)}) collective-permute-start(bf16[2,256]{1,0:T(2,128)(2,1)} %get-tuple-element.103), channel_id=1, source_target_pairs={{0,16},{1,17},{2,18},{3,19},{4,20},{5,21},{6,22},{7,23},{8,24},{9,... | collective-permute-start | bytes 3080 | tf_op jit(solution)/shard_map/ppermute | solution.py:35
  7.5 41.8 %collective-permute-start.2 = (bf16[2,256]{1,0:T(2,128)(2,1)}, bf16[2,256]{1,0:T(2,128)(2,1)}, u32[]{:S(2)}, u32[]{:S(2)}) collective-permute-start(bf16[2,256]{1,0:T(2,128)(2,1)} %get-tuple-element.103), channel_id=1, source_target_pairs={{0,24},{1,25},{2,26},{3,27},{4,28},{5,29},{6,30},{7,31},{8,16},{9,... | collective-permute-start | bytes 3080 | tf_op jit(solution)/shard_map/ppermute | solution.py:35
  9.5 1.9 copy-start.25
  11.4 1.6 copy-start.58
  11.4 1.9 copy-start.29
  13.2 206.4 %copy-start.3 = (f32[320,320]{1,0:T(8,128)}, f32[320,320]{1,0:T(8,128)S(1)}, u32[]{:S(2)}) copy-start(f32[320,320]{1,0:T(8,128)S(1)} %compare_select_fusion.bias_ref.refs_13_) | copy-start | bytes 1228804
  14.4 10.9 %copy-start.40 = (bf16[2,80,2048]{2,1,0:T(8,128)(2,1)}, bf16[2,80,2048]{2,1,0:T(8,128)(2,1)S(1)}, u32[]{:S(2)}) copy-start(bf16[2,80,2048]{2,1,0:T(8,128)(2,1)S(1)} %get-tuple-element.166) | copy-start | bytes 1966084
  25.3 28.6 %copy-start.5 = (bf16[2,80,2048]{2,1,0:T(8,128)(2,1)}, bf16[2,80,2048]{2,1,0:T(8,128)(2,1)S(1)}, u32[]{:S(2)}) copy-start(bf16[2,80,2048]{2,1,0:T(8,128)(2,1)S(1)} %get-tuple-element.104.tok_ref) | copy-start | bytes 1966084
  26.0 11.6 %copy-start.22 = (f32[3,256,512]{2,1,0:T(8,128)S(1)}, f32[3,256,512]{2,1,0:T(8,128)}, u32[]{:S(2)}) copy-start(f32[3,256,512]{2,1,0:T(8,128)} %param.20) | copy-start | bytes 4718596
  38.7 2.9 copy-start.38
  38.7 2.9 copy-start.39
  44.6 1.4 copy-start.36
  44.6 1.5 copy-start.37
  44.6 1.5 copy-start.52
  44.6 1.5 copy-start.53
  45.9 173.7 %copy-start.4 = (f32[3,320,128]{2,1,0:T(8,128)}, f32[3,320,128]{2,1,0:T(8,128)S(1)}, u32[]{:S(2)}) copy-start(f32[3,320,128]{2,1,0:T(8,128)S(1)} %pad_maximum_fusion.tables_ref.refs_12_) | copy-start | bytes 1474564
  49.1 5.5 %copy-start.7 = (bf16[2,80,2048]{2,1,0:T(8,128)(2,1)}, bf16[2,80,2048]{2,1,0:T(8,128)(2,1)S(1)}, u32[]{:S(2)}) copy-start(bf16[2,80,2048]{2,1,0:T(8,128)(2,1)S(1)} %constant_dynamic-update-slice_fusion.21.refs_9_.cot_ref) | copy-start | bytes 1966084
  50.0 3.8 collective-permute-start.3
  229.6 9.0 %copy-start.9 = (bf16[4,4,80,256]{3,2,1,0:T(8,128)(2,1)}, bf16[4,4,80,256]{3,2,1,0:T(8,128)(2,1)S(1)}, u32[]{:S(2)}) copy-start(bf16[4,4,80,256]{3,2,1,0:T(8,128)(2,1)S(1)} %get-tuple-element.61.refs_3_) | copy-start | bytes 1966084
  238.6 2.6 copy-start.1
  241.2 2.5 copy-start.2
  254.2 2.5 copy-start
  436.1 1.4 copy-start.11
  437.5 1.4 copy-start.12
  443.1 7.6 %copy-start.6 = (bf16[2,80,2048]{2,1,0:T(8,128)(2,1)S(1)}, bf16[2,80,2048]{2,1,0:T(8,128)(2,1)}, u32[]{:S(2)}) copy-start(bf16[2,80,2048]{2,1,0:T(8,128)(2,1)} %copy-done.5) | copy-start | bytes 1966084
  443.1 7.6 %copy-start.8 = (bf16[2,80,2048]{2,1,0:T(8,128)(2,1)S(1)}, bf16[2,80,2048]{2,1,0:T(8,128)(2,1)}, u32[]{:S(2)}) copy-start(bf16[2,80,2048]{2,1,0:T(8,128)(2,1)} %copy-done.7) | copy-start | bytes 1966084
  443.1 7.6 %copy-start.13 = (f32[2,80,2048]{2,1,0:T(8,128)S(1)}, f32[2,80,2048]{2,1,0:T(8,128)}, u32[]{:S(2)}) copy-start(f32[2,80,2048]{2,1,0:T(8,128)} %get-tuple-element.67.sum_ref) | copy-start | bytes 3932164
  443.1 7.6 %copy-start.14 = (f32[2,80,2048]{2,1,0:T(8,128)S(1)}, f32[2,80,2048]{2,1,0:T(8,128)}, u32[]{:S(2)}) copy-start(f32[2,80,2048]{2,1,0:T(8,128)} %get-tuple-element.68.sum_out_ref) | copy-start | bytes 3932164
  443.1 7.6 %copy-start.17 = (bf16[2,80,2048]{2,1,0:T(8,128)(2,1)S(1)}, bf16[2,80,2048]{2,1,0:T(8,128)(2,1)}, u32[]{:S(2)}) copy-start(bf16[2,80,2048]{2,1,0:T(8,128)(2,1)} %get-tuple-element.65.far_ref) | copy-start | bytes 1966084
  443.1 7.6 %copy-start.18 = (bf16[2,80,2048]{2,1,0:T(8,128)(2,1)S(1)}, bf16[2,80,2048]{2,1,0:T(8,128)(2,1)}, u32[]{:S(2)}) copy-start(bf16[2,80,2048]{2,1,0:T(8,128)(2,1)} %get-tuple-element.66.far_out_ref) | copy-start | bytes 1966084
  450.7 22.2 %copy-start.54 = (f32[2,256]{1,0:T(2,128)S(1)}, f32[2,256]{1,0:T(2,128)}, u32[]{:S(2)}) copy-start(f32[2,256]{1,0:T(2,128)} %param.24) | copy-start | bytes 6148
  450.7 22.2 %copy-start.56 = (f32[2,256]{1,0:T(2,128)S(1)}, f32[2,256]{1,0:T(2,128)}, u32[]{:S(2)}) copy-start(f32[2,256]{1,0:T(2,128)} %param.29) | copy-start | bytes 6148
  450.7 22.2 %copy-start.57 = (f32[2,256]{1,0:T(2,128)S(1)}, f32[2,256]{1,0:T(2,128)}, u32[]{:S(2)}) copy-start(f32[2,256]{1,0:T(2,128)} %param.34) | copy-start | bytes 6148
  450.7 22.8 %copy-start.26 = (f32[1408,256]{1,0:T(8,128)S(1)}, f32[1408,256]{1,0:T(8,128)}, u32[]{:S(2)}) copy-start(f32[1408,256]{1,0:T(8,128)} %param.23) | copy-start | bytes 4325380
  450.7 22.8 %copy-start.35 = (f32[1408,256]{1,0:T(8,128)S(1)}, f32[1408,256]{1,0:T(8,128)}, u32[]{:S(2)}) copy-start(f32[1408,256]{1,0:T(8,128)} %param.28) | copy-start | bytes 4325380
  470.9 7.3 %copy-start.55 = (f32[2,256]{1,0:T(2,128)}, f32[2,256]{1,0:T(2,128)S(1)}, u32[]{:S(2)}) copy-start(f32[2,256]{1,0:T(2,128)S(1)} %reshape_squeeze.3) | copy-start | bytes 6148
  473.5 4.7 copy-start.21
  473.5 4.7 copy-start.27
  473.5 6.0 %copy-start.28 = (f32[2,256,1408]{2,1,0:T(8,128)S(1)}, f32[2,256,1408]{2,1,0:T(8,128)}, u32[]{:S(2)}) copy-start(f32[2,256,1408]{2,1,0:T(8,128)} %param.32) | copy-start | bytes 8650756
  479.5 7.0 %copy-start.31 = (f32[512,256]{1,0:T(8,128)S(1)}, f32[512,256]{1,0:T(8,128)}, u32[]{:S(2)}) copy-start(f32[512,256]{1,0:T(8,128)} %param.21) | copy-start | bytes 1572868
  479.5 7.0 %copy-start.49 = (f32[512,256]{1,0:T(8,128)S(1)}, f32[512,256]{1,0:T(8,128)}, u32[]{:S(2)}) copy-start(f32[512,256]{1,0:T(8,128)} %param.26) | copy-start | bytes 1572868
  479.5 7.0 %copy-start.50 = (f32[512,256]{1,0:T(8,128)S(1)}, f32[512,256]{1,0:T(8,128)}, u32[]{:S(2)}) copy-start(f32[512,256]{1,0:T(8,128)} %param.31) | copy-start | bytes 1572868
  479.5 7.0 %copy-start.51 = (f32[512,256]{1,0:T(8,128)S(1)}, f32[512,256]{1,0:T(8,128)}, u32[]{:S(2)}) copy-start(f32[512,256]{1,0:T(8,128)} %get-tuple-element.35) | copy-start | bytes 1572868
  479.5 8.5 %copy-start.33 = (f32[3,256,512]{2,1,0:T(8,128)S(1)}, f32[3,256,512]{2,1,0:T(8,128)}, u32[]{:S(2)}) copy-start(f32[3,256,512]{2,1,0:T(8,128)} %param.30) | copy-start | bytes 4718596
  479.5 8.5 %copy-start.34 = (f32[3,256,512]{2,1,0:T(8,128)S(1)}, f32[3,256,512]{2,1,0:T(8,128)}, u32[]{:S(2)}) copy-start(f32[3,256,512]{2,1,0:T(8,128)} %get-tuple-element.34) | copy-start | bytes 4718596
  486.5 2.0 copy-start.23
  486.5 2.4 copy-start.32
  (15 other events, 17.4 us)
